TPU v7x, 32 devices: a whole 2x2x4 slice. The times are simulated.
32 devices in a mesh: slab: 8 (over z, y), pair: 4 (over x, core).
Axes of the slice: x: 2, y: 2, z: 4, core: 2. Of those that a mesh axis runs over, the one named last changes fastest.
Arguments:
- initial_warmth: float32 [128, 256, 512], P('slab', 'pair'), may hold values from 0.5 to 1.5
- heat_passing_coefficient: float32 [128, 256, 512], P('slab', 'pair'), may hold values from 0.2 to 2
- mirror_fraction: float32 [512, 128], P(('slab', 'pair')), may hold values from 0.3 to 0.9
- element_facing_site: int32 [512, 128], P(('slab', 'pair')), may hold values from 0 to 1023
- tile_block_couples: int32 [8192, 2], P(('slab', 'pair')), may hold values from 0 to 511, as said below
- active_slot_count: int32 [32], P(('slab', 'pair')), may hold values from 42 to 256, as said below
- view_factor_blocks: float32 [8192, 128, 128], P(('slab', 'pair')), as said below
Outputs:
- radiosity: float32 [512, 128], P(('slab', 'pair'))
- warmed_liner: float32 [128, 256, 512], P('slab', 'pair')
Inputs may be any that keep to these rules, and one draw needn't show every extreme that they name: `tile_block_couples`: each row names two different blocks, and no unordered pair of blocks appears twice in the whole list. A device's slots from its active_slot_count on are not used; in every draw some device has all 256 slots live, and some other device has the fewest allowed. `view_factor_blocks`: entries are nonnegative.
All inputs are finite; a program needn't handle non-finite values.
Results may differ from a plain program's by a relative error of at most 0.0003.
Values sent between devices are 32-bit elements; how exact they have to be, the bound alone decides.
No kernel may reach another device: no remote copies, remote signals or barrier semaphores. Data moves between devices by JAX's collectives and lax.ppermute only.
A program may use at most 192 MiB of HBM per device.

v0:
```python
import jax
import jax.numpy as jnp
from jax import lax
from jax.sharding import PartitionSpec as P

BLK = 128
SWEEPS = 2
STEPS = 4


step_size = 0.07


def padded_2(block, sides, width):
    for axis, dim in sides:
        count = lax.axis_size(axis)
        forward = [(i, i + 1) for i in range(count - 1)]
        backward = [(target, source) for source, target in forward]
        low = lax.ppermute(
            lax.slice_in_dim(block, block.shape[dim] - width, None, axis=dim), axis, forward
        )
        high = lax.ppermute(lax.slice_in_dim(block, 0, width, axis=dim), axis, backward)
        block = jnp.concatenate([low, block, high], axis=dim)
    return block


def sides(padded):
    return [
        padded[2:, 1:-1, 1:-1],
        padded[:-2, 1:-1, 1:-1],
        padded[1:-1, 2:, 1:-1],
        padded[1:-1, :-2, 1:-1],
        padded[1:-1, 1:-1, 2:],
        padded[1:-1, 1:-1, :-2],
    ]


def heat_flux(temp_pad, cond_pad, temp, cond):
    total = jnp.zeros_like(temp)
    for near_temp, near_cond in zip(sides(temp_pad), sides(cond_pad)):
        face_cond = jnp.where(near_cond > 0.0, 0.5 * (cond + near_cond), cond)
        total = total + face_cond * (near_temp - temp)
    return total


def depth_pad(field):
    return jnp.pad(field, ((0, 0), (0, 0), (1, 1)))


def collect(radiosity):
    return lax.all_gather(radiosity, ("slab", "pair"), axis=0, tiled=True)


def spread_back(term):
    return lax.psum_scatter(term, ("slab", "pair"), scatter_dimension=0, tiled=True)


def tile_terms(whole, tile_block_couples, view_factor_blocks, live_now):
    count = view_factor_blocks.shape[0]
    alive = (jnp.arange(count) < live_now).astype(jnp.float32)
    first = whole[tile_block_couples[:, 0]]
    second = whole[tile_block_couples[:, 1]]
    to_first = (
        jnp.einsum("tpq,tq->tp", view_factor_blocks, second, precision=lax.Precision.HIGHEST)
        * alive[:, None]
    )
    to_second = (
        jnp.einsum("tpq,tp->tq", view_factor_blocks, first, precision=lax.Precision.HIGHEST)
        * alive[:, None]
    )
    total = jnp.zeros(whole.shape, jnp.float32)
    total = total.at[tile_block_couples[:, 0]].add(to_first)
    return total.at[tile_block_couples[:, 1]].add(to_second)


def shards(
    initial_warmth,
    heat_passing_coefficient,
    mirror_fraction,
    element_facing_site,
    tile_block_couples,
    active_slot_count,
    view_factor_blocks,
):
    owned_horizontals, owned_verticals, thickness_span = initial_warmth.shape
    blocks_here = mirror_fraction.shape[0]
    lowest_sheet = initial_warmth[:, :, 0].reshape(-1)
    facing_sheet = lowest_sheet[element_facing_site]
    emitted = (1.0 - mirror_fraction) * jnp.square(jnp.square(facing_sheet))
    radiosity = emitted
    incident = jnp.zeros_like(emitted)
    for sweep in range(SWEEPS):
        whole = collect(radiosity)
        term = tile_terms(whole, tile_block_couples, view_factor_blocks, active_slot_count[0])
        incident = spread_back(term)
        radiosity = emitted + mirror_fraction * incident
    absorbed = (1.0 - mirror_fraction) * incident - emitted
    weight = owned_horizontals * owned_verticals / (blocks_here * BLK * 1.0)
    summed = jax.ops.segment_sum(
        absorbed.reshape(-1), element_facing_site.reshape(-1), owned_horizontals * owned_verticals
    )
    source = summed.reshape(owned_horizontals, owned_verticals) * weight
    cond_pad = depth_pad(padded_2(heat_passing_coefficient, (("slab", 0), ("pair", 1)), 1))
    warmed_liner = initial_warmth
    for step in range(STEPS):
        temp_pad = depth_pad(padded_2(warmed_liner, (("slab", 0), ("pair", 1)), 1))
        warmed_liner = warmed_liner + step_size * heat_flux(
            temp_pad, cond_pad, warmed_liner, heat_passing_coefficient
        )
        warmed_liner = warmed_liner.at[:, :, 0].add(step_size * source)
    return (radiosity, warmed_liner)


def solution(mesh):
    return jax.shard_map(
        shards,
        mesh=mesh,
        in_specs=(
            P("slab", "pair", None),
            P("slab", "pair", None),
            P(("slab", "pair"), None),
            P(("slab", "pair"), None),
            P(("slab", "pair"), None),
            P(("slab", "pair")),
            P(("slab", "pair"), None, None),
        ),
        out_specs=(P(("slab", "pair"), None), P("slab", "pair", None)),
        check_vma=False,
    )
```

profile of v0, /device:TPU:0, one launch (start us, length us, event | category | flops | bytes accessed | tf_op | source)
XLA Modules:
  0.0 694.6 jit_solution(17742113825377172394)
XLA Ops:
  8.9 4.9 collective-permute-start.2
  16.1 4.6 collective-permute-start.3
  24.7 8.6 %gather_fusion = f32[2048]{0:T(1024)S(1)} fusion(f32[1024]{0:T(1024)S(1)} %reshape_squeeze.3, s32[2048]{0:T(1024)S(1)} %fusion.68), kind=kCustom, calls=%fused_computation | custom fusion | bytes 24576 | tf_op jit(solution)/shard_map/gather | solution.py:88
  33.3 43.6 %all_gather.6 = f32[512,128]{1,0:T(8,128)S(1)} all-gather(f32[16,128]{1,0:T(8,128)S(1)} %bitcast_multiply_fusion), channel_id=1, replica_groups=mesh['slab'=8,'pair'=4] {'slab','pair'}, dimensions={0}, use_global_device_ids=true | all-gather | bytes 270336 | tf_op jit(solution)/shard_map/all_gather | solution.py:51
  78.4 29.5 %fusion.82 = f32[256,1,128]{2,1,0:T(1,128)S(1)} fusion(f32[256,128,1]{1,2,0:T(1,128)S(1)} %bitcast.53, f32[256,128,128]{2,1,0:T(8,128)} %param.21), kind=kOutput, calls=%fused_computation.176 | convolution fusion | flops 50331648 | bytes 17039360 | tf_op jit(solution)/shard_map/tpq,tq->tp/dot_general | solution.py:64
  107.9 14.5 %fusion.83 = f32[256,1,128]{2,1,0:T(1,128)S(1)} fusion(f32[256,128,1]{1,2,0:T(1,128)S(1)} %bitcast.54, f32[256,128,128]{2,1,0:T(8,128)S(1)} %copy-done), kind=kOutput, calls=%fused_computation.177 | convolution fusion | flops 50331648 | bytes 17039360 | tf_op jit(solution)/shard_map/tpq,tp->tq/dot_general | solution.py:68
  124.9 2.6 scatter_custom_fusion.1
  128.3 4.8 copy.106
  133.1 3.8 copy.133
  137.0 5.9 constant_dynamic-update-slice_fusion.1
  144.3 3.0 collective-permute-start.6
  147.4 2.7 pad_maximum_fusion.35
  152.8 4.1 collective-permute-start.7
  157.0 4.9 copy.161
  161.8 5.0 copy.162
  166.8 3.9 copy.163
  170.7 5.0 copy.164
  175.7 2.6 pad_maximum_fusion.30
  178.4 4.9 copy.165
  183.3 5.1 copy.167
  188.3 2.7 pad_maximum_fusion.31
  191.0 5.0 copy.166
  196.0 3.8 copy.168
  199.9 2.1 pad_maximum_fusion.6
  202.0 4.2 copy.125
  206.1 2.1 pad_maximum_fusion.7
  208.2 4.2 copy.128
  212.4 45.5 %reduce-scatter.3.cloned.1.call-done = f32[16,128]{1,0:T(8,128)} async-done(((f32[512,128]{1,0:T(8,128)}), f32[16,128]{1,0:T(8,128)}) %reduce-scatter.3.cloned.1.call-update) | async-done | bytes 8208 | tf_op jit(solution)/shard_map/reduce_scatter | solution.py:55
  258.6 37.2 %all_gather.7 = f32[512,128]{1,0:T(8,128)S(1)} all-gather(f32[16,128]{1,0:T(8,128)S(1)} %multiply_add_fusion.1), channel_id=1, replica_groups=mesh['slab'=8,'pair'=4] {'slab','pair'}, dimensions={0}, use_global_device_ids=true | all-gather | bytes 270336 | tf_op jit(solution)/shard_map/all_gather | solution.py:51
  297.3 28.6 %fusion.84 = f32[256,1,128]{2,1,0:T(1,128)S(1)} fusion(f32[256,128,1]{1,2,0:T(1,128)S(1)} %bitcast.52, f32[256,128,128]{2,1,0:T(8,128)} %param.21), kind=kOutput, calls=%fused_computation.178 | convolution fusion | flops 50331648 | bytes 17039360 | tf_op jit(solution)/shard_map/tpq,tq->tp/dot_general | solution.py:64
  327.4 16.6 %fusion.85 = f32[256,1,128]{2,1,0:T(1,128)S(1)} fusion(f32[256,128,1]{1,2,0:T(1,128)S(1)} %bitcast.51, f32[256,128,128]{2,1,0:T(8,128)} %param.21), kind=kOutput, calls=%fused_computation.179 | convolution fusion | flops 50331648 | bytes 17039360 | tf_op jit(solution)/shard_map/tpq,tp->tq/dot_general | solution.py:68
  344.0 2.3 scatter_custom_fusion.3
  347.1 33.3 %fusion.5 = (f32[16,64,512]{1,0,2:T(8,128)}, f32[16,64,512]{1,0,2:T(8,128)}, f32[16,64,512]{1,0,2:T(8,128)}, f32[16,64,512]{1,0,2:T(8,128)}, f32[16,64,512]{1,0,...) fusion(f32[16,64,512]{1,0,2:T(8,128)} %copy.133, f32[18,66,512]{1,0,2:T(8,128)} %copy.128, ...), kind=kLoop, calls=%fused_computation.25 | loop fusion | flops 22544384 | bytes 40517632 | tf_op jit(solution)/shard_map/add | solution.py:107
  380.4 98.0 %reduce-scatter.5.cloned.1.call-done = f32[16,128]{1,0:T(8,128)} async-done(((f32[512,128]{1,0:T(8,128)}), f32[16,128]{1,0:T(8,128)}) %reduce-scatter.5.cloned.1.call-update) | async-done | bytes 8208 | tf_op jit(solution)/shard_map/reduce_scatter | solution.py:55
  479.7 14.8 %scatter_custom_fusion.4 = f32[1024]{0:T(1024)S(1)} fusion(s32[2048]{0:T(1024)} %bitcast.55, f32[2048]{0:T(1024)S(1)} %get-tuple-element.99, f32[]{:T(128)} %constant.104.clone.1), kind=kCustom, calls=%fused_computation.166 | custom fusion | flops 2048 | bytes 4608 | tf_op jit(solution)/shard_map/scatter-add | solution.py:99
  495.9 2.6 fusion.77
  501.1 2.8 copy.135
  504.1 4.0 collective-permute-done.8
  509.6 3.0 collective-permute-start.11
  513.5 2.7 pad_maximum_fusion.26
  516.1 4.9 copy.169
  521.0 4.9 copy.170
  525.9 2.0 pad_maximum_fusion.8
  527.9 5.7 copy.139
  533.7 20.4 %fusion.13 = f32[16,64,512]{1,0,2:T(8,128)S(1)} fusion(f32[16,64,512]{1,0,2:T(8,128)} %fusion.72, f32[16,64,512]{1,0,2:T(8,128)} %get-tuple-element.62, f32[18,66,512]{1,0,2:T(8,128)} %copy.139, f32[16,64,512]{1,0,2:T(8,128)} %get-tuple-element.61, f32[16,64,512]{1,0,2:T(8,128)} %get-tuple-element.58, f32[1,64,512]{1,0,2:T(1,128)S(1)} %collective-permute-done.9, ...), kind=kLoop, calls=%fused_computation.33 | loop fusion | flops 11010048 | bytes 23666688 | tf_op jit(solution)/shard_map/add | solution.py:107
  559.3 2.8 copy.141
  562.1 7.6 %collective-permute-done.13 = f32[1,64,512]{1,0,2:T(1,128)S(1)} collective-permute-done((f32[1,64,512]{1,0,2:T(1,128)S(1)}, f32[1,64,512]{1,0,2:T(1,128)S(1)}, u32[]{:S(2)}, u32[]{:S(2)}) %collective-permute-start.13) | collective-permute-done | bytes 131104 | tf_op jit(solution)/shard_map/ppermute | solution.py:19
  571.4 3.3 collective-permute-start.15
  575.2 2.7 pad_maximum_fusion.20
  577.9 4.9 copy.171
  582.8 4.9 copy.172
  589.7 5.7 copy.145
  595.4 20.4 %fusion.21 = f32[16,64,512]{1,0,2:T(8,128)S(1)} fusion(f32[16,64,512]{1,0,2:T(8,128)} %copy-done.1, f32[16,64,512]{1,0,2:T(8,128)} %get-tuple-element.62, f32[18,66,512]{1,0,2:T(8,128)} %copy.145, f32[16,64,512]{1,0,2:T(8,128)} %get-tuple-element.61, f32[16,64,512]{1,0,2:T(8,128)} %get-tuple-element.58, f32[1,64,512]{1,0,2:T(1,128)S(1)} %collective-permute-done.13, ...), kind=kLoop, calls=%fused_computation.41 | loop fusion | flops 11010048 | bytes 23666688 | tf_op jit(solution)/shard_map/add | solution.py:107
  618.3 4.4 collective-permute-start.17
  624.0 2.8 copy.147
  626.8 8.0 %collective-permute-done.17 = f32[1,64,512]{1,0,2:T(1,128)S(1)} collective-permute-done((f32[1,64,512]{1,0,2:T(1,128)S(1)}, f32[1,64,512]{1,0,2:T(1,128)S(1)}, u32[]{:S(2)}, u32[]{:S(2)}) %collective-permute-start.17) | collective-permute-done | bytes 131104 | tf_op jit(solution)/shard_map/ppermute | solution.py:19
  636.4 3.0 collective-permute-start.19
  640.3 2.7 pad_maximum_fusion.14
  643.0 4.9 copy.173
  647.8 4.9 copy.174
  652.7 2.0 pad_maximum_fusion.10
  654.7 5.7 copy.151
  660.5 21.8 %fusion.29 = f32[16,64,512]{1,0,2:T(8,128)} fusion(f32[16,64,512]{1,0,2:T(8,128)} %copy-done.2, f32[16,64,512]{1,0,2:T(8,128)} %get-tuple-element.62, f32[18,66,512]{1,0,2:T(8,128)} %copy.151, f32[16,64,512]{1,0,2:T(8,128)} %get-tuple-element.61, f32[16,64,512]{1,0,2:T(8,128)} %get-tuple-element.58, f32[1,64,512]{1,0,2:T(1,128)S(1)} %collective-permute-done.17, ...), kind=kLoop, calls=%fused_computation.49 | loop fusion | flops 11010048 | bytes 23666688 | tf_op jit(solution)/shard_map/add | solution.py:107
  683.6 3.8 copy.152
  (100 shorter events, 44.9 us)
Async XLA Ops:
  7.2 250.7 %reduce-scatter.3.cloned.1.call-start = ((), (), s32[]{:S(2)}) async-start(), calls=%async_computation.2 | async-start | bytes 270336 | tf_op jit(solution)/shard_map/reduce_scatter | solution.py:55
  8.9 128.1 %collective-permute-start.2 = (f32[1,64,512]{2,1,0:T(8,128)}, f32[1,64,512]{2,1,0:T(8,128)S(1)}, u32[]{:S(2)}, u32[]{:S(2)}) collective-permute-start(f32[1,64,512]{2,1,0:T(8,128)} %get-tuple-element.92), channel_id=1, source_target_pairs={{0,4},{4,8},{8,12},{12,16},{16,20},{20,24},{24,28},{1,5},{5,9},{9,... | collective-permute-start | bytes 393224 | tf_op jit(solution)/shard_map/ppermute | solution.py:19
  13.8 123.2 %collective-permute-start = (f32[1,64,512]{2,1,0:T(8,128)}, f32[1,64,512]{2,1,0:T(8,128)S(1)}, u32[]{:S(2)}, u32[]{:S(2)}) collective-permute-start(f32[1,64,512]{2,1,0:T(8,128)} %get-tuple-element.93), channel_id=1, source_target_pairs={{4,0},{8,4},{12,8},{16,12},{20,16},{24,20},{28,24},{5,1},{9,5},{13... | collective-permute-start | bytes 393224 | tf_op jit(solution)/shard_map/ppermute | solution.py:22
  16.1 131.2 %collective-permute-start.3 = (f32[1,64,512]{2,1,0:T(8,128)S(1)}, f32[1,64,512]{2,1,0:T(8,128)S(1)}, u32[]{:S(2)}, u32[]{:S(2)}) collective-permute-start(f32[1,64,512]{2,1,0:T(8,128)S(1)} %get-tuple-element.98), channel_id=1, source_target_pairs={{0,4},{4,8},{8,12},{12,16},{16,20},{20,24},{24,28},{1,5},{5,9},{9,... | collective-permute-start | bytes 393224 | tf_op jit(solution)/shard_map/ppermute | solution.py:19
  20.6 126.7 %collective-permute-start.1 = (f32[1,64,512]{2,1,0:T(8,128)S(1)}, f32[1,64,512]{2,1,0:T(8,128)S(1)}, u32[]{:S(2)}, u32[]{:S(2)}) collective-permute-start(f32[1,64,512]{2,1,0:T(8,128)S(1)} %get-tuple-element.97), channel_id=1, source_target_pairs={{4,0},{8,4},{12,8},{16,12},{20,16},{24,20},{28,24},{5,1},{9,5},{13... | collective-permute-start | bytes 393224 | tf_op jit(solution)/shard_map/ppermute | solution.py:22
  24.7 8.6 %copy-start.12 = (f32[16,128]{1,0:T(8,128)S(1)}, f32[16,128]{1,0:T(8,128)}, u32[]{:S(2)}) copy-start(f32[16,128]{1,0:T(8,128)} %param.17) | copy-start | bytes 24580
  78.4 29.5 %copy-start = (f32[256,128,128]{2,1,0:T(8,128)S(1)}, f32[256,128,128]{2,1,0:T(8,128)}, u32[]{:S(2)}) copy-start(f32[256,128,128]{2,1,0:T(8,128)} %param.21) | copy-start | bytes 50331652
  122.5 10.7 %copy-start.3 = (f32[16,64,512]{2,1,0:T(8,128)S(1)}, f32[16,64,512]{2,1,0:T(8,128)}, u32[]{:S(2)}) copy-start(f32[16,64,512]{2,1,0:T(8,128)} %param.15) | copy-start | bytes 6291460
  127.5 0.7 copy-start.11
  128.2 350.2 %reduce-scatter.5.cloned.1.call-start = ((), (), s32[]{:S(2)}) async-start(), calls=%async_computation.3 | async-start | bytes 270336 | tf_op jit(solution)/shard_map/reduce_scatter | solution.py:55
  142.9 7.1 %copy-start.4 = (f32[18,64,512]{2,1,0:T(8,128)}, f32[18,64,512]{2,1,0:T(8,128)S(1)}, u32[]{:S(2)}) copy-start(f32[18,64,512]{2,1,0:T(8,128)S(1)} %constant_dynamic-update-slice_fusion) | copy-start | bytes 7077892
  143.0 32.8 %collective-permute-start.4 = (f32[18,1,512]{2,1,0:T(1,128)S(1)}, f32[18,1,512]{2,1,0:T(1,128)S(1)}, u32[]{:S(2)}, u32[]{:S(2)}) collective-permute-start(f32[18,1,512]{2,1,0:T(1,128)S(1)} %get-tuple-element.84), channel_id=1, source_target_pairs={{1,0},{2,1},{3,2},{5,4},{6,5},{7,6},{9,8},{10,9},{11,10},{13,12},{... | collective-permute-start | bytes 110600 | tf_op jit(solution)/shard_map/ppermute | solution.py:22
  144.3 31.5 %collective-permute-start.6 = (f32[18,1,512]{2,1,0:T(1,128)S(1)}, f32[18,1,512]{2,1,0:T(1,128)S(1)}, u32[]{:S(2)}, u32[]{:S(2)}) collective-permute-start(f32[18,1,512]{2,1,0:T(1,128)S(1)} %get-tuple-element.83), channel_id=1, source_target_pairs={{0,1},{1,2},{2,3},{4,5},{5,6},{6,7},{8,9},{9,10},{10,11},{12,13},{... | collective-permute-start | bytes 110600 | tf_op jit(solution)/shard_map/ppermute | solution.py:19
  150.0 1.4 copy-start.6
  151.5 36.8 %collective-permute-start.5 = (f32[18,1,512]{2,1,0:T(1,128)S(1)}, f32[18,1,512]{2,1,0:T(1,128)S(1)}, u32[]{:S(2)}, u32[]{:S(2)}) collective-permute-start(f32[18,1,512]{2,1,0:T(1,128)S(1)} %get-tuple-element.88), channel_id=1, source_target_pairs={{1,0},{2,1},{3,2},{5,4},{6,5},{7,6},{9,8},{10,9},{11,10},{13,12},{... | collective-permute-start | bytes 110600 | tf_op jit(solution)/shard_map/ppermute | solution.py:22
  152.8 35.5 %collective-permute-start.7 = (f32[18,1,512]{2,1,0:T(1,128)S(1)}, f32[18,1,512]{2,1,0:T(1,128)S(1)}, u32[]{:S(2)}, u32[]{:S(2)}) collective-permute-start(f32[18,1,512]{2,1,0:T(1,128)S(1)} %get-tuple-element.87), channel_id=1, source_target_pairs={{0,1},{1,2},{2,3},{4,5},{5,6},{6,7},{8,9},{9,10},{10,11},{12,13},{... | collective-permute-start | bytes 110600 | tf_op jit(solution)/shard_map/ppermute | solution.py:19
  161.8 5.0 copy-start.9
  170.7 5.0 copy-start.5
  183.3 5.1 copy-start.7
  191.0 5.0 copy-start.8
  346.4 0.7 copy-start.10
  498.5 5.5 collective-permute-start.9
  499.8 8.3 %collective-permute-start.8 = (f32[1,64,512]{1,0,2:T(1,128)S(1)}, f32[1,64,512]{1,0,2:T(1,128)S(1)}, u32[]{:S(2)}, u32[]{:S(2)}) collective-permute-start(f32[1,64,512]{1,0,2:T(1,128)S(1)} %get-tuple-element.68), channel_id=1, source_target_pairs={{4,0},{8,4},{12,8},{16,12},{20,16},{24,20},{28,24},{5,1},{9,5},{13... | collective-permute-start | bytes 393224 | tf_op jit(solution)/shard_map/ppermute | solution.py:22
  508.3 4.3 collective-permute-start.10
  509.6 3.9 collective-permute-start.11
  554.1 2.0 copy-start.1
  556.5 13.3 %collective-permute-start.13 = (f32[1,64,512]{1,0,2:T(1,128)S(1)}, f32[1,64,512]{1,0,2:T(1,128)S(1)}, u32[]{:S(2)}, u32[]{:S(2)}) collective-permute-start(f32[1,64,512]{1,0,2:T(1,128)S(1)} %get-tuple-element.65), channel_id=1, source_target_pairs={{0,4},{4,8},{8,12},{12,16},{16,20},{20,24},{24,28},{1,5},{5,9},{9,... | collective-permute-start | bytes 393224 | tf_op jit(solution)/shard_map/ppermute | solution.py:19
  558.0 11.9 %collective-permute-start.12 = (f32[1,64,512]{1,0,2:T(1,128)S(1)}, f32[1,64,512]{1,0,2:T(1,128)S(1)}, u32[]{:S(2)}, u32[]{:S(2)}) collective-permute-start(f32[1,64,512]{1,0,2:T(1,128)S(1)} %get-tuple-element.66), channel_id=1, source_target_pairs={{4,0},{8,4},{12,8},{16,12},{20,16},{24,20},{28,24},{5,1},{9,5},{13... | collective-permute-start | bytes 393224 | tf_op jit(solution)/shard_map/ppermute | solution.py:22
  570.1 4.6 collective-permute-start.14
  571.4 3.9 collective-permute-start.15
  615.9 2.0 copy-start.2
  618.3 16.5 %collective-permute-start.17 = (f32[1,64,512]{1,0,2:T(1,128)S(1)}, f32[1,64,512]{1,0,2:T(1,128)S(1)}, u32[]{:S(2)}, u32[]{:S(2)}) collective-permute-start(f32[1,64,512]{1,0,2:T(1,128)S(1)} %get-tuple-element.63), channel_id=1, source_target_pairs={{0,4},{4,8},{8,12},{12,16},{16,20},{20,24},{24,28},{1,5},{5,9},{9,... | collective-permute-start | bytes 393224 | tf_op jit(solution)/shard_map/ppermute | solution.py:19
  622.7 12.3 %collective-permute-start.16 = (f32[1,64,512]{1,0,2:T(1,128)S(1)}, f32[1,64,512]{1,0,2:T(1,128)S(1)}, u32[]{:S(2)}, u32[]{:S(2)}) collective-permute-start(f32[1,64,512]{1,0,2:T(1,128)S(1)} %get-tuple-element.64), channel_id=1, source_target_pairs={{4,0},{8,4},{12,8},{16,12},{20,16},{24,20},{28,24},{5,1},{9,5},{13... | collective-permute-start | bytes 393224 | tf_op jit(solution)/shard_map/ppermute | solution.py:22
  635.1 4.3 collective-permute-start.18
  636.4 3.9 collective-permute-start.19
Sparse Core Ops, SparseCore 0:
  128.4 129.5 reduce-scatter.2
  347.2 131.1 reduce-scatter.4
where the time goes:
time: 708 us; the launch traced here: 695 us
  waiting for transfers between devices  165 us (23%)
  other arithmetic  157 us (22%)
  local copies, waits for them, and re-layouts  140 us (20%)
  matrix products  89.2 us (13%)
  blocking collectives  80.8 us (11%)
  starting transfers between devices  46.1 us (7%)
  between operations  15.9 us (2%)
    reduce_scatter x2, waiting for transfers between devices, spread_back(): lax.psum_scatter(term, ('slab', 'pair'), scatter_dimension=0, tiled=True)  144 us
    add x4, other arithmetic, shards(): warmed_liner + step_size * heat_flux(temp_pad, cond_pad, warmed_liner, he...  96 us
    unnamed x45, local copies, waits for them, and re-layouts  86.2 us
    all_gather x2, blocking collectives, collect(): return lax.all_gather(radiosity, ('slab', 'pair'), axis=0, tiled=True)  80.8 us
    dot_general x2, matrix products, tile_terms(): jnp.einsum('tpq,tq->tp', view_factor_blocks, second, precision=lax.Precis...  58.1 us
    ppermute x10, starting transfers between devices, padded_2(): lax.ppermute(lax.slice_in_dim(block, block.shape[dim] - width, None, axis...  33.1 us
    dot_general x2, matrix products, tile_terms(): jnp.einsum('tpq,tp->tq', view_factor_blocks, first, precision=lax.Precisi...  31.1 us
    concatenate x14, other arithmetic, padded_2(): block = jnp.concatenate([low, block, high], axis=dim)  26.4 us
  transfers between devices with their start and end apart: 22, of which 8 were waited for; matrix products, arithmetic and copies ran while one was open for 25% of the time, Pallas kernels for 0%

commit v1 on v0

--- a/solution.py
+++ b/solution.py
@@ -48,11 +48,16 @@
 
 
 def collect(radiosity):
-    return lax.all_gather(radiosity, ("slab", "pair"), axis=0, tiled=True)
+    count = lax.axis_size("slab") * lax.axis_size("pair")
+    copies = jnp.broadcast_to(radiosity[None], (count,) + radiosity.shape)
+    copies = copies.reshape(count * radiosity.shape[0], radiosity.shape[1])
+    return lax.all_to_all(copies, ("slab", "pair"), split_axis=0, concat_axis=0, tiled=True)
 
 
 def spread_back(term):
-    return lax.psum_scatter(term, ("slab", "pair"), scatter_dimension=0, tiled=True)
+    count = lax.axis_size("slab") * lax.axis_size("pair")
+    parts = lax.all_to_all(term, ("slab", "pair"), split_axis=0, concat_axis=0, tiled=True)
+    return parts.reshape(count, -1, term.shape[1]).sum(axis=0)
 
 
 def tile_terms(whole, tile_block_couples, view_factor_blocks, live_now):

time: 708 us -> 503 us (0.71)
  waiting for transfers between devices: 165 us -> 23.8 us
  blocking collectives: 80.8 us -> 0 us
  starting transfers between devices: 46.1 us -> 77.7 us
  between operations: 15.9 us -> 2.16 us
    reduce_scatter x2 -> x0, waiting for transfers between devices: 144 us -> none  [spread_back(): lax.psum_scatter(term, ('slab', 'pair'), scatter_dimension=0, tiled=True)]
    all_gather x2 -> x0, blocking collectives: 80.8 us -> none  [collect(): return lax.all_gather(radiosity, ('slab', 'pair'), axis=0, tiled=True)]
    all_to_all x0 -> x4, starting transfers between devices: none -> 25.5 us  [the longest x2 13.7 us: collect(): lax.all_to_all(copies, ('slab', 'pair'), split_axis=0, concat_axis=0, til...]
    unnamed x45 -> x39, local copies, waits for them, and re-layouts: 86.2 us -> 81.9 us
  transfers between devices with their start and end apart: 22 -> 24, of which waited for: 8 -> 8; matrix products, arithmetic and copies ran while one was open for 25% -> 37% of each run, Pallas kernels for 0% -> 0%
where the time goes in v1:
time: 503 us; the launch traced here: 493 us
  other arithmetic  161 us (32%)
  local copies, waits for them, and re-layouts  138 us (27%)
  matrix products  90.5 us (18%)
  starting transfers between devices  77.7 us (15%)
  waiting for transfers between devices  23.8 us (5%)
    add x4, other arithmetic, shards(): warmed_liner + step_size * heat_flux(temp_pad, cond_pad, warmed_liner, he...  96.1 us
    unnamed x39, local copies, waits for them, and re-layouts  81.9 us
    dot_general x2, matrix products, tile_terms(): jnp.einsum('tpq,tq->tp', view_factor_blocks, second, precision=lax.Precis...  57.2 us
    ppermute x10, starting transfers between devices, padded_2(): lax.ppermute(lax.slice_in_dim(block, block.shape[dim] - width, None, axis...  39.1 us
    dot_general x2, matrix products, tile_terms(): jnp.einsum('tpq,tp->tq', view_factor_blocks, first, precision=lax.Precisi...  33.3 us
    concatenate x14, other arithmetic, padded_2(): block = jnp.concatenate([low, block, high], axis=dim)  28.3 us
    concatenate x7, local copies, waits for them, and re-layouts, padded_2(): block = jnp.concatenate([low, block, high], axis=dim)  26.3 us
    scatter-add x1, other arithmetic, shards(): jax.ops.segment_sum(absorbed.reshape(-1), element_facing_site.reshape(-1)...  14.8 us
  transfers between devices with their start and end apart: 24, of which 8 were waited for; matrix products, arithmetic and copies ran while one was open for 37% of the time, Pallas kernels for 0%

profile of v1, /device:TPU:0, one launch (start us, length us, event | category | flops | bytes accessed | tf_op | source)
XLA Modules:
  0.0 493.0 jit_solution(5922049122033779896)
XLA Ops:
  1.6 4.9 collective-permute-start.2
  8.8 4.6 collective-permute-start.3
  16.7 8.6 %gather_fusion = f32[2048]{0:T(1024)S(1)} fusion(f32[1024]{0:T(1024)S(1)} %reshape_squeeze.3, s32[2048]{0:T(1024)S(1)} %fusion.68), kind=kCustom, calls=%fused_computation | custom fusion | bytes 24576 | tf_op jit(solution)/shard_map/gather | solution.py:93
  26.0 7.8 %all-to-all-start = ((f32[32,16,128]{2,1,0:T(8,128)}), f32[32,16,128]{2,1,0:T(8,128)S(1)}, u32[]{:S(2)}, u32[]{:S(2)}) async-start(f32[32,16,128]{2,1,0:T(8,128)} %broadcast_in_dim.9), calls=%async_computation | async-start | bytes 524288 | tf_op jit(solution)/shard_map/all_to_all | solution.py:54
  34.5 4.8 copy.106
  39.4 3.8 copy.133
  43.2 6.0 %constant_dynamic-update-slice_fusion.1 = (f32[18,64,512]{2,1,0:T(8,128)S(1)}, f32[16,64,512]{2,1,0:T(8,128)}, f32[16,64,512]{2,1,0:T(8,128)}) fusion(f32[18,64,512]{2,1,0:T(8,128)S(1)} %constant_dynamic-update-slice_fusion.2, f32[16,64,512]{2,1,0:T(8,128)} %param.16, f32[1,64,512]{2,1,0:T(8,128)S(1)} %collective-permute-done.2, ...), kind=kLoop, calls=%fused_computation.142 | loop fusion | flops 1048576 | bytes 8650752
  50.6 3.2 collective-permute-start.6
  54.5 3.0 pad_maximum_fusion.35
  59.0 28.6 %fusion.82 = f32[256,1,128]{2,1,0:T(1,128)S(1)} fusion(f32[256,128,1]{1,2,0:T(1,128)S(1)} %bitcast.61, f32[256,128,128]{2,1,0:T(8,128)} %param.21), kind=kOutput, calls=%fused_computation.176 | convolution fusion | flops 50331648 | bytes 17039360 | tf_op jit(solution)/shard_map/tpq,tq->tp/dot_general | solution.py:69
  87.6 16.7 %fusion.83 = f32[256,1,128]{2,1,0:T(1,128)S(1)} fusion(f32[256,128,1]{1,2,0:T(1,128)S(1)} %bitcast.62, f32[256,128,128]{2,1,0:T(8,128)} %param.21), kind=kOutput, calls=%fused_computation.177 | convolution fusion | flops 50331648 | bytes 17039360 | tf_op jit(solution)/shard_map/tpq,tp->tq/dot_general | solution.py:73
  104.3 2.2 scatter_custom_fusion
  106.5 3.5 scatter_custom_fusion.1
  110.0 5.9 %all-to-all-start.1 = ((f32[32,16,128]{2,1,0:T(8,128)}), f32[32,16,128]{2,1,0:T(8,128)S(1)}, u32[]{:S(2)}, u32[]{:S(2)}) async-start(f32[32,16,128]{2,1,0:T(8,128)} %bitcast.14), calls=%async_computation.1 | async-start | bytes 524288 | tf_op jit(solution)/shard_map/all_to_all | solution.py:59
  119.0 3.4 collective-permute-start.7
  122.4 3.9 copy.161
  126.3 5.0 %copy.162 = f32[16,64,512]{1,0,2:T(8,128)} copy(f32[16,64,512]{2,1,0:T(8,128)} %get-tuple-element.94) | data formatting | bytes 4194304
  131.3 3.8 copy.163
  135.1 5.0 %copy.164 = f32[16,64,512]{1,0,2:T(8,128)} copy(f32[16,64,512]{2,1,0:T(8,128)} %get-tuple-element.96) | data formatting | bytes 4194304
  140.2 2.7 pad_maximum_fusion.30
  142.8 5.0 %copy.165 = f32[16,64,512]{1,0,2:T(8,128)} copy(f32[16,64,512]{2,1,0:T(8,128)} %get-tuple-element.82) | data formatting | bytes 4194304
  147.8 3.8 copy.167
  152.5 5.9 %all-to-all-start.2 = ((f32[32,16,128]{2,1,0:T(8,128)}), f32[32,16,128]{2,1,0:T(8,128)S(1)}, u32[]{:S(2)}, u32[]{:S(2)}) async-start(f32[32,16,128]{2,1,0:T(8,128)} %broadcast_in_dim.10), calls=%async_computation.2 | async-start | bytes 524288 | tf_op jit(solution)/shard_map/all_to_all | solution.py:54
  158.4 4.3 pad_maximum_fusion.31
  162.7 4.9 copy.166
  167.6 3.8 copy.168
  173.5 4.2 copy.125
  179.7 4.2 copy.128
  185.4 28.6 %fusion.84 = f32[256,1,128]{2,1,0:T(1,128)S(1)} fusion(f32[256,128,1]{1,2,0:T(1,128)S(1)} %bitcast.60, f32[256,128,128]{2,1,0:T(8,128)} %param.21), kind=kOutput, calls=%fused_computation.178 | convolution fusion | flops 50331648 | bytes 17039360 | tf_op jit(solution)/shard_map/tpq,tq->tp/dot_general | solution.py:69
  214.0 2.3 scatter_custom_fusion.2
  216.4 16.6 %fusion.85 = f32[256,1,128]{2,1,0:T(1,128)S(1)} fusion(f32[256,128,1]{1,2,0:T(1,128)S(1)} %bitcast.59, f32[256,128,128]{2,1,0:T(8,128)} %param.21), kind=kOutput, calls=%fused_computation.179 | convolution fusion | flops 50331648 | bytes 17039360 | tf_op jit(solution)/shard_map/tpq,tp->tq/dot_general | solution.py:73
  232.9 3.5 scatter_custom_fusion.3
  236.4 5.8 %all-to-all-start.3 = ((f32[32,16,128]{2,1,0:T(8,128)}), f32[32,16,128]{2,1,0:T(8,128)S(1)}, u32[]{:S(2)}, u32[]{:S(2)}) async-start(f32[32,16,128]{2,1,0:T(8,128)} %bitcast.24), calls=%async_computation.3 | async-start | bytes 524288 | tf_op jit(solution)/shard_map/all_to_all | solution.py:59
  242.3 33.2 %fusion.5 = (f32[16,64,512]{1,0,2:T(8,128)}, f32[16,64,512]{1,0,2:T(8,128)}, f32[16,64,512]{1,0,2:T(8,128)}, f32[16,64,512]{1,0,2:T(8,128)}, f32[16,64,512]{1,0,...) fusion(f32[16,64,512]{1,0,2:T(8,128)} %copy.133, f32[18,66,512]{1,0,2:T(8,128)} %copy.128, ...), kind=kLoop, calls=%fused_computation.25 | loop fusion | flops 22544384 | bytes 40517632 | tf_op jit(solution)/shard_map/add | solution.py:112
  276.1 14.8 %scatter_custom_fusion.4 = f32[1024]{0:T(1024)S(1)} fusion(s32[2048]{0:T(1024)} %bitcast.63, f32[2048]{0:T(1024)S(1)} %get-tuple-element.99, f32[]{:T(128)} %constant.105.clone.1), kind=kCustom, calls=%fused_computation.166 | custom fusion | flops 2048 | bytes 4608 | tf_op jit(solution)/shard_map/scatter-add | solution.py:104
  292.3 2.6 fusion.77
  294.9 3.7 collective-permute-start.9
  299.9 2.8 copy.135
  302.7 7.3 %collective-permute-done.9 = f32[1,64,512]{1,0,2:T(1,128)S(1)} collective-permute-done((f32[1,64,512]{1,0,2:T(1,128)S(1)}, f32[1,64,512]{1,0,2:T(1,128)S(1)}, u32[]{:S(2)}, u32[]{:S(2)}) %collective-permute-start.9) | collective-permute-done | bytes 131104 | tf_op jit(solution)/shard_map/ppermute | solution.py:19
  311.7 3.2 collective-permute-start.11
  315.6 2.7 pad_maximum_fusion.26
  318.2 4.9 copy.169
  323.2 4.9 copy.170
  330.1 5.7 %copy.139 = f32[18,66,512]{1,0,2:T(8,128)} copy(f32[18,66,512]{2,1,0:T(8,128)} %pad_maximum_fusion.8) | data formatting | bytes 4866048 | tf_op jit(solution)/shard_map/concatenate | solution.py:23
  335.8 20.6 %fusion.13 = f32[16,64,512]{1,0,2:T(8,128)S(1)} fusion(f32[16,64,512]{1,0,2:T(8,128)} %fusion.72, f32[16,64,512]{1,0,2:T(8,128)} %get-tuple-element.62, f32[18,66,512]{1,0,2:T(8,128)} %copy.139, f32[16,64,512]{1,0,2:T(8,128)} %get-tuple-element.61, f32[16,64,512]{1,0,2:T(8,128)} %get-tuple-element.58, f32[1,64,512]{1,0,2:T(1,128)S(1)} %collective-permute-done.9, ...), kind=kLoop, calls=%fused_computation.33 | loop fusion | flops 11010048 | bytes 23666688 | tf_op jit(solution)/shard_map/add | solution.py:112
  358.8 4.4 collective-permute-start.13
  364.5 2.8 copy.141
  369.6 4.5 collective-permute-done.12
  375.5 4.2 collective-permute-start.15
  380.6 2.7 pad_maximum_fusion.20
  383.2 4.9 copy.171
  388.2 4.9 copy.172
  395.1 5.7 %copy.145 = f32[18,66,512]{1,0,2:T(8,128)} copy(f32[18,66,512]{2,1,0:T(8,128)} %pad_maximum_fusion.9) | data formatting | bytes 4866048 | tf_op jit(solution)/shard_map/concatenate | solution.py:23
  400.8 20.6 %fusion.21 = f32[16,64,512]{1,0,2:T(8,128)S(1)} fusion(f32[16,64,512]{1,0,2:T(8,128)} %copy-done, f32[16,64,512]{1,0,2:T(8,128)} %get-tuple-element.62, f32[18,66,512]{1,0,2:T(8,128)} %copy.145, f32[16,64,512]{1,0,2:T(8,128)} %get-tuple-element.61, f32[16,64,512]{1,0,2:T(8,128)} %get-tuple-element.58, f32[1,64,512]{1,0,2:T(1,128)S(1)} %collective-permute-done.13, ...), kind=kLoop, calls=%fused_computation.41 | loop fusion | flops 11010048 | bytes 23666688 | tf_op jit(solution)/shard_map/add | solution.py:112
  423.9 4.5 collective-permute-start.17
  429.6 2.8 copy.147
  434.6 5.6 %collective-permute-done.16 = f32[1,64,512]{1,0,2:T(1,128)S(1)} collective-permute-done((f32[1,64,512]{1,0,2:T(1,128)S(1)}, f32[1,64,512]{1,0,2:T(1,128)S(1)}, u32[]{:S(2)}, u32[]{:S(2)}) %collective-permute-start.16) | collective-permute-done | bytes 131104 | tf_op jit(solution)/shard_map/ppermute | solution.py:22
  441.9 3.0 collective-permute-start.19
  445.8 2.7 pad_maximum_fusion.14
  448.4 4.9 copy.173
  453.3 4.9 copy.174
  460.2 5.7 %copy.151 = f32[18,66,512]{1,0,2:T(8,128)} copy(f32[18,66,512]{2,1,0:T(8,128)} %pad_maximum_fusion.10) | data formatting | bytes 4866048 | tf_op jit(solution)/shard_map/concatenate | solution.py:23
  466.0 21.7 %fusion.29 = f32[16,64,512]{1,0,2:T(8,128)} fusion(f32[16,64,512]{1,0,2:T(8,128)} %copy-done.1, f32[16,64,512]{1,0,2:T(8,128)} %get-tuple-element.62, f32[18,66,512]{1,0,2:T(8,128)} %copy.151, f32[16,64,512]{1,0,2:T(8,128)} %get-tuple-element.61, f32[16,64,512]{1,0,2:T(8,128)} %get-tuple-element.58, f32[1,64,512]{1,0,2:T(1,128)S(1)} %collective-permute-done.17, ...), kind=kLoop, calls=%fused_computation.49 | loop fusion | flops 11010048 | bytes 23666688 | tf_op jit(solution)/shard_map/add | solution.py:112
  489.0 3.8 copy.152
  (98 shorter events, 49.7 us)
Async XLA Ops:
  1.6 41.6 %collective-permute-start.2 = (f32[1,64,512]{2,1,0:T(8,128)S(1)}, f32[1,64,512]{2,1,0:T(8,128)S(1)}, u32[]{:S(2)}, u32[]{:S(2)}) collective-permute-start(f32[1,64,512]{2,1,0:T(8,128)S(1)} %get-tuple-element.92), channel_id=1, source_target_pairs={{0,4},{4,8},{8,12},{12,16},{16,20},{20,24},{24,28},{1,5},{5,9},{9,... | collective-permute-start | bytes 393224 | tf_op jit(solution)/shard_map/ppermute | solution.py:19
  6.5 36.7 %collective-permute-start = (f32[1,64,512]{2,1,0:T(8,128)S(1)}, f32[1,64,512]{2,1,0:T(8,128)S(1)}, u32[]{:S(2)}, u32[]{:S(2)}) collective-permute-start(f32[1,64,512]{2,1,0:T(8,128)S(1)} %get-tuple-element.93), channel_id=1, source_target_pairs={{4,0},{8,4},{12,8},{16,12},{20,16},{24,20},{28,24},{5,1},{9,5},{13... | collective-permute-start | bytes 393224 | tf_op jit(solution)/shard_map/ppermute | solution.py:22
  8.8 45.1 %collective-permute-start.3 = (f32[1,64,512]{2,1,0:T(8,128)S(1)}, f32[1,64,512]{2,1,0:T(8,128)S(1)}, u32[]{:S(2)}, u32[]{:S(2)}) collective-permute-start(f32[1,64,512]{2,1,0:T(8,128)S(1)} %get-tuple-element.98), channel_id=1, source_target_pairs={{0,4},{4,8},{8,12},{12,16},{16,20},{20,24},{24,28},{1,5},{5,9},{9,... | collective-permute-start | bytes 393224 | tf_op jit(solution)/shard_map/ppermute | solution.py:19
  13.4 41.2 %collective-permute-start.1 = (f32[1,64,512]{2,1,0:T(8,128)S(1)}, f32[1,64,512]{2,1,0:T(8,128)S(1)}, u32[]{:S(2)}, u32[]{:S(2)}) collective-permute-start(f32[1,64,512]{2,1,0:T(8,128)S(1)} %get-tuple-element.97), channel_id=1, source_target_pairs={{4,0},{8,4},{12,8},{16,12},{20,16},{24,20},{28,24},{5,1},{9,5},{13... | collective-permute-start | bytes 393224 | tf_op jit(solution)/shard_map/ppermute | solution.py:22
  16.7 8.6 %copy-start.8 = (f32[16,128]{1,0:T(8,128)S(1)}, f32[16,128]{1,0:T(8,128)}, u32[]{:S(2)}) copy-start(f32[16,128]{1,0:T(8,128)} %param.17) | copy-start | bytes 24580
  16.7 17.2 %copy-start.9 = (s32[256,2]{0,1:T(2,128)S(1)}, s32[256,2]{0,1:T(2,128)}, u32[]{:S(2)}) copy-start(s32[256,2]{0,1:T(2,128)} %param.19) | copy-start | bytes 6148
  25.3 14.1 %copy-start.2 = (f32[16,64,512]{2,1,0:T(8,128)S(1)}, f32[16,64,512]{2,1,0:T(8,128)}, u32[]{:S(2)}) copy-start(f32[16,64,512]{2,1,0:T(8,128)} %param.15) | copy-start | bytes 6291460
  26.0 31.5 %all-to-all-start = ((f32[32,16,128]{2,1,0:T(8,128)}), f32[32,16,128]{2,1,0:T(8,128)S(1)}, u32[]{:S(2)}, u32[]{:S(2)}) async-start(f32[32,16,128]{2,1,0:T(8,128)} %broadcast_in_dim.9), calls=%async_computation | async-start | bytes 524288 | tf_op jit(solution)/shard_map/all_to_all | solution.py:54
  49.3 5.3 %copy-start.3 = (f32[18,64,512]{2,1,0:T(8,128)}, f32[18,64,512]{2,1,0:T(8,128)S(1)}, u32[]{:S(2)}) copy-start(f32[18,64,512]{2,1,0:T(8,128)S(1)} %constant_dynamic-update-slice_fusion) | copy-start | bytes 7077892
  49.3 90.8 %collective-permute-start.4 = (f32[18,1,512]{2,1,0:T(1,128)S(1)}, f32[18,1,512]{2,1,0:T(1,128)S(1)}, u32[]{:S(2)}, u32[]{:S(2)}) collective-permute-start(f32[18,1,512]{2,1,0:T(1,128)S(1)} %get-tuple-element.84), channel_id=1, source_target_pairs={{1,0},{2,1},{3,2},{5,4},{6,5},{7,6},{9,8},{10,9},{11,10},{13,12},{... | collective-permute-start | bytes 110600 | tf_op jit(solution)/shard_map/ppermute | solution.py:22
  50.6 89.5 %collective-permute-start.6 = (f32[18,1,512]{2,1,0:T(1,128)S(1)}, f32[18,1,512]{2,1,0:T(1,128)S(1)}, u32[]{:S(2)}, u32[]{:S(2)}) collective-permute-start(f32[18,1,512]{2,1,0:T(1,128)S(1)} %get-tuple-element.83), channel_id=1, source_target_pairs={{0,1},{1,2},{2,3},{4,5},{5,6},{6,7},{8,9},{9,10},{10,11},{12,13},{... | collective-permute-start | bytes 110600 | tf_op jit(solution)/shard_map/ppermute | solution.py:19
  87.6 34.8 %copy-start.7 = (f32[16,64,512]{2,1,0:T(8,128)S(1)}, f32[16,64,512]{2,1,0:T(8,128)}, u32[]{:S(2)}) copy-start(f32[16,64,512]{2,1,0:T(8,128)} %get-tuple-element.91) | copy-start | bytes 6291460
  110.0 41.7 %all-to-all-start.1 = ((f32[32,16,128]{2,1,0:T(8,128)}), f32[32,16,128]{2,1,0:T(8,128)S(1)}, u32[]{:S(2)}, u32[]{:S(2)}) async-start(f32[32,16,128]{2,1,0:T(8,128)} %bitcast.14), calls=%async_computation.1 | async-start | bytes 524288 | tf_op jit(solution)/shard_map/all_to_all | solution.py:59
  117.7 40.7 %collective-permute-start.5 = (f32[18,1,512]{2,1,0:T(1,128)S(1)}, f32[18,1,512]{2,1,0:T(1,128)S(1)}, u32[]{:S(2)}, u32[]{:S(2)}) collective-permute-start(f32[18,1,512]{2,1,0:T(1,128)S(1)} %get-tuple-element.88), channel_id=1, source_target_pairs={{1,0},{2,1},{3,2},{5,4},{6,5},{7,6},{9,8},{10,9},{11,10},{13,12},{... | collective-permute-start | bytes 110600 | tf_op jit(solution)/shard_map/ppermute | solution.py:22
  119.0 39.4 %collective-permute-start.7 = (f32[18,1,512]{2,1,0:T(1,128)S(1)}, f32[18,1,512]{2,1,0:T(1,128)S(1)}, u32[]{:S(2)}, u32[]{:S(2)}) collective-permute-start(f32[18,1,512]{2,1,0:T(1,128)S(1)} %get-tuple-element.87), channel_id=1, source_target_pairs={{0,1},{1,2},{2,3},{4,5},{5,6},{6,7},{8,9},{9,10},{10,11},{12,13},{... | collective-permute-start | bytes 110600 | tf_op jit(solution)/shard_map/ppermute | solution.py:19
  126.3 5.0 %copy-start.6 = (f32[16,64,512]{2,1,0:T(8,128)S(1)}, f32[16,64,512]{2,1,0:T(8,128)}, u32[]{:S(2)}) copy-start(f32[16,64,512]{2,1,0:T(8,128)} %get-tuple-element.90) | copy-start | bytes 6291460
  135.1 5.0 %copy-start.4 = (f32[18,64,512]{2,1,0:T(8,128)S(1)}, f32[18,64,512]{2,1,0:T(8,128)}, u32[]{:S(2)}) copy-start(f32[18,64,512]{2,1,0:T(8,128)} %copy-done.3) | copy-start | bytes 7077892
  142.8 5.0 %copy-start.5 = (f32[16,64,512]{2,1,0:T(8,128)S(1)}, f32[16,64,512]{2,1,0:T(8,128)}, u32[]{:S(2)}) copy-start(f32[16,64,512]{2,1,0:T(8,128)} %get-tuple-element.81) | copy-start | bytes 6291460
  152.5 31.5 %all-to-all-start.2 = ((f32[32,16,128]{2,1,0:T(8,128)}), f32[32,16,128]{2,1,0:T(8,128)S(1)}, u32[]{:S(2)}, u32[]{:S(2)}) async-start(f32[32,16,128]{2,1,0:T(8,128)} %broadcast_in_dim.10), calls=%async_computation.2 | async-start | bytes 524288 | tf_op jit(solution)/shard_map/all_to_all | solution.py:54
  236.4 39.0 %all-to-all-start.3 = ((f32[32,16,128]{2,1,0:T(8,128)}), f32[32,16,128]{2,1,0:T(8,128)S(1)}, u32[]{:S(2)}, u32[]{:S(2)}) async-start(f32[32,16,128]{2,1,0:T(8,128)} %bitcast.24), calls=%async_computation.3 | async-start | bytes 524288 | tf_op jit(solution)/shard_map/all_to_all | solution.py:59
  294.9 15.2 %collective-permute-start.9 = (f32[1,64,512]{1,0,2:T(1,128)S(1)}, f32[1,64,512]{1,0,2:T(1,128)S(1)}, u32[]{:S(2)}, u32[]{:S(2)}) collective-permute-start(f32[1,64,512]{1,0,2:T(1,128)S(1)} %get-tuple-element.67), channel_id=1, source_target_pairs={{0,4},{4,8},{8,12},{12,16},{16,20},{20,24},{24,28},{1,5},{5,9},{9,... | collective-permute-start | bytes 393224 | tf_op jit(solution)/shard_map/ppermute | solution.py:19
  298.6 11.6 %collective-permute-start.8 = (f32[1,64,512]{1,0,2:T(1,128)S(1)}, f32[1,64,512]{1,0,2:T(1,128)S(1)}, u32[]{:S(2)}, u32[]{:S(2)}) collective-permute-start(f32[1,64,512]{1,0,2:T(1,128)S(1)} %get-tuple-element.68), channel_id=1, source_target_pairs={{4,0},{8,4},{12,8},{16,12},{20,16},{24,20},{28,24},{5,1},{9,5},{13... | collective-permute-start | bytes 393224 | tf_op jit(solution)/shard_map/ppermute | solution.py:22
  310.4 4.6 collective-permute-start.10
  311.7 3.9 collective-permute-start.11
  356.4 2.0 copy-start
  358.8 10.7 %collective-permute-start.13 = (f32[1,64,512]{1,0,2:T(1,128)S(1)}, f32[1,64,512]{1,0,2:T(1,128)S(1)}, u32[]{:S(2)}, u32[]{:S(2)}) collective-permute-start(f32[1,64,512]{1,0,2:T(1,128)S(1)} %get-tuple-element.65), channel_id=1, source_target_pairs={{0,4},{4,8},{8,12},{12,16},{16,20},{20,24},{24,28},{1,5},{5,9},{9,... | collective-permute-start | bytes 393224 | tf_op jit(solution)/shard_map/ppermute | solution.py:19
  363.2 10.9 %collective-permute-start.12 = (f32[1,64,512]{1,0,2:T(1,128)S(1)}, f32[1,64,512]{1,0,2:T(1,128)S(1)}, u32[]{:S(2)}, u32[]{:S(2)}) collective-permute-start(f32[1,64,512]{1,0,2:T(1,128)S(1)} %get-tuple-element.66), channel_id=1, source_target_pairs={{4,0},{8,4},{12,8},{16,12},{20,16},{24,20},{28,24},{5,1},{9,5},{13... | collective-permute-start | bytes 393224 | tf_op jit(solution)/shard_map/ppermute | solution.py:22
  374.2 5.5 %collective-permute-start.14 = (f32[18,1,512]{2,1,0:T(1,128)S(1)}, f32[18,1,512]{2,1,0:T(1,128)S(1)}, u32[]{:S(2)}, u32[]{:S(2)}) collective-permute-start(f32[18,1,512]{2,1,0:T(1,128)S(1)} %get-tuple-element.76), channel_id=1, source_target_pairs={{1,0},{2,1},{3,2},{5,4},{6,5},{7,6},{9,8},{10,9},{11,10},{13,12},{... | collective-permute-start | bytes 110600 | tf_op jit(solution)/shard_map/ppermute | solution.py:22
  375.5 5.0 %collective-permute-start.15 = (f32[18,1,512]{2,1,0:T(1,128)S(1)}, f32[18,1,512]{2,1,0:T(1,128)S(1)}, u32[]{:S(2)}, u32[]{:S(2)}) collective-permute-start(f32[18,1,512]{2,1,0:T(1,128)S(1)} %get-tuple-element.75), channel_id=1, source_target_pairs={{0,1},{1,2},{2,3},{4,5},{5,6},{6,7},{8,9},{9,10},{10,11},{12,13},{... | collective-permute-start | bytes 110600 | tf_op jit(solution)/shard_map/ppermute | solution.py:19
  421.4 2.1 copy-start.1
  423.9 10.6 %collective-permute-start.17 = (f32[1,64,512]{1,0,2:T(1,128)S(1)}, f32[1,64,512]{1,0,2:T(1,128)S(1)}, u32[]{:S(2)}, u32[]{:S(2)}) collective-permute-start(f32[1,64,512]{1,0,2:T(1,128)S(1)} %get-tuple-element.63), channel_id=1, source_target_pairs={{0,4},{4,8},{8,12},{12,16},{16,20},{20,24},{24,28},{1,5},{5,9},{9,... | collective-permute-start | bytes 393224 | tf_op jit(solution)/shard_map/ppermute | solution.py:19
  428.3 11.8 %collective-permute-start.16 = (f32[1,64,512]{1,0,2:T(1,128)S(1)}, f32[1,64,512]{1,0,2:T(1,128)S(1)}, u32[]{:S(2)}, u32[]{:S(2)}) collective-permute-start(f32[1,64,512]{1,0,2:T(1,128)S(1)} %get-tuple-element.64), channel_id=1, source_target_pairs={{4,0},{8,4},{12,8},{16,12},{20,16},{24,20},{28,24},{5,1},{9,5},{13... | collective-permute-start | bytes 393224 | tf_op jit(solution)/shard_map/ppermute | solution.py:22
  440.3 4.6 collective-permute-start.18
  441.9 3.9 collective-permute-start.19

commit v2 on v0

v2 whole, which is shorter than its diff:
```python
import functools

import jax
import jax.numpy as jnp
from jax import lax
from jax.experimental import pallas as pl
from jax.experimental.pallas import tpu as pltpu
from jax.sharding import PartitionSpec as P

BLK = 128
SWEEPS = 2
STEPS = 4
HALO = STEPS
LANES = 128
CHUNK = 16

step_size = 0.07

NT = (((1,), (1,)), ((), ()))
NN = (((1,), (0,)), ((), ()))


def params(mib):
    return pltpu.CompilerParams(vmem_limit_bytes=mib * 1024 * 1024)


def cost(flops, nbytes):
    return pl.CostEstimate(flops=flops, bytes_accessed=nbytes, transcendentals=0)


def parts_of(x, count):
    out = []
    for _ in range(count - 1):
        part = x.astype(jnp.bfloat16)
        out.append(part)
        x = x - part.astype(jnp.float32)
    out.append(x.astype(jnp.bfloat16))
    return out


def emit_kernel(plane_ref, site_ref, mirror_ref, emitted_ref, copies_ref):
    sheets = plane_ref.shape[0]
    for half in range(site_ref.shape[0] // 8):
        rows = pl.ds(half * 8, 8)
        site = site_ref[rows, :]
        lane = site & (LANES - 1)
        sheet = site >> 7
        warmth = jnp.zeros(site.shape, jnp.float32)
        for r in range(sheets):
            line = jnp.broadcast_to(plane_ref[r : r + 1, :], site.shape)
            picked = jnp.take_along_axis(line, lane, axis=1)
            warmth = jnp.where(sheet == r, picked, warmth)
        square = warmth * warmth
        emitted = (1.0 - mirror_ref[rows, :]) * (square * square)
        emitted_ref[rows, :] = emitted
        for d in range(copies_ref.shape[0]):
            copies_ref[d, rows, :] = emitted


def emit(plane, site, mirror, count):
    shape = mirror.shape
    return pl.pallas_call(
        emit_kernel,
        out_shape=(
            jax.ShapeDtypeStruct(shape, jnp.float32),
            jax.ShapeDtypeStruct((count,) + shape, jnp.float32),
        ),
        compiler_params=params(8),
        cost_estimate=cost(10_000, 400_000),
        name="emit",
    )(plane, site, mirror)


def tiles_kernel(
    live_ref, pairs_ref, lanes_ref, whole_ref, tiles_ref, out_ref, held, terms, sems
):
    slots = held.shape[0]
    live = live_ref[0]
    chunks = (live + CHUNK - 1) // CHUNK

    def chunk_copy(c):
        span = pl.ds(c * CHUNK, CHUNK)
        return pltpu.make_async_copy(tiles_ref.at[span], held.at[span], sems.at[c])

    @pl.loop(0, chunks)
    def _(c):
        chunk_copy(c).start()

    top = lax.broadcasted_iota(jnp.int32, (8, BLK), 0) == 0

    def split_row(block):
        row = jnp.broadcast_to(whole_ref[pl.ds(block, 1), :], (8, BLK))
        high = row.astype(jnp.bfloat16).astype(jnp.float32)
        return jnp.where(top, high, row - high)

    def vectors(a, b):
        stacked = jnp.concatenate([split_row(a), split_row(b)], axis=0)
        stacked = stacked.astype(jnp.bfloat16)
        return jnp.concatenate([stacked, stacked], axis=1)

    @pl.loop(0, chunks)
    def _(c):
        chunk_copy(c).wait()
        for u in range(0, CHUNK, 2):
            t = c * CHUNK + u
            high_a, low_a = parts_of(held[t], 2)
            high_b, low_b = parts_of(held[t + 1], 2)
            both = jnp.concatenate(
                [
                    jnp.concatenate([high_a, high_b], axis=1),
                    jnp.concatenate([low_a, low_b], axis=1),
                ],
                axis=0,
            )
            second = lax.dot_general(
                vectors(pairs_ref[0, t], pairs_ref[0, t + 1]),
                both,
                NN,
                preferred_element_type=jnp.float32,
            )
            turned = jnp.concatenate(
                [
                    jnp.concatenate([high_a, low_a], axis=1),
                    jnp.concatenate([high_b, low_b], axis=1),
                ],
                axis=0,
            )
            first = lax.dot_general(
                vectors(pairs_ref[1, t], pairs_ref[1, t + 1]),
                turned,
                NT,
                preferred_element_type=jnp.float32,
            )
            for side, result in ((0, first), (1, second)):
                terms[side, pl.ds(t, 1), :] = result[0:1, :BLK] + result[1:2, :BLK]
                terms[side, pl.ds(t + 1, 1), :] = result[8:9, BLK:] + result[9:10, BLK:]

    used = lax.broadcasted_iota(jnp.int32, (slots, BLK), 0) < live
    used_lane = lax.broadcasted_iota(jnp.int32, (1, slots), 1) < live
    blocks = out_ref.shape[0]
    group = min(blocks, 512)
    split = []
    for side in range(2):
        masked = jnp.where(used, terms[side], 0.0)
        split.append(jnp.concatenate(parts_of(masked, 2), axis=1))
    for base in range(0, blocks, group):
        rows = lax.broadcasted_iota(jnp.int32, (group, slots), 0) + base
        total = jnp.zeros((group, 2 * BLK), jnp.float32)
        for side in range(2):
            target = jnp.where(used_lane, lanes_ref[side : side + 1, :], -1)
            choose = jnp.where(rows == target, 1.0, 0.0).astype(jnp.bfloat16)
            total = total + jnp.dot(choose, split[side], preferred_element_type=jnp.float32)
        out_ref[base : base + group, :] = total[:, :BLK] + total[:, BLK:]


def tile_terms(whole, couples, live, tiles):
    slots = tiles.shape[0]
    smem = pl.BlockSpec(memory_space=pltpu.SMEM)
    vmem = pl.BlockSpec(memory_space=pltpu.VMEM)
    return pl.pallas_call(
        tiles_kernel,
        out_shape=jax.ShapeDtypeStruct(whole.shape, jnp.float32),
        in_specs=[smem, smem, vmem, vmem, pl.BlockSpec(memory_space=pl.ANY)],
        out_specs=vmem,
        scratch_shapes=[
            pltpu.VMEM(tiles.shape, jnp.float32),
            pltpu.VMEM((2, slots, BLK), jnp.float32),
            pltpu.SemaphoreType.DMA((slots // CHUNK,)),
        ],
        compiler_params=params(36),
        cost_estimate=cost(slots * BLK * BLK * 32, slots * BLK * BLK * 4),
        name="tiles",
    )(live, couples, couples, whole, tiles)


def sum_parts(parts_ref, rows):
    total = parts_ref[0, rows, :]
    for d in range(1, parts_ref.shape[0]):
        total = total + parts_ref[d, rows, :]
    return total


def middle_kernel(parts_ref, emitted_ref, mirror_ref, copies_ref):
    for half in range(emitted_ref.shape[0] // 8):
        rows = pl.ds(half * 8, 8)
        incident = sum_parts(parts_ref, rows)
        radiosity = emitted_ref[rows, :] + mirror_ref[rows, :] * incident
        for d in range(copies_ref.shape[0]):
            copies_ref[d, rows, :] = radiosity


def middle(parts, emitted, mirror):
    return pl.pallas_call(
        middle_kernel,
        out_shape=jax.ShapeDtypeStruct(parts.shape, jnp.float32),
        compiler_params=params(8),
        cost_estimate=cost(100_000, 600_000),
        name="middle",
    )(parts, emitted, mirror)


def last_kernel(scale, parts_ref, emitted_ref, mirror_ref, site_ref, rad_ref, source_ref):
    blocks = emitted_ref.shape[0]
    incident = sum_parts(parts_ref, slice(None))
    emitted = emitted_ref[...]
    mirror = mirror_ref[...]
    rad_ref[...] = emitted + mirror * incident
    absorbed = ((1.0 - mirror) * incident - emitted) * scale
    site = site_ref[...]
    lane = site & (LANES - 1)
    sheet = site >> 7
    sheets = source_ref.shape[1]
    sheet_iota = lax.broadcasted_iota(jnp.int32, (sheets, BLK), 0)
    lane_iota = lax.broadcasted_iota(jnp.int32, (LANES, BLK), 0)
    left = []
    right = []
    for b in range(blocks):
        here = jnp.where(sheet_iota == sheet[b : b + 1, :], absorbed[b : b + 1, :], 0.0)
        left.append(here)
        pick = jnp.where(lane_iota == lane[b : b + 1, :], 1.0, 0.0)
        right.append(pick.astype(jnp.bfloat16))
    left = jnp.concatenate(left, axis=1)
    right = jnp.concatenate(right, axis=1)
    source = jnp.zeros((sheets, LANES), jnp.float32)
    for part in parts_of(left, 3):
        source = source + lax.dot_general(part, right, NT, preferred_element_type=jnp.float32)
    for d in range(source_ref.shape[0]):
        source_ref[d] = source


def last(parts, emitted, mirror, site, cells):
    count = parts.shape[0]
    weight = cells / (mirror.shape[0] * BLK * 1.0)
    return pl.pallas_call(
        functools.partial(last_kernel, step_size * weight),
        out_shape=(
            jax.ShapeDtypeStruct(mirror.shape, jnp.float32),
            jax.ShapeDtypeStruct((count, cells // LANES, LANES), jnp.float32),
        ),
        compiler_params=params(16),
        cost_estimate=cost(10_000_000, 600_000),
        name="last",
    )(parts, emitted, mirror, site)


def pack_x_kernel(t_low, k_low, t_high, k_high, low_ref, high_ref):
    low_ref[:HALO] = t_low[...]
    low_ref[HALO:] = k_low[...]
    high_ref[:HALO] = t_high[...]
    high_ref[HALO:] = k_high[...]


def pack_x(temp, cond):
    nx, ny, nz = temp.shape
    first = pl.BlockSpec((HALO, ny, nz), lambda i: (0, 0, 0))
    final = pl.BlockSpec((HALO, ny, nz), lambda i: (nx // HALO - 1, 0, 0))
    whole = pl.BlockSpec((2 * HALO, ny, nz), lambda i: (0, 0, 0))
    shape = jax.ShapeDtypeStruct((2 * HALO, ny, nz), jnp.float32)
    return pl.pallas_call(
        pack_x_kernel,
        grid=(1,),
        out_shape=(shape, shape),
        in_specs=[first, first, final, final],
        out_specs=(whole, whole),
        compiler_params=params(20),
        cost_estimate=cost(0, 4 * 2 * HALO * ny * nz * 4),
        name="pack_x",
    )(temp, cond, temp, cond)


def pack_y_kernel(nx, t0, k0, t7, k7, lo0, hi0, lo7, hi7, down_ref, up_ref):
    upper = lax.broadcasted_iota(jnp.int32, down_ref.shape[1:], 0) < HALO

    def put(x, t_first, k_first, t_final, k_final):
        down_ref[x] = jnp.where(upper, t_first, pltpu.roll(k_first, HALO, 0))
        up_ref[x] = jnp.where(upper, pltpu.roll(t_final, HALO, 0), k_final)

    for x in range(HALO):
        put(x, lo0[x], lo0[HALO + x], lo7[x], lo7[HALO + x])
        put(HALO + nx + x, hi0[x], hi0[HALO + x], hi7[x], hi7[HALO + x])
    for x in range(nx):
        put(HALO + x, t0[x], k0[x], t7[x], k7[x])


def pack_y(temp, cond, low, high):
    nx, ny, nz = temp.shape

    def edges(planes):
        return (
            pl.BlockSpec((planes, 8, nz), lambda i: (0, 0, 0)),
            pl.BlockSpec((planes, 8, nz), lambda i: (0, ny // 8 - 1, 0)),
        )

    first, final = edges(nx)
    halo_first, halo_final = edges(2 * HALO)
    tall = nx + 2 * HALO
    whole = pl.BlockSpec((tall, 8, nz), lambda i: (0, 0, 0))
    shape = jax.ShapeDtypeStruct((tall, 8, nz), jnp.float32)
    return pl.pallas_call(
        functools.partial(pack_y_kernel, nx),
        grid=(1,),
        out_shape=(shape, shape),
        in_specs=[first, first, final, final, halo_first, halo_first, halo_final, halo_final],
        out_specs=(whole, whole),
        compiler_params=params(20),
        cost_estimate=cost(0, 4 * tall * 8 * nz * 4),
        name="pack_y",
    )(temp, cond, temp, cond, low, high, low, high)


def coupling(a, b):
    return jnp.where(jnp.minimum(a, b) > 0.0, (0.5 * step_size) * (a + b), 0.0)


def heat_kernel(
    t_ref, k_ref, low_ref, high_ref, below_ref, above_ref, out_ref, thin_ref,
    field, cond, centre, cx, cy, cz,
):
    nx, ny, nz = t_ref.shape
    tall = nx + 2 * HALO
    wide = ny + 2 * HALO
    upper = lax.broadcasted_iota(jnp.int32, (8, nz), 0) < HALO

    field[0, :HALO, :ny] = low_ref[:HALO]
    field[0, HALO : HALO + nx, :ny] = t_ref[...]
    field[0, HALO + nx :, :ny] = high_ref[:HALO]
    cond[:HALO, :ny] = low_ref[HALO:]
    cond[HALO : HALO + nx, :ny] = k_ref[...]
    cond[HALO + nx :, :ny] = high_ref[HALO:]

    @pl.loop(0, tall)
    def _(x):
        down = above_ref[x]
        up = below_ref[x]
        field[0, x, ny:] = jnp.where(upper, down, pltpu.roll(up, HALO, 0))
        cond[x, ny:] = jnp.where(upper, pltpu.roll(down, HALO, 0), up)

    depth = lax.broadcasted_iota(jnp.int32, (wide, nz), 1)

    @pl.loop(0, tall)
    def _(x):
        here = cond[x]
        outer = here * 0.0
        total = 6.0 * here
        after = cond[jnp.minimum(x + 1, tall - 1)]
        before = cond[jnp.maximum(x - 1, 0)]
        cx[x] = coupling(here, after)
        y_after = pltpu.roll(here, wide - 1, 0)
        y_before = pltpu.roll(here, 1, 0)
        cy[x] = coupling(here, y_after)
        z_after = jnp.where(depth == nz - 1, outer, pltpu.roll(here, nz - 1, 1))
        z_before = jnp.where(depth == 0, outer, pltpu.roll(here, 1, 1))
        cz[x] = coupling(here, z_after)
        for near in (after, before, y_after, y_before, z_after, z_before):
            total = total + jnp.where(near > 0.0, near, here)
        centre[x] = 1.0 - (0.5 * step_size) * total

    def update(old, x):
        here = field[old, x]
        new = centre[x] * here
        new = new + (cx[x] * field[old, x + 1] + cx[x - 1] * field[old, x - 1])
        new = new + cy[x] * pltpu.roll(here, wide - 1, 0)
        new = new + pltpu.roll(cy[x] * here, 1, 0)
        new = new + cz[x] * pltpu.roll(here, nz - 1, 1)
        return new + pltpu.roll(cz[x] * here, 1, 1)

    @pl.loop(0, STEPS - 1)
    def _(step):
        old = step & 1

        @pl.loop(1 + step, tall - 1 - step)
        def _(x):
            field[1 - old, x] = update(old, x)

    @pl.loop(0, nx)
    def _(x):
        out_ref[x] = update((STEPS - 1) & 1, x + HALO)[:ny]

    lane = lax.broadcasted_iota(jnp.int32, (wide, LANES), 1)
    y_lane = lax.broadcasted_iota(jnp.int32, (8, LANES), 1)
    for base in range(0, tall, 16):
        planes = min(16, tall - base)
        gathered = jnp.zeros((wide, LANES), jnp.float32)
        for g in range(planes):
            piece = cond[base + g, :, :LANES]
            if g:
                piece = pltpu.roll(piece, 8 * g, 1)
            gathered = jnp.where((lane >> 3) == g, piece, gathered)
        square = jnp.concatenate(
            [gathered, jnp.zeros((LANES - wide, LANES), jnp.float32)], axis=0
        )
        turned = square.T
        for g in range(planes):
            rows = turned[8 * g : 8 * g + 8, :]
            moved = pltpu.roll(rows, LANES - wide, 1)
            thin_ref[base + g] = jnp.where(
                y_lane < ny + HALO, rows, jnp.where(y_lane >= LANES - HALO, moved, 0.0)
            )


def heat(temp, cond, low, high, below, above):
    nx, ny, nz = temp.shape
    tall, wide = nx + 2 * HALO, ny + 2 * HALO
    big = pltpu.VMEM((tall, wide, nz), jnp.float32)
    return pl.pallas_call(
        heat_kernel,
        out_shape=(
            jax.ShapeDtypeStruct(temp.shape, jnp.float32),
            jax.ShapeDtypeStruct((tall, 8, LANES), jnp.float32),
        ),
        scratch_shapes=[pltpu.VMEM((2, tall, wide, nz), jnp.float32)] + [big] * 5,
        compiler_params=params(48),
        cost_estimate=cost(tall * wide * nz * 100, 12 * nx * ny * nz * 4),
        name="heat",
    )(temp, cond, low, high, below, above)


def source_kernel(ny, near_ref, flag_ref, all_ref, thin_ref, base_ref, out_ref):
    tall = thin_ref.shape[0]
    nx = tall - 2 * HALO
    sheets = all_ref.shape[1]
    sub = lax.broadcasted_iota(jnp.int32, (8, LANES), 0)
    y_lane = lax.broadcasted_iota(jnp.int32, (8, LANES), 1)

    def sheet(k):
        return all_ref[near_ref[k]] * flag_ref[k].astype(jnp.float32)

    def rows_of(slab):
        low, own, high = (sheet(3 * slab + k) for k in range(3))
        out = []
        for half in range(2):
            if half == 0:
                own_at, high_at, low_at = own, pltpu.roll(high, ny, 1), pltpu.roll(low, ny, 1)
            else:
                own_at, high_at, low_at = pltpu.roll(own, ny, 1), high, low
            out.append(
                jnp.where(
                    y_lane < ny,
                    own_at,
                    jnp.where(
                        y_lane < ny + HALO,
                        high_at,
                        jnp.where(y_lane >= LANES - HALO, low_at, 0.0),
                    ),
                )
            )
        return out

    lines = [rows_of(s) for s in range(3)]
    source = []
    for x in range(-HALO, nx + HALO):
        which, local = (x + nx) // nx, x % nx
        row = lines[which][local % 2][local // 2 : local // 2 + 1, :]
        source.append(jnp.where(sub == 0, jnp.broadcast_to(row, (8, LANES)), 0.0))

    cond = [thin_ref[x] for x in range(tall)]
    cx, cy, cz, centre = [], [], [], []
    for x in range(tall):
        here = cond[x]
        after = cond[min(x + 1, tall - 1)]
        before = cond[max(x - 1, 0)]
        y_after = pltpu.roll(here, LANES - 1, 1)
        y_before = pltpu.roll(here, 1, 1)
        z_after = jnp.where(sub == 7, 0.0, pltpu.roll(here, 7, 0))
        z_before = jnp.where(sub == 0, 0.0, pltpu.roll(here, 1, 0))
        cx.append(coupling(here, after))
        cy.append(coupling(here, y_after))
        cz.append(coupling(here, z_after))
        total = 6.0 * here
        for near in (after, before, y_after, y_before, z_after, z_before):
            total = total + jnp.where(near > 0.0, near, here)
        centre.append(1.0 - (0.5 * step_size) * total)

    added = source
    for step in range(1, STEPS):
        new = list(added)
        for x in range(step, tall - step):
            here = added[x]
            total = source[x] + centre[x] * here
            total = total + (cx[x] * added[x + 1] + cx[x - 1] * added[x - 1])
            total = total + cy[x] * pltpu.roll(here, LANES - 1, 1)
            total = total + pltpu.roll(cy[x] * here, 1, 1)
            total = total + cz[x] * pltpu.roll(here, 7, 0)
            new[x] = total + pltpu.roll(cz[x] * here, 1, 0)
        added = new

    lane = lax.broadcasted_iota(jnp.int32, (ny, LANES), 1)
    turned = jnp.concatenate(added[HALO : HALO + nx], axis=0).T[:ny]
    for x in range(nx):
        piece = turned if x == 0 else pltpu.roll(turned, LANES - 8 * x, 1)
        out_ref[x] = base_ref[x] + jnp.where(lane < STEPS, piece, 0.0)


def add_source(near, flag, everything, thin, base):
    nx, ny, nz = base.shape
    smem = pl.BlockSpec(memory_space=pltpu.SMEM)
    block = pl.BlockSpec((nx, ny, LANES), lambda i: (0, 0, 0))
    return pl.pallas_call(
        functools.partial(source_kernel, ny),
        grid=(1,),
        out_shape=jax.ShapeDtypeStruct(base.shape, jnp.float32),
        in_specs=[
            smem,
            smem,
            pl.BlockSpec(everything.shape, lambda i: (0, 0, 0)),
            pl.BlockSpec(thin.shape, lambda i: (0, 0, 0)),
            block,
        ],
        out_specs=block,
        input_output_aliases={4: 0},
        compiler_params=params(16),
        cost_estimate=cost(1_000_000, 2 * nx * ny * LANES * 4),
        name="add_source",
    )(near, flag, everything, thin, base)


def exchange(copies):
    return lax.all_to_all(copies, ("slab", "pair"), split_axis=0, concat_axis=0, tiled=True)


def both_ways(low, high, axis):
    count = lax.axis_size(axis)
    forward = [(i, i + 1) for i in range(count - 1)]
    backward = [(target, source) for source, target in forward]
    from_low = lax.ppermute(high, axis, forward)
    from_high = lax.ppermute(low, axis, backward)
    return from_low, from_high


def shards(
    initial_warmth,
    heat_passing_coefficient,
    mirror_fraction,
    element_facing_site,
    tile_block_couples,
    active_slot_count,
    view_factor_blocks,
):
    nx, ny, _ = initial_warmth.shape
    slabs, pairs = lax.axis_size("slab"), lax.axis_size("pair")
    count = slabs * pairs
    blocks = mirror_fraction.shape[0]
    cells = nx * ny
    plane = initial_warmth[:, :, 0].reshape(cells // LANES, LANES)
    couples = tile_block_couples.T

    emitted, copies = emit(plane, element_facing_site, mirror_fraction, count)
    for sweep in range(SWEEPS):
        whole = exchange(copies).reshape(count * blocks, BLK)
        term = tile_terms(whole, couples, active_slot_count, view_factor_blocks)
        parts = exchange(term.reshape(count, blocks, BLK))
        if sweep + 1 < SWEEPS:
            copies = middle(parts, emitted, mirror_fraction)
    radiosity, source = last(parts, emitted, mirror_fraction, element_facing_site, cells)
    everything = exchange(source)

    send_low, send_high = pack_x(initial_warmth, heat_passing_coefficient)
    low, high = both_ways(send_low, send_high, "slab")
    send_down, send_up = pack_y(initial_warmth, heat_passing_coefficient, low, high)
    below, above = both_ways(send_down, send_up, "pair")
    base, thin = heat(initial_warmth, heat_passing_coefficient, low, high, below, above)

    slab, pair = lax.axis_index("slab"), lax.axis_index("pair")
    near, flag = [], []
    for ds in (-1, 0, 1):
        for dp in (-1, 0, 1):
            s, p = slab + ds, pair + dp
            inside = (s >= 0) & (s < slabs) & (p >= 0) & (p < pairs)
            near.append(jnp.where(inside, s * pairs + p, 0))
            flag.append(inside)
    near = jnp.stack(near).astype(jnp.int32)
    flag = jnp.stack(flag).astype(jnp.int32)
    warmed_liner = add_source(near, flag, everything, thin, base)
    return (radiosity, warmed_liner)


def solution(mesh):
    return jax.shard_map(
        shards,
        mesh=mesh,
        in_specs=(
            P("slab", "pair", None),
            P("slab", "pair", None),
            P(("slab", "pair"), None),
            P(("slab", "pair"), None),
            P(("slab", "pair"), None),
            P(("slab", "pair")),
            P(("slab", "pair"), None, None),
        ),
        out_specs=(P(("slab", "pair"), None), P("slab", "pair", None)),
        check_vma=False,
    )
```

time: 708 us -> 161 us (0.23); the launches traced: 695 us -> 161 us
  other arithmetic: 157 us -> 0.01 us
  waiting for transfers between devices: 165 us -> 15.3 us
  local copies, waits for them, and re-layouts: 140 us -> 18.3 us
  matrix products: 89.2 us -> 0 us
  Pallas kernels: 0 us -> 37.1 us
  blocking collectives: 80.8 us -> 44.6 us
  between operations: 15.9 us -> 1.49 us
    reduce_scatter x2 -> x0, waiting for transfers between devices: 144 us -> none  [spread_back(): lax.psum_scatter(term, ('slab', 'pair'), scatter_dimension=0, tiled=True)]
    add x5 -> x0, other arithmetic: 96.7 us -> none  [the longest x4 96 us: shards(): warmed_liner + step_size * heat_flux(temp_pad, cond_pad, warmed_liner, he...]
    dot_general x4 -> x0, matrix products: 89.2 us -> none  [the longest x2 58.1 us: tile_terms(): jnp.einsum('tpq,tq->tp', view_factor_blocks, second, precision=lax.Precis...]
    all_gather x2 -> x0, blocking collectives: 80.8 us -> none  [collect(): return lax.all_gather(radiosity, ('slab', 'pair'), axis=0, tiled=True)]
    unnamed x45 -> x22, local copies, waits for them, and re-layouts: 86.2 us -> 16.8 us
    all_to_all x0 -> x1, blocking collectives: none -> 44.6 us  [exchange(): lax.all_to_all(copies, ('slab', 'pair'), split_axis=0, concat_axis=0, til...]
    pallas_call x0 -> x9, Pallas kernels: none -> 37.1 us  [the longest x1 21.9 us: heat(): pl.pallas_call(heat_kernel, out_shape=(jax.ShapeDtypeStruct(temp.shape, j...]
    ppermute x20 -> x4, starting transfers between devices: 46 us -> 9.2 us  [the longest x2 6.63 us: both_ways(): from_low = lax.ppermute(high, axis, forward)]
  transfers between devices with their start and end apart: 22 -> 8, of which waited for: 8 -> 3; matrix products, arithmetic and copies ran while one was open for 25% -> 0% of each run, Pallas kernels for 0% -> 19%
where the time goes in v2:
time: 161 us
  blocking collectives  44.6 us (28%)
  starting transfers between devices  44.5 us (28%)
  Pallas kernels  37.1 us (23%)
  local copies, waits for them, and re-layouts  18.3 us (11%)
  waiting for transfers between devices  15.3 us (10%)
    all_to_all x1, blocking collectives, exchange(): lax.all_to_all(copies, ('slab', 'pair'), split_axis=0, concat_axis=0, til...  44.6 us
    all_to_all x4, starting transfers between devices, exchange(): lax.all_to_all(copies, ('slab', 'pair'), split_axis=0, concat_axis=0, til...  35.3 us
    pallas_call x1, Pallas kernels, heat(): pl.pallas_call(heat_kernel, out_shape=(jax.ShapeDtypeStruct(temp.shape, j...  21.9 us
    unnamed x22, local copies, waits for them, and re-layouts  16.8 us
    all_to_all x4, waiting for transfers between devices, exchange(): lax.all_to_all(copies, ('slab', 'pair'), split_axis=0, concat_axis=0, til...  15.3 us
    pallas_call x2, Pallas kernels, tile_terms(): pl.pallas_call(tiles_kernel, out_shape=jax.ShapeDtypeStruct(whole.shape,...  7.22 us
    ppermute x2, starting transfers between devices, both_ways(): from_low = lax.ppermute(high, axis, forward)  6.63 us
  transfers between devices with their start and end apart: 8, of which 3 were waited for; matrix products, arithmetic and copies ran while one was open for 0% of the time, Pallas kernels for 19%

profile of v2, /device:TPU:0, one launch (start us, length us, event | category | flops | bytes accessed | tf_op | source)
XLA Modules:
  0.0 161.3 jit_solution(11793753999887746190)
XLA Ops:
  0.6 1.3 slice_reduce_fusion
  1.9 0.1 reshape_squeeze.3.plane_ref
  2.0 0.0 copy-start.5
  2.0 0.7 copy-done.5
  2.7 0.0 copy-start.9
  2.7 0.7 copy-done.9
  3.4 0.8 emit.1
  4.2 7.3 %all-to-all-start = ((f32[32,16,128]{2,1,0:T(8,128)}), f32[32,16,128]{2,1,0:T(8,128)S(1)}, u32[]{:S(2)}, u32[]{:S(2)}) async-start(f32[32,16,128]{2,1,0:T(8,128)} %get-tuple-element.12), calls=%async_computation | async-start | bytes 524288 | tf_op jit(solution)/shard_map/all_to_all | solution.py:518
  12.1 10.0 %all-to-all-done = f32[32,16,128]{2,1,0:T(8,128)S(1)} async-done(((f32[32,16,128]{2,1,0:T(8,128)}), f32[32,16,128]{2,1,0:T(8,128)S(1)}, u32[]{:S(2)}, u32[]{:S(2)}) %all-to-all-start) | async-done | bytes 262176 | tf_op jit(solution)/shard_map/all_to_all | solution.py:518
  22.1 0.0 copy-start
  22.1 5.8 %copy-done = f32[256,128,128]{2,1,0:T(8,128)S(1)} copy-done((f32[256,128,128]{2,1,0:T(8,128)S(1)}, f32[256,128,128]{2,1,0:T(8,128)}, u32[]{:S(2)}) %copy-start) | copy-done | bytes 16777240
  27.8 0.0 copy-start.7
  27.8 0.7 copy-done.7
  28.5 0.0 copy-start.2
  28.5 3.6 %tiles.2 = f32[512,128]{1,0:T(8,128)} custom-call(s32[1]{0:T(128)S(6)} %copy.11.live_ref, s32[2,256]{1,0:T(2,128)S(1)} %bitcast.25, s32[2,256]{1,0:T(2,128)S(1)} %bitcast.26, f32[512,128]{1,0:T(8,128)S(1)} %bitcast.23, f32[256,128,128]{2,1,0:T(8,128)S(1)} %copy-done), custom_call_target="tpu_custom_call" | custom-call | flops 134217728 | bytes 16777216 | tf_op jit(solution)/shard_map/tiles/pallas_call | solution.py:160
  32.1 10.4 %all-to-all-start.1 = ((f32[32,16,128]{2,1,0:T(8,128)}), f32[32,16,128]{2,1,0:T(8,128)S(1)}, u32[]{:S(2)}, u32[]{:S(2)}) async-start(f32[32,16,128]{2,1,0:T(8,128)} %bitcast.2), calls=%async_computation.1 | async-start | bytes 524288 | tf_op jit(solution)/shard_map/all_to_all | solution.py:518
  42.6 0.0 copy-done.2
  42.6 0.0 copy-start.3
  42.6 1.6 copy-done.3
  44.2 0.0 copy-start.6
  44.2 0.0 copy-start.8
  44.2 1.4 pack_x.1
  45.6 3.7 %collective-permute-start = (f32[8,64,512]{2,1,0:T(8,128)}, f32[8,64,512]{2,1,0:T(8,128)S(1)}, u32[]{:S(2)}, u32[]{:S(2)}) collective-permute-start(f32[8,64,512]{2,1,0:T(8,128)} %get-tuple-element.16), channel_id=1, source_target_pairs={{0,4},{4,8},{8,12},{12,16},{16,20},{20,24},{24,28},{1,5},{5,9},{9,... | collective-permute-start | bytes 3145736 | tf_op jit(solution)/shard_map/ppermute | solution.py:525
  49.4 1.3 collective-permute-start.1
  50.7 2.5 %all-to-all-done.1.parts_ref = f32[32,16,128]{2,1,0:T(8,128)S(1)} async-done(((f32[32,16,128]{2,1,0:T(8,128)}), f32[32,16,128]{2,1,0:T(8,128)S(1)}, u32[]{:S(2)}, u32[]{:S(2)}) %all-to-all-start.1) | async-done | bytes 262176 | tf_op jit(solution)/shard_map/all_to_all | solution.py:518
  53.2 0.0 copy-done.6
  53.2 0.1 middle.1
  53.2 44.6 %all_to_all.25 = f32[32,16,128]{2,1,0:T(8,128)S(1)} all-to-all(f32[32,16,128]{2,1,0:T(8,128)S(1)} %middle.1), channel_id=1, replica_groups=mesh['slab'=8,'pair'=4] {'slab','pair'}, dimensions={0} | all-to-all | bytes 524288 | tf_op jit(solution)/shard_map/all_to_all | solution.py:518
  97.9 0.0 copy-done.8
  97.9 0.0 copy-start.1
  97.9 5.8 %copy-done.1 = f32[256,128,128]{2,1,0:T(8,128)S(1)} copy-done((f32[256,128,128]{2,1,0:T(8,128)S(1)}, f32[256,128,128]{2,1,0:T(8,128)}, u32[]{:S(2)}) %copy-start.1) | copy-done | bytes 16777240
  103.6 3.6 %tiles.3 = f32[512,128]{1,0:T(8,128)} custom-call(s32[1]{0:T(128)S(6)} %copy.11.live_ref, s32[2,256]{1,0:T(2,128)S(1)} %bitcast.27, s32[2,256]{1,0:T(2,128)S(1)} %bitcast.28, f32[512,128]{1,0:T(8,128)S(1)} %bitcast.24, f32[256,128,128]{2,1,0:T(8,128)S(1)} %copy-done.1), custom_call_target="tpu_custom_call" | custom-call | flops 134217728 | bytes 16777216 | tf_op jit(solution)/shard_map/tiles/pallas_call | solution.py:160
  107.3 0.0 copy-start.10
  107.3 13.2 %all-to-all-start.3 = ((f32[32,16,128]{2,1,0:T(8,128)}), f32[32,16,128]{2,1,0:T(8,128)S(1)}, u32[]{:S(2)}, u32[]{:S(2)}) async-start(f32[32,16,128]{2,1,0:T(8,128)} %bitcast.4), calls=%async_computation.3 | async-start | bytes 524288 | tf_op jit(solution)/shard_map/all_to_all | solution.py:518
  120.4 0.0 collective-permute-done.lo0.lo7.low_ref
  120.5 0.0 collective-permute-done.1.hi0.hi7.high_ref
  120.5 0.0 copy-start.4
  120.5 1.6 copy-done.4
  122.1 2.0 %pack_y.1 = (f32[24,8,512]{2,1,0:T(8,128)}, f32[24,8,512]{2,1,0:T(8,128)}) custom-call(f32[16,64,512]{2,1,0:T(8,128)S(1)} %copy-done.2, f32[16,64,512]{2,1,0:T(8,128)S(1)} %copy-done.4, f32[16,64,512]{2,1,0:T(8,128)S(1)} %copy-done.2, f32[16,64,512]{2,1,0:T(8,128)S(1)} %copy-done.4, f32[8,64,512]{2,1,0:T(8,128)S(1)} %collective-permute-done.lo0.lo7.low_ref, ...), custom_call_target="tpu_custom_call" | custom-call | bytes 1572864 | tf_op jit(solution)/shard_map/pack_y/pallas_call | solution.py:299
  124.1 2.9 %collective-permute-start.2 = (f32[24,8,512]{2,1,0:T(8,128)}, f32[24,8,512]{2,1,0:T(8,128)}, u32[]{:S(2)}, u32[]{:S(2)}) collective-permute-start(f32[24,8,512]{2,1,0:T(8,128)} %get-tuple-element.18), channel_id=1, source_target_pairs={{0,1},{1,2},{2,3},{4,5},{5,6},{6,7},{8,9},{9,10},{10,11},{12,13},{... | collective-permute-start | bytes 1179656 | tf_op jit(solution)/shard_map/ppermute | solution.py:525
  127.0 1.3 collective-permute-start.3
  128.2 2.8 %all-to-all-done.3.parts_ref = f32[32,16,128]{2,1,0:T(8,128)S(1)} async-done(((f32[32,16,128]{2,1,0:T(8,128)}), f32[32,16,128]{2,1,0:T(8,128)S(1)}, u32[]{:S(2)}, u32[]{:S(2)}) %all-to-all-start.3) | async-done | bytes 262176 | tf_op jit(solution)/shard_map/all_to_all | solution.py:518
  131.0 0.0 copy-done.10
  131.0 1.2 last.1
  132.2 4.4 %all-to-all-start.4 = ((f32[32,8,128]{2,1,0:T(8,128)}), f32[32,8,128]{2,1,0:T(8,128)S(1)}, u32[]{:S(2)}, u32[]{:S(2)}) async-start(f32[32,8,128]{2,1,0:T(8,128)} %get-tuple-element.15), calls=%async_computation.4 | async-start | bytes 262144 | tf_op jit(solution)/shard_map/all_to_all | solution.py:518
  136.7 0.1 stack.79
  136.9 0.1 stack.69.near_ref
  136.9 0.0 collective-permute-done.2.below_ref
  136.9 0.0 collective-permute-done.3.above_ref
  137.0 21.9 %heat.1 = (f32[16,64,512]{2,1,0:T(8,128)}, f32[24,8,128]{2,1,0:T(8,128)S(1)}) custom-call(f32[16,64,512]{2,1,0:T(8,128)S(1)} %copy-done.2, f32[16,64,512]{2,1,0:T(8,128)} %k_ref.1, f32[8,64,512]{2,1,0:T(8,128)S(1)} %collective-permute-done.lo0.lo7.low_ref, f32[8,64,512]{2,1,0:T(8,128)} %collective-permute-done.1.hi0.hi7.high_ref, ...), custom_call_target="tpu_custom_call" | custom-call | flops 88473600 | bytes 25165824 | tf_op jit(solution)/shard_map/heat/pallas_call | solution.py:405
  158.8 0.0 all-to-all-done.4.all_ref
  158.8 2.5 %add_source.1 = f32[16,64,512]{2,1,0:T(8,128)} custom-call(s32[9]{0:T(128)S(1)} %stack.69.near_ref, s32[9]{0:T(128)S(1)} %convert_element_type.3.flag_ref, f32[32,8,128]{2,1,0:T(8,128)S(1)} %all-to-all-done.4.all_ref, f32[24,8,128]{2,1,0:T(8,128)S(1)} %get-tuple-element.20.thin_ref, ...), custom_call_target="tpu_custom_call", output_to_operand_aliasing={{}: (4, {})} | custom-call | flops 1000000 | bytes 1048576 | tf_op jit(solution)/shard_map/add_source/pallas_call | solution.py:498
  (1 shorter events, 0.0 us)
Async XLA Ops:
  2.0 0.7 copy-start.5
  2.7 0.7 copy-start.9
  4.2 17.9 %all-to-all-start = ((f32[32,16,128]{2,1,0:T(8,128)}), f32[32,16,128]{2,1,0:T(8,128)S(1)}, u32[]{:S(2)}, u32[]{:S(2)}) async-start(f32[32,16,128]{2,1,0:T(8,128)} %get-tuple-element.12), calls=%async_computation | async-start | bytes 524288 | tf_op jit(solution)/shard_map/all_to_all | solution.py:518
  22.1 5.8 %copy-start = (f32[256,128,128]{2,1,0:T(8,128)S(1)}, f32[256,128,128]{2,1,0:T(8,128)}, u32[]{:S(2)}) copy-start(f32[256,128,128]{2,1,0:T(8,128)} %tiles_ref.3) | copy-start | bytes 50331652
  27.8 0.7 copy-start.7
  28.5 14.1 %copy-start.2 = (f32[16,64,512]{2,1,0:T(8,128)S(1)}, f32[16,64,512]{2,1,0:T(8,128)}, u32[]{:S(2)}) copy-start(f32[16,64,512]{2,1,0:T(8,128)} %t_ref.1) | copy-start | bytes 6291460
  32.1 21.0 %all-to-all-start.1 = ((f32[32,16,128]{2,1,0:T(8,128)}), f32[32,16,128]{2,1,0:T(8,128)S(1)}, u32[]{:S(2)}, u32[]{:S(2)}) async-start(f32[32,16,128]{2,1,0:T(8,128)} %bitcast.2), calls=%async_computation.1 | async-start | bytes 524288 | tf_op jit(solution)/shard_map/all_to_all | solution.py:518
  42.6 1.6 copy-start.3
  44.2 9.0 %copy-start.6 = (f32[16,128]{1,0:T(8,128)S(1)}, f32[16,128]{1,0:T(8,128)}, u32[]{:S(2)}) copy-start(f32[16,128]{1,0:T(8,128)} %mirror_ref.5) | copy-start | bytes 24580
  44.2 53.7 %copy-start.8 = (s32[256,2]{0,1:T(2,128)S(1)}, s32[256,2]{0,1:T(2,128)}, u32[]{:S(2)}) copy-start(s32[256,2]{0,1:T(2,128)} %param.11) | copy-start | bytes 6148
  45.6 74.8 %collective-permute-start = (f32[8,64,512]{2,1,0:T(8,128)}, f32[8,64,512]{2,1,0:T(8,128)S(1)}, u32[]{:S(2)}, u32[]{:S(2)}) collective-permute-start(f32[8,64,512]{2,1,0:T(8,128)} %get-tuple-element.16), channel_id=1, source_target_pairs={{0,4},{4,8},{8,12},{12,16},{16,20},{20,24},{24,28},{1,5},{5,9},{9,... | collective-permute-start | bytes 3145736 | tf_op jit(solution)/shard_map/ppermute | solution.py:525
  49.4 71.1 %collective-permute-start.1 = (f32[8,64,512]{2,1,0:T(8,128)}, f32[8,64,512]{2,1,0:T(8,128)}, u32[]{:S(2)}, u32[]{:S(2)}) collective-permute-start(f32[8,64,512]{2,1,0:T(8,128)} %get-tuple-element.17), channel_id=1, source_target_pairs={{4,0},{8,4},{12,8},{16,12},{20,16},{24,20},{28,24},{5,1},{9,5},{13... | collective-permute-start | bytes 3145736 | tf_op jit(solution)/shard_map/ppermute | solution.py:526
  97.9 5.8 %copy-start.1 = (f32[256,128,128]{2,1,0:T(8,128)S(1)}, f32[256,128,128]{2,1,0:T(8,128)}, u32[]{:S(2)}) copy-start(f32[256,128,128]{2,1,0:T(8,128)} %tiles_ref.3) | copy-start | bytes 50331652
  107.3 23.8 %copy-start.10 = (s32[16,128]{1,0:T(8,128)S(1)}, s32[16,128]{1,0:T(8,128)}, u32[]{:S(2)}) copy-start(s32[16,128]{1,0:T(8,128)} %site_ref.3) | copy-start | bytes 24580
  107.3 23.8 %all-to-all-start.3 = ((f32[32,16,128]{2,1,0:T(8,128)}), f32[32,16,128]{2,1,0:T(8,128)S(1)}, u32[]{:S(2)}, u32[]{:S(2)}) async-start(f32[32,16,128]{2,1,0:T(8,128)} %bitcast.4), calls=%async_computation.3 | async-start | bytes 524288 | tf_op jit(solution)/shard_map/all_to_all | solution.py:518
  120.5 1.6 copy-start.4
  124.1 12.9 %collective-permute-start.2 = (f32[24,8,512]{2,1,0:T(8,128)}, f32[24,8,512]{2,1,0:T(8,128)}, u32[]{:S(2)}, u32[]{:S(2)}) collective-permute-start(f32[24,8,512]{2,1,0:T(8,128)} %get-tuple-element.18), channel_id=1, source_target_pairs={{0,1},{1,2},{2,3},{4,5},{5,6},{6,7},{8,9},{9,10},{10,11},{12,13},{... | collective-permute-start | bytes 1179656 | tf_op jit(solution)/shard_map/ppermute | solution.py:525
  127.0 10.0 %collective-permute-start.3 = (f32[24,8,512]{2,1,0:T(8,128)}, f32[24,8,512]{2,1,0:T(8,128)}, u32[]{:S(2)}, u32[]{:S(2)}) collective-permute-start(f32[24,8,512]{2,1,0:T(8,128)} %get-tuple-element.19), channel_id=1, source_target_pairs={{1,0},{2,1},{3,2},{5,4},{6,5},{7,6},{9,8},{10,9},{11,10},{13,12},{... | collective-permute-start | bytes 1179656 | tf_op jit(solution)/shard_map/ppermute | solution.py:526
  132.2 26.6 %all-to-all-start.4 = ((f32[32,8,128]{2,1,0:T(8,128)}), f32[32,8,128]{2,1,0:T(8,128)S(1)}, u32[]{:S(2)}, u32[]{:S(2)}) async-start(f32[32,8,128]{2,1,0:T(8,128)} %get-tuple-element.15), calls=%async_computation.4 | async-start | bytes 262144 | tf_op jit(solution)/shard_map/all_to_all | solution.py:518

commit v3 on v2

--- a/solution.py
+++ b/solution.py
@@ -11,6 +11,8 @@
 SWEEPS = 2
 STEPS = 4
 HALO = STEPS
+DEPTH = STEPS // 2
+ROWS = STEPS
 LANES = 128
 CHUNK = 16
 
@@ -38,8 +40,18 @@
     return out
 
 
-def emit_kernel(plane_ref, site_ref, mirror_ref, emitted_ref, copies_ref):
-    sheets = plane_ref.shape[0]
+def emit_kernel(temp_ref, site_ref, mirror_ref, emitted_ref, copies_ref):
+    nx, ny, _ = temp_ref.shape
+    sheets = nx * ny // LANES
+    per = LANES // ny
+    lanes = lax.broadcasted_iota(jnp.int32, (LANES, LANES), 1)
+    gathered = jnp.zeros((LANES, LANES), jnp.float32)
+    for r in range(sheets):
+        piece = temp_ref[per * r : per * r + per].reshape(LANES, LANES)
+        if r:
+            piece = pltpu.roll(piece, r, 1)
+        gathered = jnp.where(lanes == r, piece, gathered)
+    plane = gathered.T[:sheets]
     for half in range(site_ref.shape[0] // 8):
         rows = pl.ds(half * 8, 8)
         site = site_ref[rows, :]
@@ -47,7 +59,7 @@
         sheet = site >> 7
         warmth = jnp.zeros(site.shape, jnp.float32)
         for r in range(sheets):
-            line = jnp.broadcast_to(plane_ref[r : r + 1, :], site.shape)
+            line = jnp.broadcast_to(plane[r : r + 1, :], site.shape)
             picked = jnp.take_along_axis(line, lane, axis=1)
             warmth = jnp.where(sheet == r, picked, warmth)
         square = warmth * warmth
@@ -57,18 +69,23 @@
             copies_ref[d, rows, :] = emitted
 
 
-def emit(plane, site, mirror, count):
+def emit(temp, site, mirror, count):
     shape = mirror.shape
+    nx, ny, _ = temp.shape
+    patch = pl.BlockSpec(shape, lambda i: (0, 0))
     return pl.pallas_call(
         emit_kernel,
+        grid=(1,),
         out_shape=(
             jax.ShapeDtypeStruct(shape, jnp.float32),
             jax.ShapeDtypeStruct((count,) + shape, jnp.float32),
         ),
-        compiler_params=params(8),
-        cost_estimate=cost(10_000, 400_000),
+        in_specs=[pl.BlockSpec((nx, ny, LANES), lambda i: (0, 0, 0)), patch, patch],
+        out_specs=(patch, pl.BlockSpec((count,) + shape, lambda i: (0, 0, 0))),
+        compiler_params=params(56),
+        cost_estimate=cost(10_000, 900_000),
         name="emit",
-    )(plane, site, mirror)
+    )(temp, site, mirror)
 
 
 def tiles_kernel(
@@ -167,7 +184,7 @@
             pltpu.VMEM((2, slots, BLK), jnp.float32),
             pltpu.SemaphoreType.DMA((slots // CHUNK,)),
         ],
-        compiler_params=params(36),
+        compiler_params=params(56),
         cost_estimate=cost(slots * BLK * BLK * 32, slots * BLK * BLK * 4),
         name="tiles",
     )(live, couples, couples, whole, tiles)
@@ -243,176 +260,395 @@
     )(parts, emitted, mirror, site)
 
 
-def pack_x_kernel(t_low, k_low, t_high, k_high, low_ref, high_ref):
-    low_ref[:HALO] = t_low[...]
-    low_ref[HALO:] = k_low[...]
-    high_ref[:HALO] = t_high[...]
-    high_ref[HALO:] = k_high[...]
+def first_planes(depth, ny, nz):
+    return pl.BlockSpec((depth, ny, nz), lambda i: (0, 0, 0))
+
+
+def pack_x_kernel(t_low, k_low, k_low_thin, t_high, k_high, k_high_thin, low_ref, high_ref):
+    ny, nz = t_low.shape[1:]
+    tail = 2 * DEPTH * ny
+    piece = ny * LANES // nz
+    for send, temp, cond, thin, at in (
+        (low_ref, t_low, k_low, k_low_thin, DEPTH),
+        (high_ref, t_high, k_high, k_high_thin, k_high_thin.shape[0] - DEPTH - 1),
+    ):
+        for p in range(DEPTH):
+            send[p * ny : p * ny + ny, :] = temp[p]
+            send[(DEPTH + p) * ny : (DEPTH + p + 1) * ny, :] = cond[p]
+        for j in range(nz // LANES):
+            send[tail:, j * LANES : (j + 1) * LANES] = thin[at, j * piece : (j + 1) * piece, :]
 
 
 def pack_x(temp, cond):
     nx, ny, nz = temp.shape
-    first = pl.BlockSpec((HALO, ny, nz), lambda i: (0, 0, 0))
-    final = pl.BlockSpec((HALO, ny, nz), lambda i: (nx // HALO - 1, 0, 0))
-    whole = pl.BlockSpec((2 * HALO, ny, nz), lambda i: (0, 0, 0))
-    shape = jax.ShapeDtypeStruct((2 * HALO, ny, nz), jnp.float32)
+    ends = 2 * DEPTH
+    rows = 2 * DEPTH * ny + ny * LANES // nz
+    first = pl.BlockSpec((DEPTH, ny, nz), lambda i: (0, 0, 0))
+    final = pl.BlockSpec((DEPTH, ny, nz), lambda i: (nx // DEPTH - 1, 0, 0))
+    first_thin = pl.BlockSpec((ends, ny, LANES), lambda i: (0, 0, 0))
+    final_thin = pl.BlockSpec((ends, ny, LANES), lambda i: (nx // ends - 1, 0, 0))
+    whole = pl.BlockSpec((rows, nz), lambda i: (0, 0))
+    shape = jax.ShapeDtypeStruct((rows, nz), jnp.float32)
     return pl.pallas_call(
         pack_x_kernel,
         grid=(1,),
         out_shape=(shape, shape),
-        in_specs=[first, first, final, final],
+        in_specs=[first, first, first_thin, final, final, final_thin],
         out_specs=(whole, whole),
-        compiler_params=params(20),
-        cost_estimate=cost(0, 4 * 2 * HALO * ny * nz * 4),
+        compiler_params=params(56),
+        cost_estimate=cost(0, 4 * rows * nz * 4),
         name="pack_x",
-    )(temp, cond, temp, cond)
-
-
-def pack_y_kernel(nx, t0, k0, t7, k7, lo0, hi0, lo7, hi7, down_ref, up_ref):
-    upper = lax.broadcasted_iota(jnp.int32, down_ref.shape[1:], 0) < HALO
+    )(temp, cond, cond, temp, cond, cond)
+
+
+def pack_y_kernel(nx, ny, t0, k0, t7, k7, low_ref, high_ref, down_ref, up_ref):
+    upper = lax.broadcasted_iota(jnp.int32, down_ref.shape[1:], 0) < ROWS
 
     def put(x, t_first, k_first, t_final, k_final):
-        down_ref[x] = jnp.where(upper, t_first, pltpu.roll(k_first, HALO, 0))
-        up_ref[x] = jnp.where(upper, pltpu.roll(t_final, HALO, 0), k_final)
-
-    for x in range(HALO):
-        put(x, lo0[x], lo0[HALO + x], lo7[x], lo7[HALO + x])
-        put(HALO + nx + x, hi0[x], hi0[HALO + x], hi7[x], hi7[HALO + x])
+        down_ref[x] = jnp.where(upper, t_first, pltpu.roll(k_first, ROWS, 0))
+        up_ref[x] = jnp.where(upper, pltpu.roll(t_final, ROWS, 0), k_final)
+
+    for side, base in ((low_ref, 0), (high_ref, DEPTH + nx)):
+        for p in range(DEPTH):
+            t_at, k_at = p * ny, (DEPTH + p) * ny
+            put(
+                base + p,
+                side[t_at : t_at + 8, :],
+                side[k_at : k_at + 8, :],
+                side[t_at + ny - 8 : t_at + ny, :],
+                side[k_at + ny - 8 : k_at + ny, :],
+            )
     for x in range(nx):
-        put(HALO + x, t0[x], k0[x], t7[x], k7[x])
+        put(DEPTH + x, t0[x], k0[x], t7[x], k7[x])
 
 
 def pack_y(temp, cond, low, high):
     nx, ny, nz = temp.shape
-
-    def edges(planes):
-        return (
-            pl.BlockSpec((planes, 8, nz), lambda i: (0, 0, 0)),
-            pl.BlockSpec((planes, 8, nz), lambda i: (0, ny // 8 - 1, 0)),
-        )
-
-    first, final = edges(nx)
-    halo_first, halo_final = edges(2 * HALO)
-    tall = nx + 2 * HALO
+    first = pl.BlockSpec((nx, 8, nz), lambda i: (0, 0, 0))
+    final = pl.BlockSpec((nx, 8, nz), lambda i: (0, ny // 8 - 1, 0))
+    halo = pl.BlockSpec(low.shape, lambda i: (0, 0))
+    tall = nx + 2 * DEPTH
     whole = pl.BlockSpec((tall, 8, nz), lambda i: (0, 0, 0))
     shape = jax.ShapeDtypeStruct((tall, 8, nz), jnp.float32)
     return pl.pallas_call(
-        functools.partial(pack_y_kernel, nx),
+        functools.partial(pack_y_kernel, nx, ny),
         grid=(1,),
         out_shape=(shape, shape),
-        in_specs=[first, first, final, final, halo_first, halo_first, halo_final, halo_final],
+        in_specs=[first, first, final, final, halo, halo],
         out_specs=(whole, whole),
-        compiler_params=params(20),
+        compiler_params=params(56),
         cost_estimate=cost(0, 4 * tall * 8 * nz * 4),
         name="pack_y",
-    )(temp, cond, temp, cond, low, high, low, high)
+    )(temp, cond, temp, cond, low, high)
 
 
 def coupling(a, b):
     return jnp.where(jnp.minimum(a, b) > 0.0, (0.5 * step_size) * (a + b), 0.0)
 
 
-def heat_kernel(
-    t_ref, k_ref, low_ref, high_ref, below_ref, above_ref, out_ref, thin_ref,
-    field, cond, centre, cx, cy, cz,
-):
-    nx, ny, nz = t_ref.shape
-    tall = nx + 2 * HALO
-    wide = ny + 2 * HALO
-    upper = lax.broadcasted_iota(jnp.int32, (8, nz), 0) < HALO
-
-    field[0, :HALO, :ny] = low_ref[:HALO]
-    field[0, HALO : HALO + nx, :ny] = t_ref[...]
-    field[0, HALO + nx :, :ny] = high_ref[:HALO]
-    cond[:HALO, :ny] = low_ref[HALO:]
-    cond[HALO : HALO + nx, :ny] = k_ref[...]
-    cond[HALO + nx :, :ny] = high_ref[HALO:]
+def neighbours():
+    slab, pair = lax.axis_index("slab"), lax.axis_index("pair")
+    return slab > 0, slab < lax.axis_size("slab") - 1, pair > 0, pair < lax.axis_size("pair") - 1
+
+
+def lane_tiles(nz):
+    return [slice(j * LANES, (j + 1) * LANES) for j in range(nz // LANES)]
+
+
+def prepare(cond, gx, gy, gz, gb):
+    tall, wide, nz = cond.shape
+    tiles = wide // 8
+    lane = lax.broadcasted_iota(jnp.int32, (8, LANES), 1)
+    half = 0.5 * step_size
 
     @pl.loop(0, tall)
     def _(x):
-        down = above_ref[x]
-        up = below_ref[x]
-        field[0, x, ny:] = jnp.where(upper, down, pltpu.roll(up, HALO, 0))
-        cond[x, ny:] = jnp.where(upper, pltpu.roll(down, HALO, 0), up)
-
-    depth = lax.broadcasted_iota(jnp.int32, (wide, nz), 1)
-
-    @pl.loop(0, tall)
+        after = jnp.minimum(x + 1, tall - 1)
+        for z in lane_tiles(nz):
+            last = z.stop == nz
+            for t in range(tiles):
+                rows = slice(8 * t, 8 * t + 8)
+                here = cond[x, rows, z]
+                gx[x, rows, z] = half * (here + cond[after, rows, z])
+                if t + 1 < tiles:
+                    beside = cond[x, 8 * t + 8 : 8 * t + 16, z]
+                else:
+                    beside = pltpu.roll(cond[x, :8, z], 7, 0)
+                gy[x, rows, z] = half * (here + beside)
+                turned = pltpu.roll(here, LANES - 1, 1)
+                if last:
+                    deeper = here
+                else:
+                    deeper = pltpu.roll(cond[x, rows, z.stop : z.stop + LANES], LANES - 1, 1)
+                gz[x, rows, z] = half * (here + jnp.where(lane < LANES - 1, turned, deeper))
+                if z.start == 0:
+                    gb[x, rows, :] = step_size * here
+
+
+def one_step(field, old, begin, end, store, gx, gy, gz, gb, carried):
+    wide, nz = field.shape[2:]
+    tiles = wide // 8
+    lane = lax.broadcasted_iota(jnp.int32, (8, LANES), 1)
+    sub = lax.broadcasted_iota(jnp.int32, (8, LANES), 0)
+    _, _, has_below, has_above = neighbours()
+    keep_above = (sub < 7) | has_above
+    keep_below = (sub < 7) | has_below
+
+    carried[...] = gx[begin - 1] * (field[old, begin] - field[old, begin - 1])
+
+    @pl.loop(begin, end)
     def _(x):
-        here = cond[x]
-        outer = here * 0.0
-        total = 6.0 * here
-        after = cond[jnp.minimum(x + 1, tall - 1)]
-        before = cond[jnp.maximum(x - 1, 0)]
-        cx[x] = coupling(here, after)
-        y_after = pltpu.roll(here, wide - 1, 0)
-        y_before = pltpu.roll(here, 1, 0)
-        cy[x] = coupling(here, y_after)
-        z_after = jnp.where(depth == nz - 1, outer, pltpu.roll(here, nz - 1, 1))
-        z_before = jnp.where(depth == 0, outer, pltpu.roll(here, 1, 1))
-        cz[x] = coupling(here, z_after)
-        for near in (after, before, y_after, y_before, z_after, z_before):
-            total = total + jnp.where(near > 0.0, near, here)
-        centre[x] = 1.0 - (0.5 * step_size) * total
-
-    def update(old, x):
-        here = field[old, x]
-        new = centre[x] * here
-        new = new + (cx[x] * field[old, x + 1] + cx[x - 1] * field[old, x - 1])
-        new = new + cy[x] * pltpu.roll(here, wide - 1, 0)
-        new = new + pltpu.roll(cy[x] * here, 1, 0)
-        new = new + cz[x] * pltpu.roll(here, nz - 1, 1)
-        return new + pltpu.roll(cz[x] * here, 1, 1)
-
-    @pl.loop(0, STEPS - 1)
-    def _(step):
-        old = step & 1
-
-        @pl.loop(1 + step, tall - 1 - step)
-        def _(x):
-            field[1 - old, x] = update(old, x)
-
-    @pl.loop(0, nx)
-    def _(x):
-        out_ref[x] = update((STEPS - 1) & 1, x + HALO)[:ny]
-
+        here, across_y = {}, {}
+        spans = lane_tiles(nz)
+        count = len(spans)
+
+        def tile(t, j):
+            if (t, j) not in here:
+                here[t, j] = field[old, x, 8 * t : 8 * t + 8, spans[j]]
+            return here[t, j]
+
+        def y_flux(t, j):
+            if (t, j) not in across_y:
+                if t + 1 < tiles:
+                    beside = tile(t + 1, j)
+                else:
+                    beside = pltpu.roll(tile(0, j), 7, 0)
+                across_y[t, j] = gy[x, 8 * t : 8 * t + 8, spans[j]] * (beside - tile(t, j))
+            return across_y[t, j]
+
+        for t in range(tiles):
+            rows = slice(8 * t, 8 * t + 8)
+            turned = [pltpu.roll(tile(t, j), LANES - 1, 1) for j in range(count)]
+            flux = []
+            for j in range(count):
+                deeper = turned[j + 1] if j + 1 < count else 0.0
+                deeper = jnp.where(lane < LANES - 1, turned[j], deeper)
+                flux.append(gz[x, rows, spans[j]] * (deeper - tile(t, j)))
+            back = [pltpu.roll(f, 1, 1) for f in flux]
+            for j in range(count):
+                now = tile(t, j)
+                low_z = back[j - 1] if j else gb[x, rows, :] * now
+                low_z = jnp.where(lane > 0, back[j], low_z)
+                x_flux = gx[x, rows, spans[j]] * (field[old, x + 1, rows, spans[j]] - now)
+                low_x = carried[rows, spans[j]]
+                carried[rows, spans[j]] = x_flux
+                low_y = y_flux(t - 1, j) if t else pltpu.roll(y_flux(tiles - 1, j), 1, 0)
+                new = now + (x_flux - low_x) + (y_flux(t, j) - low_y) + (flux[j] - low_z)
+                if t:
+                    new = jnp.where(keep_above if t <= ROWS else keep_below, new, 0.0)
+                store(x, t, spans[j], new)
+
+
+def thin_planes(cond, ny, thin_ref, base_plane):
+    tall, _, wide, _ = cond.shape
     lane = lax.broadcasted_iota(jnp.int32, (wide, LANES), 1)
     y_lane = lax.broadcasted_iota(jnp.int32, (8, LANES), 1)
     for base in range(0, tall, 16):
         planes = min(16, tall - base)
         gathered = jnp.zeros((wide, LANES), jnp.float32)
         for g in range(planes):
-            piece = cond[base + g, :, :LANES]
+            piece = cond[base + g, 0]
             if g:
                 piece = pltpu.roll(piece, 8 * g, 1)
             gathered = jnp.where((lane >> 3) == g, piece, gathered)
-        square = jnp.concatenate(
+        turned = jnp.concatenate(
             [gathered, jnp.zeros((LANES - wide, LANES), jnp.float32)], axis=0
-        )
-        turned = square.T
+        ).T
         for g in range(planes):
             rows = turned[8 * g : 8 * g + 8, :]
             moved = pltpu.roll(rows, LANES - wide, 1)
-            thin_ref[base + g] = jnp.where(
-                y_lane < ny + HALO, rows, jnp.where(y_lane >= LANES - HALO, moved, 0.0)
+            thin_ref[base_plane + base + g] = jnp.where(
+                y_lane < ny + ROWS, rows, jnp.where(y_lane >= LANES - ROWS, moved, 0.0)
             )
 
 
-def heat(temp, cond, low, high, below, above):
+def first_round_kernel(
+    t_ref, k_ref, low_ref, high_ref, below_ref, above_ref,
+    out_ref, low_out, high_out, cond_out, thin_ref,
+    loaded, field, gx, gy, gz, gb, carried, sems,
+):
+    nx, ny, nz = t_ref.shape
+    tall, wide = nx + 2 * DEPTH, ny + 2 * ROWS
+    tiles = wide // 8
+    raw_t, raw_k = loaded.at[0], loaded.at[1]
+    spans = lane_tiles(nz)
+    copies = [
+        pltpu.make_async_copy(
+            ref.at[:, :, pl.ds(z.start, LANES)],
+            loaded.at[which, pl.ds(DEPTH, nx), j, pl.ds(0, ny)],
+            sems.at[which, j],
+        )
+        for which, ref in ((1, k_ref), (0, t_ref))
+        for j, z in enumerate(spans)
+    ]
+    for copy in copies:
+        copy.start()
+    has_low, has_high, has_below, has_above = neighbours()
+    upper = lax.broadcasted_iota(jnp.int32, (8, LANES), 0) < ROWS
+    for side, base in ((low_ref, 0), (high_ref, DEPTH + nx)):
+        for p in range(DEPTH):
+            for j, z in enumerate(spans):
+                raw_t[base + p, j, :ny] = side[p * ny : p * ny + ny, z]
+                raw_k[base + p, j, :ny] = side[(DEPTH + p) * ny : (DEPTH + p + 1) * ny, z]
+
+    @pl.loop(0, tall)
+    def _(x):
+        for j, z in enumerate(spans):
+            down, up = above_ref[x, :, z], below_ref[x, :, z]
+            raw_t[x, j, ny:] = jnp.where(upper, down, pltpu.roll(up, ROWS, 0))
+            raw_k[x, j, ny:] = jnp.where(upper, pltpu.roll(down, ROWS, 0), up)
+
+    for copy in copies:
+        copy.wait()
+
+    piece = ny * LANES // nz
+    tail = 2 * DEPTH * ny
+    thin_planes(raw_k, ny, thin_ref, HALO - DEPTH)
+    for side, at in ((low_ref, HALO - DEPTH - 1), (high_ref, HALO + nx + DEPTH)):
+        edge = [side[tail:, z] for z in lane_tiles(nz)]
+        edge.append(jnp.zeros((LANES - ny, LANES), jnp.float32))
+        turned = jnp.concatenate(edge, axis=0).T
+        thin_ref[at] = turned[:8]
+    for at in [*range(HALO - DEPTH - 1), *range(HALO + nx + DEPTH + 1, nx + 2 * HALO)]:
+        thin_ref[at] = jnp.zeros((8, LANES), jnp.float32)
+
+    @pl.loop(0, tall)
+    def _(x):
+        missing = (upper & jnp.logical_not(has_above)) | (
+            jnp.logical_not(upper) & jnp.logical_not(has_below)
+        )
+        for j in range(len(spans)):
+            edge = raw_k[x, j, ny:]
+            last = jnp.broadcast_to(raw_k[x, j, ny - 1 : ny, :], edge.shape)
+            first = jnp.broadcast_to(raw_k[x, j, 0:1, :], edge.shape)
+            raw_k[x, j, ny:] = jnp.where(missing, jnp.where(upper, last, first), edge)
+
+    @pl.when(jnp.logical_not(has_low))
+    def _():
+        for p in range(DEPTH):
+            raw_k[p] = raw_k[DEPTH]
+
+    @pl.when(jnp.logical_not(has_high))
+    def _():
+        for p in range(DEPTH):
+            raw_k[DEPTH + nx + p] = raw_k[DEPTH + nx - 1]
+
+    @pl.loop(0, tall)
+    def _(x):
+        for t in range(tiles):
+            rows = pl.ds(t, 8, stride=tiles)
+            for j, z in enumerate(spans):
+                field[0, x, 8 * t : 8 * t + 8, z] = loaded[0, x, j, rows, :]
+                cond_out[x, 8 * t : 8 * t + 8, z] = loaded[1, x, j, rows, :]
+
+    prepare(cond_out, gx, gy, gz, gb)
+    two_steps(field, gx, gy, gz, gb, carried, lambda x, t, z, new: out_ref.__setitem__(
+        (x - DEPTH, slice(8 * t, 8 * t + 8), z), new))
+    low_out[...] = out_ref[:DEPTH]
+    high_out[...] = out_ref[nx - DEPTH :]
+
+
+def two_steps(field, gx, gy, gz, gb, carried, store):
+    tall = field.shape[1]
+    has_low, has_high, _, _ = neighbours()
+    for x in (1, tall - 2):
+        field[1, x] = jnp.zeros(field.shape[2:], jnp.float32)
+
+    def keep(x, t, z, new):
+        field[1, x, 8 * t : 8 * t + 8, z] = new
+
+    begin = jnp.where(has_low, 1, DEPTH)
+    end = jnp.where(has_high, tall - 1, tall - DEPTH)
+    one_step(field, 0, begin, end, keep, gx, gy, gz, gb, carried)
+    one_step(field, 1, DEPTH, tall - DEPTH, store, gx, gy, gz, gb, carried)
+
+
+def heat_scratch(tall, wide, nz):
+    big = pltpu.VMEM((tall, wide, nz), jnp.float32)
+    return [
+        pltpu.VMEM((2, tall, wide, nz), jnp.float32),
+        big,
+        big,
+        big,
+        pltpu.VMEM((tall, wide, LANES), jnp.float32),
+        pltpu.VMEM((wide, nz), jnp.float32),
+    ]
+
+
+def first_round(temp, cond, low, high, below, above):
     nx, ny, nz = temp.shape
-    tall, wide = nx + 2 * HALO, ny + 2 * HALO
-    big = pltpu.VMEM((tall, wide, nz), jnp.float32)
+    tall, wide = nx + 2 * DEPTH, ny + 2 * ROWS
+    hbm = pl.BlockSpec(memory_space=pl.ANY)
+    vmem = pl.BlockSpec(memory_space=pltpu.VMEM)
+    plane = jax.ShapeDtypeStruct((DEPTH, wide, nz), jnp.float32)
     return pl.pallas_call(
-        heat_kernel,
+        first_round_kernel,
         out_shape=(
-            jax.ShapeDtypeStruct(temp.shape, jnp.float32),
-            jax.ShapeDtypeStruct((tall, 8, LANES), jnp.float32),
+            jax.ShapeDtypeStruct((nx, wide, nz), jnp.float32),
+            plane,
+            plane,
+            jax.ShapeDtypeStruct((tall, wide, nz), jnp.float32),
+            jax.ShapeDtypeStruct((nx + 2 * HALO, 8, LANES), jnp.float32),
         ),
-        scratch_shapes=[pltpu.VMEM((2, tall, wide, nz), jnp.float32)] + [big] * 5,
-        compiler_params=params(48),
+        in_specs=[hbm, hbm] + [vmem] * 4,
+        scratch_shapes=[pltpu.VMEM((2, tall, nz // LANES, wide, LANES), jnp.float32)]
+        + heat_scratch(tall, wide, nz)
+        + [pltpu.SemaphoreType.DMA((2, nz // LANES))],
+        compiler_params=params(56),
         cost_estimate=cost(tall * wide * nz * 100, 12 * nx * ny * nz * 4),
-        name="heat",
+        name="first_round",
     )(temp, cond, low, high, below, above)
+
+
+def second_round_kernel(
+    t_ref, low_ref, high_ref, k_ref, out_ref,
+    cond, field, gx, gy, gz, gb, carried, placed, sems,
+):
+    nx, wide, nz = t_ref.shape
+    ny = out_ref.shape[1]
+    tiles = wide // 8
+    copies = [
+        pltpu.make_async_copy(k_ref, cond, sems.at[0]),
+        pltpu.make_async_copy(t_ref, field.at[0, pl.ds(DEPTH, nx)], sems.at[1]),
+        pltpu.make_async_copy(low_ref, field.at[0, pl.ds(0, DEPTH)], sems.at[2]),
+        pltpu.make_async_copy(high_ref, field.at[0, pl.ds(DEPTH + nx, DEPTH)], sems.at[3]),
+    ]
+    for copy in copies:
+        copy.start()
+    copies[0].wait()
+    prepare(cond, gx, gy, gz, gb)
+    for copy in copies[1:]:
+        copy.wait()
+
+    def store(x, t, z, new):
+        placed[x - DEPTH, z.start // LANES, pl.ds(t, 8, stride=tiles), :] = new
+
+    two_steps(field, gx, gy, gz, gb, carried, store)
+
+    @pl.loop(0, nx)
+    def _(x):
+        for j, z in enumerate(lane_tiles(out_ref.shape[2])):
+            out_ref[x, :, z] = placed[x, j, :ny, :]
+
+
+def second_round(temp, low, high, cond, shape):
+    nx, wide, nz = temp.shape
+    tall = cond.shape[0]
+    hbm = pl.BlockSpec(memory_space=pl.ANY)
+    return pl.pallas_call(
+        second_round_kernel,
+        out_shape=jax.ShapeDtypeStruct(shape, jnp.float32),
+        in_specs=[hbm] * 4,
+        scratch_shapes=[pltpu.VMEM((tall, wide, nz), jnp.float32)]
+        + heat_scratch(tall, wide, nz)
+        + [
+            pltpu.VMEM((nx, nz // LANES, wide, LANES), jnp.float32),
+            pltpu.SemaphoreType.DMA((4,)),
+        ],
+        compiler_params=params(56),
+        cost_estimate=cost(tall * wide * nz * 60, 8 * nx * wide * nz * 4),
+        name="second_round",
+    )(temp, low, high, cond)
 
 
 def source_kernel(ny, near_ref, flag_ref, all_ref, thin_ref, base_ref, out_ref):
@@ -540,25 +776,27 @@
     slabs, pairs = lax.axis_size("slab"), lax.axis_size("pair")
     count = slabs * pairs
     blocks = mirror_fraction.shape[0]
-    cells = nx * ny
-    plane = initial_warmth[:, :, 0].reshape(cells // LANES, LANES)
     couples = tile_block_couples.T
 
-    emitted, copies = emit(plane, element_facing_site, mirror_fraction, count)
+    emitted, copies = emit(initial_warmth, element_facing_site, mirror_fraction, count)
+    send_low, send_high = pack_x(initial_warmth, heat_passing_coefficient)
+    low, high = both_ways(send_low, send_high, "slab")
     for sweep in range(SWEEPS):
         whole = exchange(copies).reshape(count * blocks, BLK)
         term = tile_terms(whole, couples, active_slot_count, view_factor_blocks)
         parts = exchange(term.reshape(count, blocks, BLK))
         if sweep + 1 < SWEEPS:
             copies = middle(parts, emitted, mirror_fraction)
-    radiosity, source = last(parts, emitted, mirror_fraction, element_facing_site, cells)
+    radiosity, source = last(parts, emitted, mirror_fraction, element_facing_site, nx * ny)
     everything = exchange(source)
 
-    send_low, send_high = pack_x(initial_warmth, heat_passing_coefficient)
-    low, high = both_ways(send_low, send_high, "slab")
     send_down, send_up = pack_y(initial_warmth, heat_passing_coefficient, low, high)
     below, above = both_ways(send_down, send_up, "pair")
-    base, thin = heat(initial_warmth, heat_passing_coefficient, low, high, below, above)
+    temp, send_low, send_high, cond, thin = first_round(
+        initial_warmth, heat_passing_coefficient, low, high, below, above
+    )
+    low, high = both_ways(send_low, send_high, "slab")
+    base = second_round(temp, low, high, cond, initial_warmth.shape)
 
     slab, pair = lax.axis_index("slab"), lax.axis_index("pair")
     near, flag = [], []

time: 161 us -> 147 us (0.913)
  the two profiles are of different devices: /device:TPU:0 before, /device:TPU:21 now
where the time goes in v3:
time: 147 us; the launch traced here: 146 us
  Pallas kernels  52.8 us (36%)
  starting transfers between devices  44.2 us (30%)
  waiting for transfers between devices  24.6 us (17%)
  blocking collectives  17.9 us (12%)
  local copies, waits for them, and re-layouts  4.77 us (3%)
  between operations  1.53 us (1%)
    all_to_all x4, starting transfers between devices, exchange(): lax.all_to_all(copies, ('slab', 'pair'), split_axis=0, concat_axis=0, til...  27.8 us
    all_to_all x1, blocking collectives, exchange(): lax.all_to_all(copies, ('slab', 'pair'), split_axis=0, concat_axis=0, til...  17.9 us
    pallas_call x1, Pallas kernels, first_round(): pl.pallas_call(first_round_kernel, out_shape=(jax.ShapeDtypeStruct((nx, w...  16.5 us
    ppermute x3, waiting for transfers between devices, both_ways(): from_low = lax.ppermute(high, axis, forward)  14 us
    pallas_call x1, Pallas kernels, second_round(): pl.pallas_call(second_round_kernel, out_shape=jax.ShapeDtypeStruct(shape,...  12.7 us
    pallas_call x2, Pallas kernels, tile_terms(): pl.pallas_call(tiles_kernel, out_shape=jax.ShapeDtypeStruct(whole.shape,...  12.2 us
    ppermute x3, starting transfers between devices, both_ways(): from_low = lax.ppermute(high, axis, forward)  10.2 us
    all_to_all x4, waiting for transfers between devices, exchange(): lax.all_to_all(copies, ('slab', 'pair'), split_axis=0, concat_axis=0, til...  6.25 us
  transfers between devices with their start and end apart: 10, of which 5 were waited for; matrix products, arithmetic and copies ran while one was open for 0% of the time, Pallas kernels for 28%

profile of v3, /device:TPU:21, one launch (start us, length us, event | category | flops | bytes accessed | tf_op | source)
XLA Modules:
  0.0 145.8 jit_solution(12949494590121781415)
XLA Ops:
  0.6 2.1 %emit.1 = (f32[16,128]{1,0:T(8,128)}, f32[32,16,128]{2,1,0:T(8,128)}) custom-call(f32[16,64,512]{2,1,0:T(8,128)} %t_ref.1, s32[16,128]{1,0:T(8,128)} %site_ref.3, f32[16,128]{1,0:T(8,128)} %mirror_ref.5), custom_call_target="tpu_custom_call" | custom-call | flops 10000 | bytes 900000 | tf_op jit(solution)/shard_map/emit/pallas_call | solution.py:76
  2.8 6.2 %all-to-all-start = ((f32[32,16,128]{2,1,0:T(8,128)}), f32[32,16,128]{2,1,0:T(8,128)S(1)}, u32[]{:S(2)}, u32[]{:S(2)}) async-start(f32[32,16,128]{2,1,0:T(8,128)} %get-tuple-element.15), calls=%async_computation | async-start | bytes 524288 | tf_op jit(solution)/shard_map/all_to_all | solution.py:754
  9.6 6.2 %all-to-all-done = f32[32,16,128]{2,1,0:T(8,128)S(1)} async-done(((f32[32,16,128]{2,1,0:T(8,128)}), f32[32,16,128]{2,1,0:T(8,128)S(1)}, u32[]{:S(2)}, u32[]{:S(2)}) %all-to-all-start) | async-done | bytes 262176 | tf_op jit(solution)/shard_map/all_to_all | solution.py:754
  15.9 0.0 copy-start.7
  15.9 0.7 copy-done.7
  16.6 0.0 copy-start.1
  16.6 0.0 copy-start.3
  16.6 6.1 %tiles.2 = f32[512,128]{1,0:T(8,128)} custom-call(s32[1]{0:T(128)S(6)} %copy.11.live_ref, s32[2,256]{1,0:T(2,128)} %bitcast.27, s32[2,256]{1,0:T(2,128)} %bitcast.28, f32[512,128]{1,0:T(8,128)} %bitcast.25, f32[256,128,128]{2,1,0:T(8,128)} %tiles_ref.3), custom_call_target="tpu_custom_call" | custom-call | flops 134217728 | bytes 16777216 | tf_op jit(solution)/shard_map/tiles/pallas_call | solution.py:177
  22.7 17.9 %all_to_all.25.parts_ref = f32[32,16,128]{2,1,0:T(8,128)S(1)} all-to-all(f32[32,16,128]{2,1,0:T(8,128)} %bitcast.26), channel_id=1, replica_groups=mesh['slab'=8,'pair'=4] {'slab','pair'}, dimensions={0} | all-to-all | bytes 524288 | tf_op jit(solution)/shard_map/all_to_all | solution.py:754
  40.6 0.0 copy-done.1
  40.6 0.0 copy-done.3
  40.6 0.8 middle.1
  41.4 6.3 %all-to-all-start.2 = ((f32[32,16,128]{2,1,0:T(8,128)}), f32[32,16,128]{2,1,0:T(8,128)S(1)}, u32[]{:S(2)}, u32[]{:S(2)}) async-start(f32[32,16,128]{2,1,0:T(8,128)} %middle.1), calls=%async_computation.2 | async-start | bytes 524288 | tf_op jit(solution)/shard_map/all_to_all | solution.py:754
  47.7 2.3 %pack_x.1 = (f32[272,512]{1,0:T(8,128)}, f32[272,512]{1,0:T(8,128)}) custom-call(f32[16,64,512]{2,1,0:T(8,128)} %t_ref.1, f32[16,64,512]{2,1,0:T(8,128)} %k_ref.1, f32[16,64,512]{2,1,0:T(8,128)} %k_ref.1, f32[16,64,512]{2,1,0:T(8,128)} %t_ref.1, f32[16,64,512]{2,1,0:T(8,128)} %k_ref.1, f32[16,64,512]{2,1,0:T(8,128)} %k_ref.1), custom_call_target="tpu_custom_call" | custom-call | bytes 2228224 | tf_op jit(solution)/shard_map/pack_x/pallas_call | solution.py:292
  50.0 3.1 %collective-permute-start = (f32[272,512]{1,0:T(8,128)}, f32[272,512]{1,0:T(8,128)S(1)}, u32[]{:S(2)}, u32[]{:S(2)}) collective-permute-start(f32[272,512]{1,0:T(8,128)} %get-tuple-element.19), channel_id=1, source_target_pairs={{0,4},{4,8},{8,12},{12,16},{16,20},{20,24},{24,28},{1,5},{5,9},{9,... | collective-permute-start | bytes 1671176 | tf_op jit(solution)/shard_map/ppermute | solution.py:761
  53.1 2.2 %collective-permute-start.1 = (f32[272,512]{1,0:T(8,128)}, f32[272,512]{1,0:T(8,128)S(1)}, u32[]{:S(2)}, u32[]{:S(2)}) collective-permute-start(f32[272,512]{1,0:T(8,128)} %get-tuple-element.20), channel_id=1, source_target_pairs={{4,0},{8,4},{12,8},{16,12},{20,16},{24,20},{28,24},{5,1},{9,5},{13... | collective-permute-start | bytes 1671176 | tf_op jit(solution)/shard_map/ppermute | solution.py:762
  55.3 0.0 all-to-all-done.2
  55.3 0.0 copy-start.6
  55.3 0.7 copy-done.6
  56.0 6.1 %tiles.3 = f32[512,128]{1,0:T(8,128)} custom-call(s32[1]{0:T(128)S(6)} %copy.11.live_ref, s32[2,256]{1,0:T(2,128)} %bitcast.29, s32[2,256]{1,0:T(2,128)} %bitcast.30, f32[512,128]{1,0:T(8,128)} %bitcast.24, f32[256,128,128]{2,1,0:T(8,128)} %tiles_ref.3), custom_call_target="tpu_custom_call" | custom-call | flops 134217728 | bytes 16777216 | tf_op jit(solution)/shard_map/tiles/pallas_call | solution.py:177
  62.1 10.4 %all-to-all-start.3 = ((f32[32,16,128]{2,1,0:T(8,128)}), f32[32,16,128]{2,1,0:T(8,128)S(1)}, u32[]{:S(2)}, u32[]{:S(2)}) async-start(f32[32,16,128]{2,1,0:T(8,128)} %bitcast.23), calls=%async_computation.3 | async-start | bytes 524288 | tf_op jit(solution)/shard_map/all_to_all | solution.py:754
  72.5 8.2 %collective-permute-done.low_ref = f32[272,512]{1,0:T(8,128)S(1)} collective-permute-done((f32[272,512]{1,0:T(8,128)}, f32[272,512]{1,0:T(8,128)S(1)}, u32[]{:S(2)}, u32[]{:S(2)}) %collective-permute-start) | collective-permute-done | bytes 557088 | tf_op jit(solution)/shard_map/ppermute | solution.py:761
  80.7 0.0 copy-start.4
  80.7 0.0 collective-permute-done.1.high_ref
  80.7 0.8 copy-done.4
  81.5 0.0 copy-start.5
  81.5 0.8 copy-done.5
  82.3 2.5 %pack_y.1 = (f32[20,8,512]{2,1,0:T(8,128)}, f32[20,8,512]{2,1,0:T(8,128)}) custom-call(f32[16,64,512]{2,1,0:T(8,128)} %t_ref.1, f32[16,64,512]{2,1,0:T(8,128)} %k_ref.1, f32[16,64,512]{2,1,0:T(8,128)} %t_ref.1, f32[16,64,512]{2,1,0:T(8,128)} %k_ref.1, f32[272,512]{1,0:T(8,128)} %copy-done.4, f32[272,512]{1,0:T(8,128)} %copy-done.5), custom_call_target="tpu_custom_call" | custom-call | bytes 1310720 | tf_op jit(solution)/shard_map/pack_y/pallas_call | solution.py:333
  84.8 4.0 %collective-permute-start.2 = (f32[20,8,512]{2,1,0:T(8,128)}, f32[20,8,512]{2,1,0:T(8,128)S(1)}, u32[]{:S(2)}, u32[]{:S(2)}) collective-permute-start(f32[20,8,512]{2,1,0:T(8,128)} %get-tuple-element.21), channel_id=1, source_target_pairs={{0,1},{1,2},{2,3},{4,5},{5,6},{6,7},{8,9},{9,10},{10,11},{12,13},{... | collective-permute-start | bytes 983048 | tf_op jit(solution)/shard_map/ppermute | solution.py:761
  88.8 0.0 copy-start.2
  88.8 1.9 %collective-permute-start.3 = (f32[20,8,512]{2,1,0:T(8,128)}, f32[20,8,512]{2,1,0:T(8,128)S(1)}, u32[]{:S(2)}, u32[]{:S(2)}) collective-permute-start(f32[20,8,512]{2,1,0:T(8,128)} %get-tuple-element.22), channel_id=1, source_target_pairs={{1,0},{2,1},{3,2},{5,4},{6,5},{7,6},{9,8},{10,9},{11,10},{13,12},{... | collective-permute-start | bytes 983048 | tf_op jit(solution)/shard_map/ppermute | solution.py:762
  90.7 2.4 %collective-permute-done.2.below_ref = f32[20,8,512]{2,1,0:T(8,128)S(1)} collective-permute-done((f32[20,8,512]{2,1,0:T(8,128)}, f32[20,8,512]{2,1,0:T(8,128)S(1)}, u32[]{:S(2)}, u32[]{:S(2)}) %collective-permute-start.2) | collective-permute-done | bytes 327712 | tf_op jit(solution)/shard_map/ppermute | solution.py:761
  93.1 0.0 copy-start.8
  93.1 4.3 %collective-permute-done.3.above_ref = f32[20,8,512]{2,1,0:T(8,128)S(1)} collective-permute-done((f32[20,8,512]{2,1,0:T(8,128)}, f32[20,8,512]{2,1,0:T(8,128)S(1)}, u32[]{:S(2)}, u32[]{:S(2)}) %collective-permute-start.3) | collective-permute-done | bytes 327712 | tf_op jit(solution)/shard_map/ppermute | solution.py:762
  97.4 0.0 copy-done.8
  97.4 0.0 copy-start.9
  97.4 0.7 copy-done.9
  98.1 16.5 %first_round.1 = (f32[16,72,512]{2,1,0:T(8,128)}, f32[2,72,512]{2,1,0:T(8,128)}, f32[2,72,512]{2,1,0:T(8,128)}, f32[20,72,512]{2,1,0:T(8,128)}, f32[24,8,128]{2,1,0:T(8,128)}) custom-call(f32[16,64,512]{2,1,0:T(8,128)} %t_ref.1, f32[16,64,512]{2,1,0:T(8,128)} %k_ref.1, f32[272,512]{1,0:T(8,128)} %copy-done.4, f32[272,512]{1,0:T(8,128)} %copy-done.5, ...), custom_call_target="tpu_custom_call" | custom-call | flops 73728000 | bytes 25165824 | tf_op jit(solution)/shard_map/first_round/pallas_call | solution.py:584
  114.6 3.1 %collective-permute-start.4 = (f32[2,72,512]{2,1,0:T(8,128)}, f32[2,72,512]{2,1,0:T(8,128)S(1)}, u32[]{:S(2)}, u32[]{:S(2)}) collective-permute-start(f32[2,72,512]{2,1,0:T(8,128)} %get-tuple-element.25), channel_id=1, source_target_pairs={{0,4},{4,8},{8,12},{12,16},{16,20},{20,24},{24,28},{1,5},{5,9},{9,... | collective-permute-start | bytes 884744 | tf_op jit(solution)/shard_map/ppermute | solution.py:761
  117.8 2.2 %collective-permute-start.5 = (f32[2,72,512]{2,1,0:T(8,128)}, f32[2,72,512]{2,1,0:T(8,128)S(1)}, u32[]{:S(2)}, u32[]{:S(2)}) collective-permute-start(f32[2,72,512]{2,1,0:T(8,128)} %get-tuple-element.26), channel_id=1, source_target_pairs={{4,0},{8,4},{12,8},{16,12},{20,16},{24,20},{28,24},{5,1},{9,5},{13... | collective-permute-start | bytes 884744 | tf_op jit(solution)/shard_map/ppermute | solution.py:762
  119.9 0.0 all-to-all-done.3.parts_ref
  119.9 0.0 copy-done.2
  120.0 1.2 last.1
  121.2 4.9 %all-to-all-start.4 = ((f32[32,8,128]{2,1,0:T(8,128)}), f32[32,8,128]{2,1,0:T(8,128)S(1)}, u32[]{:S(2)}, u32[]{:S(2)}) async-start(f32[32,8,128]{2,1,0:T(8,128)} %get-tuple-element.18), calls=%async_computation.4 | async-start | bytes 262144 | tf_op jit(solution)/shard_map/all_to_all | solution.py:754
  126.1 0.1 stack.79
  126.2 0.1 stack.69.near_ref
  126.3 3.5 %collective-permute-done.4.low_ref = f32[2,72,512]{2,1,0:T(8,128)S(1)} collective-permute-done((f32[2,72,512]{2,1,0:T(8,128)}, f32[2,72,512]{2,1,0:T(8,128)S(1)}, u32[]{:S(2)}, u32[]{:S(2)}) %collective-permute-start.4) | collective-permute-done | bytes 294944 | tf_op jit(solution)/shard_map/ppermute | solution.py:761
  129.8 0.0 copy-start.10
  129.8 0.0 collective-permute-done.5.high_ref
  129.8 0.0 copy-start.11
  129.8 0.7 copy-done.10
  130.5 0.1 copy-done.11
  130.6 0.0 copy-start
  130.6 12.7 %second_round.1.base_ref = f32[16,64,512]{2,1,0:T(8,128)} custom-call(f32[16,72,512]{2,1,0:T(8,128)} %get-tuple-element.24.t_ref, f32[2,72,512]{2,1,0:T(8,128)} %copy-done.10, f32[2,72,512]{2,1,0:T(8,128)} %copy-done.11, f32[20,72,512]{2,1,0:T(8,128)} %get-tuple-element.27.k_ref), custom_call_target="tpu_custom_call" | custom-call | flops 44236800 | bytes 18874368 | tf_op jit(solution)/shard_map/second_round/pallas_call | solution.py:638
  143.3 0.0 all-to-all-done.4.all_ref
  143.3 0.0 copy-done
  143.3 2.5 %add_source.1 = f32[16,64,512]{2,1,0:T(8,128)} custom-call(s32[9]{0:T(128)S(1)} %stack.69.near_ref, s32[9]{0:T(128)S(1)} %convert_element_type.3.flag_ref, f32[32,8,128]{2,1,0:T(8,128)S(1)} %all-to-all-done.4.all_ref, f32[24,8,128]{2,1,0:T(8,128)S(1)} %copy-done, f32[16,64,512]{2,1,0:T(8,128)} %second_round.1.base_ref), custom_call_target="tpu_custom_call", output_to_operand_aliasing={{}: (4, {})} | custom-call | flops 1000000 | bytes 1048576 | tf_op jit(solution)/shard_map/add_source/pallas_call | solution.py:734
  (1 shorter events, 0.0 us)
Async XLA Ops:
  2.8 13.1 %all-to-all-start = ((f32[32,16,128]{2,1,0:T(8,128)}), f32[32,16,128]{2,1,0:T(8,128)S(1)}, u32[]{:S(2)}, u32[]{:S(2)}) async-start(f32[32,16,128]{2,1,0:T(8,128)} %get-tuple-element.15), calls=%async_computation | async-start | bytes 524288 | tf_op jit(solution)/shard_map/all_to_all | solution.py:754
  15.9 0.7 copy-start.7
  16.6 24.0 %copy-start.1 = (f32[16,128]{1,0:T(8,128)S(1)}, f32[16,128]{1,0:T(8,128)}, u32[]{:S(2)}) copy-start(f32[16,128]{1,0:T(8,128)} %mirror_ref.5) | copy-start | bytes 24580
  16.6 24.0 %copy-start.3 = (f32[16,128]{1,0:T(8,128)S(1)}, f32[16,128]{1,0:T(8,128)}, u32[]{:S(2)}) copy-start(f32[16,128]{1,0:T(8,128)} %get-tuple-element.16.emitted_ref) | copy-start | bytes 24580
  41.4 13.9 %all-to-all-start.2 = ((f32[32,16,128]{2,1,0:T(8,128)}), f32[32,16,128]{2,1,0:T(8,128)S(1)}, u32[]{:S(2)}, u32[]{:S(2)}) async-start(f32[32,16,128]{2,1,0:T(8,128)} %middle.1), calls=%async_computation.2 | async-start | bytes 524288 | tf_op jit(solution)/shard_map/all_to_all | solution.py:754
  50.0 30.7 %collective-permute-start = (f32[272,512]{1,0:T(8,128)}, f32[272,512]{1,0:T(8,128)S(1)}, u32[]{:S(2)}, u32[]{:S(2)}) collective-permute-start(f32[272,512]{1,0:T(8,128)} %get-tuple-element.19), channel_id=1, source_target_pairs={{0,4},{4,8},{8,12},{12,16},{16,20},{20,24},{24,28},{1,5},{5,9},{9,... | collective-permute-start | bytes 1671176 | tf_op jit(solution)/shard_map/ppermute | solution.py:761
  53.1 27.6 %collective-permute-start.1 = (f32[272,512]{1,0:T(8,128)}, f32[272,512]{1,0:T(8,128)S(1)}, u32[]{:S(2)}, u32[]{:S(2)}) collective-permute-start(f32[272,512]{1,0:T(8,128)} %get-tuple-element.20), channel_id=1, source_target_pairs={{4,0},{8,4},{12,8},{16,12},{20,16},{24,20},{28,24},{5,1},{9,5},{13... | collective-permute-start | bytes 1671176 | tf_op jit(solution)/shard_map/ppermute | solution.py:762
  55.3 0.7 copy-start.6
  62.1 57.9 %all-to-all-start.3 = ((f32[32,16,128]{2,1,0:T(8,128)}), f32[32,16,128]{2,1,0:T(8,128)S(1)}, u32[]{:S(2)}, u32[]{:S(2)}) async-start(f32[32,16,128]{2,1,0:T(8,128)} %bitcast.23), calls=%async_computation.3 | async-start | bytes 524288 | tf_op jit(solution)/shard_map/all_to_all | solution.py:754
  80.7 0.8 copy-start.4
  81.5 0.8 copy-start.5
  84.8 8.3 %collective-permute-start.2 = (f32[20,8,512]{2,1,0:T(8,128)}, f32[20,8,512]{2,1,0:T(8,128)S(1)}, u32[]{:S(2)}, u32[]{:S(2)}) collective-permute-start(f32[20,8,512]{2,1,0:T(8,128)} %get-tuple-element.21), channel_id=1, source_target_pairs={{0,1},{1,2},{2,3},{4,5},{5,6},{6,7},{8,9},{9,10},{10,11},{12,13},{... | collective-permute-start | bytes 983048 | tf_op jit(solution)/shard_map/ppermute | solution.py:761
  88.8 31.2 %copy-start.2 = (s32[16,128]{1,0:T(8,128)S(1)}, s32[16,128]{1,0:T(8,128)}, u32[]{:S(2)}) copy-start(s32[16,128]{1,0:T(8,128)} %site_ref.3) | copy-start | bytes 24580
  88.8 8.6 %collective-permute-start.3 = (f32[20,8,512]{2,1,0:T(8,128)}, f32[20,8,512]{2,1,0:T(8,128)S(1)}, u32[]{:S(2)}, u32[]{:S(2)}) collective-permute-start(f32[20,8,512]{2,1,0:T(8,128)} %get-tuple-element.22), channel_id=1, source_target_pairs={{1,0},{2,1},{3,2},{5,4},{6,5},{7,6},{9,8},{10,9},{11,10},{13,12},{... | collective-permute-start | bytes 983048 | tf_op jit(solution)/shard_map/ppermute | solution.py:762
  93.1 4.3 %copy-start.8 = (f32[20,8,512]{2,1,0:T(8,128)}, f32[20,8,512]{2,1,0:T(8,128)S(1)}, u32[]{:S(2)}) copy-start(f32[20,8,512]{2,1,0:T(8,128)S(1)} %collective-permute-done.2.below_ref) | copy-start | bytes 983044
  97.4 0.7 copy-start.9
  114.6 15.1 %collective-permute-start.4 = (f32[2,72,512]{2,1,0:T(8,128)}, f32[2,72,512]{2,1,0:T(8,128)S(1)}, u32[]{:S(2)}, u32[]{:S(2)}) collective-permute-start(f32[2,72,512]{2,1,0:T(8,128)} %get-tuple-element.25), channel_id=1, source_target_pairs={{0,4},{4,8},{8,12},{12,16},{16,20},{20,24},{24,28},{1,5},{5,9},{9,... | collective-permute-start | bytes 884744 | tf_op jit(solution)/shard_map/ppermute | solution.py:761
  117.8 12.0 %collective-permute-start.5 = (f32[2,72,512]{2,1,0:T(8,128)}, f32[2,72,512]{2,1,0:T(8,128)S(1)}, u32[]{:S(2)}, u32[]{:S(2)}) collective-permute-start(f32[2,72,512]{2,1,0:T(8,128)} %get-tuple-element.26), channel_id=1, source_target_pairs={{4,0},{8,4},{12,8},{16,12},{20,16},{24,20},{28,24},{5,1},{9,5},{13... | collective-permute-start | bytes 884744 | tf_op jit(solution)/shard_map/ppermute | solution.py:762
  121.2 22.1 %all-to-all-start.4 = ((f32[32,8,128]{2,1,0:T(8,128)}), f32[32,8,128]{2,1,0:T(8,128)S(1)}, u32[]{:S(2)}, u32[]{:S(2)}) async-start(f32[32,8,128]{2,1,0:T(8,128)} %get-tuple-element.18), calls=%async_computation.4 | async-start | bytes 262144 | tf_op jit(solution)/shard_map/all_to_all | solution.py:754
  129.8 0.7 copy-start.10
  129.8 0.8 copy-start.11
  130.6 12.7 %copy-start = (f32[24,8,128]{2,1,0:T(8,128)S(1)}, f32[24,8,128]{2,1,0:T(8,128)}, u32[]{:S(2)}) copy-start(f32[24,8,128]{2,1,0:T(8,128)} %get-tuple-element.23.thin_ref) | copy-start | bytes 294916

commit v4 on v3

--- a/solution.py
+++ b/solution.py
@@ -82,7 +82,7 @@
         ),
         in_specs=[pl.BlockSpec((nx, ny, LANES), lambda i: (0, 0, 0)), patch, patch],
         out_specs=(patch, pl.BlockSpec((count,) + shape, lambda i: (0, 0, 0))),
-        compiler_params=params(56),
+        compiler_params=params(64),
         cost_estimate=cost(10_000, 900_000),
         name="emit",
     )(temp, site, mirror)
@@ -184,7 +184,7 @@
             pltpu.VMEM((2, slots, BLK), jnp.float32),
             pltpu.SemaphoreType.DMA((slots // CHUNK,)),
         ],
-        compiler_params=params(56),
+        compiler_params=params(64),
         cost_estimate=cost(slots * BLK * BLK * 32, slots * BLK * BLK * 4),
         name="tiles",
     )(live, couples, couples, whole, tiles)
@@ -210,7 +210,7 @@
     return pl.pallas_call(
         middle_kernel,
         out_shape=jax.ShapeDtypeStruct(parts.shape, jnp.float32),
-        compiler_params=params(8),
+        compiler_params=params(64),
         cost_estimate=cost(100_000, 600_000),
         name="middle",
     )(parts, emitted, mirror)
@@ -254,7 +254,7 @@
             jax.ShapeDtypeStruct(mirror.shape, jnp.float32),
             jax.ShapeDtypeStruct((count, cells // LANES, LANES), jnp.float32),
         ),
-        compiler_params=params(16),
+        compiler_params=params(64),
         cost_estimate=cost(10_000_000, 600_000),
         name="last",
     )(parts, emitted, mirror, site)
@@ -295,7 +295,7 @@
         out_shape=(shape, shape),
         in_specs=[first, first, first_thin, final, final, final_thin],
         out_specs=(whole, whole),
-        compiler_params=params(56),
+        compiler_params=params(64),
         cost_estimate=cost(0, 4 * rows * nz * 4),
         name="pack_x",
     )(temp, cond, cond, temp, cond, cond)
@@ -336,7 +336,7 @@
         out_shape=(shape, shape),
         in_specs=[first, first, final, final, halo, halo],
         out_specs=(whole, whole),
-        compiler_params=params(56),
+        compiler_params=params(64),
         cost_estimate=cost(0, 4 * tall * 8 * nz * 4),
         name="pack_y",
     )(temp, cond, temp, cond, low, high)
@@ -353,6 +353,26 @@
 
 def lane_tiles(nz):
     return [slice(j * LANES, (j + 1) * LANES) for j in range(nz // LANES)]
+
+
+class Lagging:
+    def __init__(self, depth):
+        self.depth = depth
+        self.waiting = []
+
+    def add(self, store):
+        self.waiting.append(store)
+        if len(self.waiting) > self.depth:
+            self.waiting.pop(0)()
+
+    def finish(self):
+        for store in self.waiting:
+            store()
+        self.waiting = []
+
+
+def put(ref, index, value):
+    return lambda: ref.__setitem__(index, value)
 
 
 def prepare(cond, gx, gy, gz, gb):
@@ -364,29 +384,32 @@
     @pl.loop(0, tall)
     def _(x):
         after = jnp.minimum(x + 1, tall - 1)
+        stores = Lagging(16)
         for z in lane_tiles(nz):
             last = z.stop == nz
             for t in range(tiles):
                 rows = slice(8 * t, 8 * t + 8)
                 here = cond[x, rows, z]
-                gx[x, rows, z] = half * (here + cond[after, rows, z])
+                stores.add(put(gx, (x, rows, z), half * (here + cond[after, rows, z])))
                 if t + 1 < tiles:
                     beside = cond[x, 8 * t + 8 : 8 * t + 16, z]
                 else:
                     beside = pltpu.roll(cond[x, :8, z], 7, 0)
-                gy[x, rows, z] = half * (here + beside)
+                stores.add(put(gy, (x, rows, z), half * (here + beside)))
                 turned = pltpu.roll(here, LANES - 1, 1)
                 if last:
                     deeper = here
                 else:
                     deeper = pltpu.roll(cond[x, rows, z.stop : z.stop + LANES], LANES - 1, 1)
-                gz[x, rows, z] = half * (here + jnp.where(lane < LANES - 1, turned, deeper))
+                deeper = jnp.where(lane < LANES - 1, turned, deeper)
+                stores.add(put(gz, (x, rows, z), half * (here + deeper)))
                 if z.start == 0:
-                    gb[x, rows, :] = step_size * here
-
-
-def one_step(field, old, begin, end, store, gx, gy, gz, gb, carried):
-    wide, nz = field.shape[2:]
+                    stores.add(put(gb, (x, rows), step_size * here))
+        stores.finish()
+
+
+def one_step(field, begin, end, target, gx, gy, gz, gb, carried):
+    wide, nz = field.shape[1:]
     tiles = wide // 8
     lane = lax.broadcasted_iota(jnp.int32, (8, LANES), 1)
     sub = lax.broadcasted_iota(jnp.int32, (8, LANES), 0)
@@ -394,17 +417,18 @@
     keep_above = (sub < 7) | has_above
     keep_below = (sub < 7) | has_below
 
-    carried[...] = gx[begin - 1] * (field[old, begin] - field[old, begin - 1])
+    carried[...] = gx[begin - 1] * (field[begin] - field[begin - 1])
 
     @pl.loop(begin, end)
     def _(x):
         here, across_y = {}, {}
+        stores = Lagging(16)
         spans = lane_tiles(nz)
         count = len(spans)
 
         def tile(t, j):
             if (t, j) not in here:
-                here[t, j] = field[old, x, 8 * t : 8 * t + 8, spans[j]]
+                here[t, j] = field[x, 8 * t : 8 * t + 8, spans[j]]
             return here[t, j]
 
         def y_flux(t, j):
@@ -429,14 +453,15 @@
                 now = tile(t, j)
                 low_z = back[j - 1] if j else gb[x, rows, :] * now
                 low_z = jnp.where(lane > 0, back[j], low_z)
-                x_flux = gx[x, rows, spans[j]] * (field[old, x + 1, rows, spans[j]] - now)
+                x_flux = gx[x, rows, spans[j]] * (field[x + 1, rows, spans[j]] - now)
                 low_x = carried[rows, spans[j]]
-                carried[rows, spans[j]] = x_flux
+                stores.add(put(carried, (rows, spans[j]), x_flux))
                 low_y = y_flux(t - 1, j) if t else pltpu.roll(y_flux(tiles - 1, j), 1, 0)
                 new = now + (x_flux - low_x) + (y_flux(t, j) - low_y) + (flux[j] - low_z)
                 if t:
                     new = jnp.where(keep_above if t <= ROWS else keep_below, new, 0.0)
-                store(x, t, spans[j], new)
+                stores.add(put(*target(x, t, spans[j]), new))
+        stores.finish()
 
 
 def thin_planes(cond, ny, thin_ref, base_plane):
@@ -465,7 +490,7 @@
 def first_round_kernel(
     t_ref, k_ref, low_ref, high_ref, below_ref, above_ref,
     out_ref, low_out, high_out, cond_out, thin_ref,
-    loaded, field, gx, gy, gz, gb, carried, sems,
+    loaded, field, between, gx, gy, gz, gb, carried, sems,
 ):
     nx, ny, nz = t_ref.shape
     tall, wide = nx + 2 * DEPTH, ny + 2 * ROWS
@@ -535,38 +560,44 @@
 
     @pl.loop(0, tall)
     def _(x):
+        stores = Lagging(16)
         for t in range(tiles):
             rows = pl.ds(t, 8, stride=tiles)
             for j, z in enumerate(spans):
-                field[0, x, 8 * t : 8 * t + 8, z] = loaded[0, x, j, rows, :]
-                cond_out[x, 8 * t : 8 * t + 8, z] = loaded[1, x, j, rows, :]
+                stores.add(put(field, (x, slice(8 * t, 8 * t + 8), z), loaded[0, x, j, rows, :]))
+                stores.add(put(cond_out, (x, slice(8 * t, 8 * t + 8), z), loaded[1, x, j, rows, :]))
+        stores.finish()
 
     prepare(cond_out, gx, gy, gz, gb)
-    two_steps(field, gx, gy, gz, gb, carried, lambda x, t, z, new: out_ref.__setitem__(
-        (x - DEPTH, slice(8 * t, 8 * t + 8), z), new))
+
+    def target(x, t, z):
+        return out_ref, (x - DEPTH, slice(8 * t, 8 * t + 8), z)
+
+    two_steps(field, between, gx, gy, gz, gb, carried, target)
     low_out[...] = out_ref[:DEPTH]
     high_out[...] = out_ref[nx - DEPTH :]
 
 
-def two_steps(field, gx, gy, gz, gb, carried, store):
-    tall = field.shape[1]
+def two_steps(field, between, gx, gy, gz, gb, carried, target):
+    tall = field.shape[0]
     has_low, has_high, _, _ = neighbours()
     for x in (1, tall - 2):
-        field[1, x] = jnp.zeros(field.shape[2:], jnp.float32)
-
-    def keep(x, t, z, new):
-        field[1, x, 8 * t : 8 * t + 8, z] = new
+        between[x] = jnp.zeros(field.shape[1:], jnp.float32)
+
+    def inner(x, t, z):
+        return between, (x, slice(8 * t, 8 * t + 8), z)
 
     begin = jnp.where(has_low, 1, DEPTH)
     end = jnp.where(has_high, tall - 1, tall - DEPTH)
-    one_step(field, 0, begin, end, keep, gx, gy, gz, gb, carried)
-    one_step(field, 1, DEPTH, tall - DEPTH, store, gx, gy, gz, gb, carried)
+    one_step(field, begin, end, inner, gx, gy, gz, gb, carried)
+    one_step(between, DEPTH, tall - DEPTH, target, gx, gy, gz, gb, carried)
 
 
 def heat_scratch(tall, wide, nz):
     big = pltpu.VMEM((tall, wide, nz), jnp.float32)
     return [
-        pltpu.VMEM((2, tall, wide, nz), jnp.float32),
+        big,
+        big,
         big,
         big,
         big,
@@ -594,7 +625,7 @@
         scratch_shapes=[pltpu.VMEM((2, tall, nz // LANES, wide, LANES), jnp.float32)]
         + heat_scratch(tall, wide, nz)
         + [pltpu.SemaphoreType.DMA((2, nz // LANES))],
-        compiler_params=params(56),
+        compiler_params=params(64),
         cost_estimate=cost(tall * wide * nz * 100, 12 * nx * ny * nz * 4),
         name="first_round",
     )(temp, cond, low, high, below, above)
@@ -602,16 +633,16 @@
 
 def second_round_kernel(
     t_ref, low_ref, high_ref, k_ref, out_ref,
-    cond, field, gx, gy, gz, gb, carried, placed, sems,
+    cond, field, between, gx, gy, gz, gb, carried, placed, sems,
 ):
     nx, wide, nz = t_ref.shape
     ny = out_ref.shape[1]
     tiles = wide // 8
     copies = [
         pltpu.make_async_copy(k_ref, cond, sems.at[0]),
-        pltpu.make_async_copy(t_ref, field.at[0, pl.ds(DEPTH, nx)], sems.at[1]),
-        pltpu.make_async_copy(low_ref, field.at[0, pl.ds(0, DEPTH)], sems.at[2]),
-        pltpu.make_async_copy(high_ref, field.at[0, pl.ds(DEPTH + nx, DEPTH)], sems.at[3]),
+        pltpu.make_async_copy(t_ref, field.at[pl.ds(DEPTH, nx)], sems.at[1]),
+        pltpu.make_async_copy(low_ref, field.at[pl.ds(0, DEPTH)], sems.at[2]),
+        pltpu.make_async_copy(high_ref, field.at[pl.ds(DEPTH + nx, DEPTH)], sems.at[3]),
     ]
     for copy in copies:
         copy.start()
@@ -620,10 +651,10 @@
     for copy in copies[1:]:
         copy.wait()
 
-    def store(x, t, z, new):
-        placed[x - DEPTH, z.start // LANES, pl.ds(t, 8, stride=tiles), :] = new
-
-    two_steps(field, gx, gy, gz, gb, carried, store)
+    def target(x, t, z):
+        return placed, (x - DEPTH, z.start // LANES, pl.ds(t, 8, stride=tiles))
+
+    two_steps(field, between, gx, gy, gz, gb, carried, target)
 
     @pl.loop(0, nx)
     def _(x):
@@ -645,7 +676,7 @@
             pltpu.VMEM((nx, nz // LANES, wide, LANES), jnp.float32),
             pltpu.SemaphoreType.DMA((4,)),
         ],
-        compiler_params=params(56),
+        compiler_params=params(64),
         cost_estimate=cost(tall * wide * nz * 60, 8 * nx * wide * nz * 4),
         name="second_round",
     )(temp, low, high, cond)
@@ -744,7 +775,7 @@
         ],
         out_specs=block,
         input_output_aliases={4: 0},
-        compiler_params=params(16),
+        compiler_params=params(64),
         cost_estimate=cost(1_000_000, 2 * nx * ny * LANES * 4),
         name="add_source",
     )(near, flag, everything, thin, base)
@@ -752,6 +783,10 @@
 
 def exchange(copies):
     return lax.all_to_all(copies, ("slab", "pair"), split_axis=0, concat_axis=0, tiled=True)
+
+
+def together(*arrays):
+    return lax.optimization_barrier(arrays)
 
 
 def both_ways(low, high, axis):
@@ -778,25 +813,34 @@
     blocks = mirror_fraction.shape[0]
     couples = tile_block_couples.T
 
-    emitted, copies = emit(initial_warmth, element_facing_site, mirror_fraction, count)
-    send_low, send_high = pack_x(initial_warmth, heat_passing_coefficient)
+    temp, cond = initial_warmth, heat_passing_coefficient
+    emitted, copies = emit(temp, element_facing_site, mirror_fraction, count)
+    temp, copies = together(temp, copies)
+
+    def sweep_terms(whole):
+        whole = whole.reshape(count * blocks, BLK)
+        term = tile_terms(whole, couples, active_slot_count, view_factor_blocks)
+        return term.reshape(count, blocks, BLK)
+
+    whole = exchange(copies)
+    send_low, send_high = pack_x(temp, cond)
+    whole, send_low, send_high = together(whole, send_low, send_high)
     low, high = both_ways(send_low, send_high, "slab")
-    for sweep in range(SWEEPS):
-        whole = exchange(copies).reshape(count * blocks, BLK)
-        term = tile_terms(whole, couples, active_slot_count, view_factor_blocks)
-        parts = exchange(term.reshape(count, blocks, BLK))
-        if sweep + 1 < SWEEPS:
-            copies = middle(parts, emitted, mirror_fraction)
+    parts = exchange(sweep_terms(whole))
+    send_down, send_up = pack_y(temp, cond, low, high)
+    parts, send_down, send_up = together(parts, send_down, send_up)
+    below, above = both_ways(send_down, send_up, "pair")
+    whole = exchange(middle(parts, emitted, mirror_fraction))
+    middle_temp, send_low, send_high, strided_cond, thin = first_round(
+        temp, cond, low, high, below, above
+    )
+    whole, send_low, send_high = together(whole, send_low, send_high)
+    low, high = both_ways(send_low, send_high, "slab")
+    parts = exchange(sweep_terms(whole))
+    parts, low, high = together(parts, low, high)
     radiosity, source = last(parts, emitted, mirror_fraction, element_facing_site, nx * ny)
     everything = exchange(source)
-
-    send_down, send_up = pack_y(initial_warmth, heat_passing_coefficient, low, high)
-    below, above = both_ways(send_down, send_up, "pair")
-    temp, send_low, send_high, cond, thin = first_round(
-        initial_warmth, heat_passing_coefficient, low, high, below, above
-    )
-    low, high = both_ways(send_low, send_high, "slab")
-    base = second_round(temp, low, high, cond, initial_warmth.shape)
+    base = second_round(middle_temp, low, high, strided_cond, temp.shape)
 
     slab, pair = lax.axis_index("slab"), lax.axis_index("pair")
     near, flag = [], []

time: 147 us -> 144 us (0.980)
  the two profiles are of different devices: /device:TPU:21 before, /device:TPU:0 now
where the time goes in v4:
time: 144 us; the launch traced here: 143 us
  Pallas kernels  55.4 us (38%)
  starting transfers between devices  52.8 us (37%)
  waiting for transfers between devices  31.7 us (22%)
  between operations  1.47 us (1%)
    all_to_all x5, starting transfers between devices, exchange(): lax.all_to_all(copies, ('slab', 'pair'), split_axis=0, concat_axis=0, til...  38.2 us
    ppermute x3, waiting for transfers between devices, both_ways(): from_low = lax.ppermute(high, axis, forward)  20 us
    pallas_call x1, Pallas kernels, first_round(): pl.pallas_call(first_round_kernel, out_shape=(jax.ShapeDtypeStruct((nx, w...  16.3 us
    pallas_call x2, Pallas kernels, tile_terms(): pl.pallas_call(tiles_kernel, out_shape=jax.ShapeDtypeStruct(whole.shape,...  13.3 us
    pallas_call x1, Pallas kernels, second_round(): pl.pallas_call(second_round_kernel, out_shape=jax.ShapeDtypeStruct(shape,...  12.4 us
    ppermute x3, starting transfers between devices, both_ways(): from_low = lax.ppermute(high, axis, forward)  10.8 us
    all_to_all x5, waiting for transfers between devices, exchange(): lax.all_to_all(copies, ('slab', 'pair'), split_axis=0, concat_axis=0, til...  8.69 us
    ppermute x3, starting transfers between devices, both_ways(): from_high = lax.ppermute(low, axis, backward)  3.84 us
  transfers between devices with their start and end apart: 11, of which 5 were waited for; matrix products, arithmetic and copies ran while one was open for 1% of the time, Pallas kernels for 28%

profile of v4, /device:TPU:0, one launch (start us, length us, event | category | flops | bytes accessed | tf_op | source)
XLA Modules:
  0.0 142.6 jit_solution(10207267164702468104)
XLA Ops:
  0.6 2.1 %emit.1 = (f32[16,128]{1,0:T(8,128)}, f32[32,16,128]{2,1,0:T(8,128)}) custom-call(f32[16,64,512]{2,1,0:T(8,128)} %t_ref, s32[16,128]{1,0:T(8,128)} %site_ref.3, f32[16,128]{1,0:T(8,128)} %mirror_ref.5), custom_call_target="tpu_custom_call" | custom-call | flops 10000 | bytes 900000 | tf_op jit(solution)/shard_map/emit/pallas_call | solution.py:76
  2.8 7.4 %all-to-all-start = ((f32[32,16,128]{2,1,0:T(8,128)}), f32[32,16,128]{2,1,0:T(8,128)}, u32[]{:S(2)}, u32[]{:S(2)}) async-start(f32[32,16,128]{2,1,0:T(8,128)} %get-tuple-element.30), calls=%async_computation | async-start | bytes 524288 | tf_op jit(solution)/shard_map/all_to_all | solution.py:785
  10.2 2.3 %pack_x.1 = (f32[272,512]{1,0:T(8,128)}, f32[272,512]{1,0:T(8,128)}) custom-call(f32[16,64,512]{2,1,0:T(8,128)} %t_ref, f32[16,64,512]{2,1,0:T(8,128)} %k_ref.1, f32[16,64,512]{2,1,0:T(8,128)} %k_ref.1, f32[16,64,512]{2,1,0:T(8,128)} %t_ref, f32[16,64,512]{2,1,0:T(8,128)} %k_ref.1, f32[16,64,512]{2,1,0:T(8,128)} %k_ref.1), custom_call_target="tpu_custom_call" | custom-call | bytes 2228224 | tf_op jit(solution)/shard_map/pack_x/pallas_call | solution.py:292
  12.5 8.3 %all-to-all-done = f32[32,16,128]{2,1,0:T(8,128)} async-done(((f32[32,16,128]{2,1,0:T(8,128)}), f32[32,16,128]{2,1,0:T(8,128)}, u32[]{:S(2)}, u32[]{:S(2)}) %all-to-all-start) | async-done | bytes 262176 | tf_op jit(solution)/shard_map/all_to_all | solution.py:785
  20.8 3.6 %collective-permute-start = (f32[272,512]{1,0:T(8,128)}, f32[272,512]{1,0:T(8,128)}, u32[]{:S(2)}, u32[]{:S(2)}) collective-permute-start(f32[272,512]{1,0:T(8,128)} %get-tuple-element.35), channel_id=1, source_target_pairs={{0,4},{4,8},{8,12},{12,16},{16,20},{20,24},{24,28},{1,5},{5,9},{9,... | collective-permute-start | bytes 1671176 | tf_op jit(solution)/shard_map/ppermute | solution.py:796
  24.4 1.3 collective-permute-start.1
  26.3 6.6 %tiles.2 = f32[512,128]{1,0:T(8,128)} custom-call(s32[1]{0:T(128)S(6)} %copy.11.live_ref, s32[2,256]{1,0:T(2,128)} %bitcast.25, s32[2,256]{1,0:T(2,128)} %bitcast.26, f32[512,128]{1,0:T(8,128)} %bitcast.1.whole_ref, f32[256,128,128]{2,1,0:T(8,128)} %tiles_ref.3), custom_call_target="tpu_custom_call" | custom-call | flops 134217728 | bytes 16777216 | tf_op jit(solution)/shard_map/tiles/pallas_call | solution.py:177
  33.0 8.7 %all-to-all-start.1 = ((f32[32,16,128]{2,1,0:T(8,128)}), f32[32,16,128]{2,1,0:T(8,128)}, u32[]{:S(2)}, u32[]{:S(2)}) async-start(f32[32,16,128]{2,1,0:T(8,128)} %bitcast.24), calls=%async_computation.1 | async-start | bytes 524288 | tf_op jit(solution)/shard_map/all_to_all | solution.py:785
  41.7 7.7 %collective-permute-done.low_ref = f32[272,512]{1,0:T(8,128)} collective-permute-done((f32[272,512]{1,0:T(8,128)}, f32[272,512]{1,0:T(8,128)}, u32[]{:S(2)}, u32[]{:S(2)}) %collective-permute-start) | collective-permute-done | bytes 557088 | tf_op jit(solution)/shard_map/ppermute | solution.py:796
  49.4 0.0 collective-permute-done.1.high_ref
  49.4 2.5 %pack_y.1 = (f32[20,8,512]{2,1,0:T(8,128)}, f32[20,8,512]{2,1,0:T(8,128)}) custom-call(f32[16,64,512]{2,1,0:T(8,128)} %t_ref, f32[16,64,512]{2,1,0:T(8,128)} %k_ref.1, f32[16,64,512]{2,1,0:T(8,128)} %t_ref, f32[16,64,512]{2,1,0:T(8,128)} %k_ref.1, f32[272,512]{1,0:T(8,128)} %collective-permute-done.low_ref, f32[272,512]{1,0:T(8,128)} %collective-permute-done.1.high_ref), custom_call_target="tpu_custom_call" | custom-call | bytes 1310720 | tf_op jit(solution)/shard_map/pack_y/pallas_call | solution.py:333
  51.8 0.4 all-to-all-done.1.parts_ref
  52.2 1.7 %middle.1 = f32[32,16,128]{2,1,0:T(8,128)} custom-call(f32[32,16,128]{2,1,0:T(8,128)} %all-to-all-done.1.parts_ref, f32[16,128]{1,0:T(8,128)} %get-tuple-element.40.emitted_ref, f32[16,128]{1,0:T(8,128)} %mirror_ref.5), custom_call_target="tpu_custom_call" | custom-call | flops 100000 | bytes 600000 | tf_op jit(solution)/shard_map/middle/pallas_call | solution.py:210
  54.0 5.1 %all-to-all-start.2 = ((f32[32,16,128]{2,1,0:T(8,128)}), f32[32,16,128]{2,1,0:T(8,128)}, u32[]{:S(2)}, u32[]{:S(2)}) async-start(f32[32,16,128]{2,1,0:T(8,128)} %middle.1), calls=%async_computation.2 | async-start | bytes 524288 | tf_op jit(solution)/shard_map/all_to_all | solution.py:785
  59.1 2.8 %collective-permute-start.2 = (f32[20,8,512]{2,1,0:T(8,128)}, f32[20,8,512]{2,1,0:T(8,128)}, u32[]{:S(2)}, u32[]{:S(2)}) collective-permute-start(f32[20,8,512]{2,1,0:T(8,128)} %get-tuple-element.41), channel_id=1, source_target_pairs={{0,1},{1,2},{2,3},{4,5},{5,6},{6,7},{8,9},{9,10},{10,11},{12,13},{... | collective-permute-start | bytes 983048 | tf_op jit(solution)/shard_map/ppermute | solution.py:796
  61.9 1.3 collective-permute-start.3
  63.2 0.0 collective-permute-done.2.below_ref
  63.2 3.0 %collective-permute-done.3.above_ref = f32[20,8,512]{2,1,0:T(8,128)} collective-permute-done((f32[20,8,512]{2,1,0:T(8,128)}, f32[20,8,512]{2,1,0:T(8,128)}, u32[]{:S(2)}, u32[]{:S(2)}) %collective-permute-start.3) | collective-permute-done | bytes 327712 | tf_op jit(solution)/shard_map/ppermute | solution.py:797
  66.2 16.3 %first_round.1 = (f32[16,72,512]{2,1,0:T(8,128)}, f32[2,72,512]{2,1,0:T(8,128)}, f32[2,72,512]{2,1,0:T(8,128)}, f32[20,72,512]{2,1,0:T(8,128)}, f32[24,8,128]{2,1,0:T(8,128)}) custom-call(f32[16,64,512]{2,1,0:T(8,128)} %t_ref, f32[16,64,512]{2,1,0:T(8,128)} %k_ref.1, f32[272,512]{1,0:T(8,128)} %collective-permute-done.low_ref, ...), custom_call_target="tpu_custom_call" | custom-call | flops 73728000 | bytes 25165824 | tf_op jit(solution)/shard_map/first_round/pallas_call | solution.py:615
  82.5 0.0 all-to-all-done.2
  82.5 6.6 %tiles.3 = f32[512,128]{1,0:T(8,128)} custom-call(s32[1]{0:T(128)S(6)} %copy.11.live_ref, s32[2,256]{1,0:T(2,128)} %bitcast.27, s32[2,256]{1,0:T(2,128)} %bitcast.28, f32[512,128]{1,0:T(8,128)} %bitcast.3.whole_ref, f32[256,128,128]{2,1,0:T(8,128)} %tiles_ref.3), custom_call_target="tpu_custom_call" | custom-call | flops 134217728 | bytes 16777216 | tf_op jit(solution)/shard_map/tiles/pallas_call | solution.py:177
  89.1 10.2 %all-to-all-start.3 = ((f32[32,16,128]{2,1,0:T(8,128)}), f32[32,16,128]{2,1,0:T(8,128)}, u32[]{:S(2)}, u32[]{:S(2)}) async-start(f32[32,16,128]{2,1,0:T(8,128)} %bitcast.23), calls=%async_computation.3 | async-start | bytes 524288 | tf_op jit(solution)/shard_map/all_to_all | solution.py:785
  99.4 4.3 %collective-permute-start.4 = (f32[2,72,512]{2,1,0:T(8,128)}, f32[2,72,512]{2,1,0:T(8,128)}, u32[]{:S(2)}, u32[]{:S(2)}) collective-permute-start(f32[2,72,512]{2,1,0:T(8,128)} %get-tuple-element.46), channel_id=1, source_target_pairs={{0,4},{4,8},{8,12},{12,16},{16,20},{20,24},{24,28},{1,5},{5,9},{9,... | collective-permute-start | bytes 884744 | tf_op jit(solution)/shard_map/ppermute | solution.py:796
  103.7 1.3 collective-permute-start.5
  105.0 12.3 %collective-permute-done.4.low_ref = f32[2,72,512]{2,1,0:T(8,128)} collective-permute-done((f32[2,72,512]{2,1,0:T(8,128)}, f32[2,72,512]{2,1,0:T(8,128)}, u32[]{:S(2)}, u32[]{:S(2)}) %collective-permute-start.4) | collective-permute-done | bytes 294944 | tf_op jit(solution)/shard_map/ppermute | solution.py:796
  117.3 0.0 collective-permute-done.5.high_ref
  117.3 0.0 all-to-all-done.3.parts_ref
  117.3 2.2 %last.1 = (f32[16,128]{1,0:T(8,128)}, f32[32,8,128]{2,1,0:T(8,128)}) custom-call(f32[32,16,128]{2,1,0:T(8,128)} %all-to-all-done.3.parts_ref, f32[16,128]{1,0:T(8,128)} %get-tuple-element.40.emitted_ref, f32[16,128]{1,0:T(8,128)} %mirror_ref.5, s32[16,128]{1,0:T(8,128)} %site_ref.3), custom_call_target="tpu_custom_call" | custom-call | flops 10000000 | bytes 600000 | tf_op jit(solution)/shard_map/last/pallas_call | solution.py:251
  119.5 6.7 %all-to-all-start.4 = ((f32[32,8,128]{2,1,0:T(8,128)}), f32[32,8,128]{2,1,0:T(8,128)}, u32[]{:S(2)}, u32[]{:S(2)}) async-start(f32[32,8,128]{2,1,0:T(8,128)} %get-tuple-element.50), calls=%async_computation.4 | async-start | bytes 262144 | tf_op jit(solution)/shard_map/all_to_all | solution.py:785
  126.3 0.1 stack.79
  126.4 0.6 convert_element_type.3.flag_ref
  127.0 0.6 stack.69.near_ref
  127.6 12.4 %second_round.1.base_ref = f32[16,64,512]{2,1,0:T(8,128)} custom-call(f32[16,72,512]{2,1,0:T(8,128)} %get-tuple-element.52.t_ref, f32[2,72,512]{2,1,0:T(8,128)} %collective-permute-done.4.low_ref, f32[2,72,512]{2,1,0:T(8,128)} %collective-permute-done.5.high_ref, f32[20,72,512]{2,1,0:T(8,128)} %get-tuple-element.55.k_ref), custom_call_target="tpu_custom_call" | custom-call | flops 44236800 | bytes 18874368 | tf_op jit(solution)/shard_map/second_round/pallas_call | solution.py:669
  140.0 0.0 all-to-all-done.4.all_ref
  140.0 2.6 %add_source.1 = f32[16,64,512]{2,1,0:T(8,128)} custom-call(s32[9]{0:T(128)} %stack.69.near_ref, s32[9]{0:T(128)} %convert_element_type.3.flag_ref, f32[32,8,128]{2,1,0:T(8,128)} %all-to-all-done.4.all_ref, f32[24,8,128]{2,1,0:T(8,128)} %get-tuple-element.51.thin_ref, f32[16,64,512]{2,1,0:T(8,128)} %second_round.1.base_ref), custom_call_target="tpu_custom_call", output_to_operand_aliasing={{}: (4, {})} | custom-call | flops 1000000 | bytes 1048576 | tf_op jit(solution)/shard_map/add_source/pallas_call | solution.py:765
Async XLA Ops:
  2.8 18.0 %all-to-all-start = ((f32[32,16,128]{2,1,0:T(8,128)}), f32[32,16,128]{2,1,0:T(8,128)}, u32[]{:S(2)}, u32[]{:S(2)}) async-start(f32[32,16,128]{2,1,0:T(8,128)} %get-tuple-element.30), calls=%async_computation | async-start | bytes 524288 | tf_op jit(solution)/shard_map/all_to_all | solution.py:785
  20.8 28.6 %collective-permute-start = (f32[272,512]{1,0:T(8,128)}, f32[272,512]{1,0:T(8,128)}, u32[]{:S(2)}, u32[]{:S(2)}) collective-permute-start(f32[272,512]{1,0:T(8,128)} %get-tuple-element.35), channel_id=1, source_target_pairs={{0,4},{4,8},{8,12},{12,16},{16,20},{20,24},{24,28},{1,5},{5,9},{9,... | collective-permute-start | bytes 1671176 | tf_op jit(solution)/shard_map/ppermute | solution.py:796
  24.4 25.0 %collective-permute-start.1 = (f32[272,512]{1,0:T(8,128)}, f32[272,512]{1,0:T(8,128)}, u32[]{:S(2)}, u32[]{:S(2)}) collective-permute-start(f32[272,512]{1,0:T(8,128)} %get-tuple-element.36), channel_id=1, source_target_pairs={{4,0},{8,4},{12,8},{16,12},{20,16},{24,20},{28,24},{5,1},{9,5},{13... | collective-permute-start | bytes 1671176 | tf_op jit(solution)/shard_map/ppermute | solution.py:797
  33.0 19.3 %all-to-all-start.1 = ((f32[32,16,128]{2,1,0:T(8,128)}), f32[32,16,128]{2,1,0:T(8,128)}, u32[]{:S(2)}, u32[]{:S(2)}) async-start(f32[32,16,128]{2,1,0:T(8,128)} %bitcast.24), calls=%async_computation.1 | async-start | bytes 524288 | tf_op jit(solution)/shard_map/all_to_all | solution.py:785
  54.0 28.5 %all-to-all-start.2 = ((f32[32,16,128]{2,1,0:T(8,128)}), f32[32,16,128]{2,1,0:T(8,128)}, u32[]{:S(2)}, u32[]{:S(2)}) async-start(f32[32,16,128]{2,1,0:T(8,128)} %middle.1), calls=%async_computation.2 | async-start | bytes 524288 | tf_op jit(solution)/shard_map/all_to_all | solution.py:785
  59.1 4.1 %collective-permute-start.2 = (f32[20,8,512]{2,1,0:T(8,128)}, f32[20,8,512]{2,1,0:T(8,128)}, u32[]{:S(2)}, u32[]{:S(2)}) collective-permute-start(f32[20,8,512]{2,1,0:T(8,128)} %get-tuple-element.41), channel_id=1, source_target_pairs={{0,1},{1,2},{2,3},{4,5},{5,6},{6,7},{8,9},{9,10},{10,11},{12,13},{... | collective-permute-start | bytes 983048 | tf_op jit(solution)/shard_map/ppermute | solution.py:796
  61.9 4.3 %collective-permute-start.3 = (f32[20,8,512]{2,1,0:T(8,128)}, f32[20,8,512]{2,1,0:T(8,128)}, u32[]{:S(2)}, u32[]{:S(2)}) collective-permute-start(f32[20,8,512]{2,1,0:T(8,128)} %get-tuple-element.42), channel_id=1, source_target_pairs={{1,0},{2,1},{3,2},{5,4},{6,5},{7,6},{9,8},{10,9},{11,10},{13,12},{... | collective-permute-start | bytes 983048 | tf_op jit(solution)/shard_map/ppermute | solution.py:797
  89.1 28.2 %all-to-all-start.3 = ((f32[32,16,128]{2,1,0:T(8,128)}), f32[32,16,128]{2,1,0:T(8,128)}, u32[]{:S(2)}, u32[]{:S(2)}) async-start(f32[32,16,128]{2,1,0:T(8,128)} %bitcast.23), calls=%async_computation.3 | async-start | bytes 524288 | tf_op jit(solution)/shard_map/all_to_all | solution.py:785
  99.4 17.9 %collective-permute-start.4 = (f32[2,72,512]{2,1,0:T(8,128)}, f32[2,72,512]{2,1,0:T(8,128)}, u32[]{:S(2)}, u32[]{:S(2)}) collective-permute-start(f32[2,72,512]{2,1,0:T(8,128)} %get-tuple-element.46), channel_id=1, source_target_pairs={{0,4},{4,8},{8,12},{12,16},{16,20},{20,24},{24,28},{1,5},{5,9},{9,... | collective-permute-start | bytes 884744 | tf_op jit(solution)/shard_map/ppermute | solution.py:796
  103.7 13.6 %collective-permute-start.5 = (f32[2,72,512]{2,1,0:T(8,128)}, f32[2,72,512]{2,1,0:T(8,128)}, u32[]{:S(2)}, u32[]{:S(2)}) collective-permute-start(f32[2,72,512]{2,1,0:T(8,128)} %get-tuple-element.47), channel_id=1, source_target_pairs={{4,0},{8,4},{12,8},{16,12},{20,16},{24,20},{28,24},{5,1},{9,5},{13... | collective-permute-start | bytes 884744 | tf_op jit(solution)/shard_map/ppermute | solution.py:797
  119.5 20.5 %all-to-all-start.4 = ((f32[32,8,128]{2,1,0:T(8,128)}), f32[32,8,128]{2,1,0:T(8,128)}, u32[]{:S(2)}, u32[]{:S(2)}) async-start(f32[32,8,128]{2,1,0:T(8,128)} %get-tuple-element.50), calls=%async_computation.4 | async-start | bytes 262144 | tf_op jit(solution)/shard_map/all_to_all | solution.py:785

commit v5 on v4

--- a/solution.py
+++ b/solution.py
@@ -15,6 +15,7 @@
 ROWS = STEPS
 LANES = 128
 CHUNK = 16
+LAG = 40
 
 step_size = 0.07
 
@@ -38,6 +39,30 @@
         x = x - part.astype(jnp.float32)
     out.append(x.astype(jnp.bfloat16))
     return out
+
+
+class Lagging:
+    def __init__(self, depth):
+        self.depth = depth
+        self.waiting = []
+
+    def add(self, store):
+        self.waiting.append(store)
+        if len(self.waiting) > self.depth:
+            self.waiting.pop(0)()
+
+    def finish(self):
+        for store in self.waiting:
+            store()
+        self.waiting = []
+
+
+def put(ref, index, value):
+    return lambda: ref.__setitem__(index, value)
+
+
+def unrolled(begin, end, most):
+    return max(u for u in range(1, most + 1) if (end - begin) % u == 0)
 
 
 def emit_kernel(temp_ref, site_ref, mirror_ref, emitted_ref, copies_ref):
@@ -118,6 +143,7 @@
     @pl.loop(0, chunks)
     def _(c):
         chunk_copy(c).wait()
+        stores = Lagging(4 * CHUNK)
         for u in range(0, CHUNK, 2):
             t = c * CHUNK + u
             high_a, low_a = parts_of(held[t], 2)
@@ -149,8 +175,10 @@
                 preferred_element_type=jnp.float32,
             )
             for side, result in ((0, first), (1, second)):
-                terms[side, pl.ds(t, 1), :] = result[0:1, :BLK] + result[1:2, :BLK]
-                terms[side, pl.ds(t + 1, 1), :] = result[8:9, BLK:] + result[9:10, BLK:]
+                for v, (top_row, cols) in enumerate(((0, slice(0, BLK)), (8, slice(BLK, 2 * BLK)))):
+                    row = result[top_row : top_row + 1, cols] + result[top_row + 1 : top_row + 2, cols]
+                    stores.add(put(terms, (side, pl.ds(t + v, 1)), row))
+        stores.finish()
 
     used = lax.broadcasted_iota(jnp.int32, (slots, BLK), 0) < live
     used_lane = lax.broadcasted_iota(jnp.int32, (1, slots), 1) < live
@@ -184,7 +212,7 @@
             pltpu.VMEM((2, slots, BLK), jnp.float32),
             pltpu.SemaphoreType.DMA((slots // CHUNK,)),
         ],
-        compiler_params=params(64),
+        compiler_params=params(50),
         cost_estimate=cost(slots * BLK * BLK * 32, slots * BLK * BLK * 4),
         name="tiles",
     )(live, couples, couples, whole, tiles)
@@ -210,7 +238,7 @@
     return pl.pallas_call(
         middle_kernel,
         out_shape=jax.ShapeDtypeStruct(parts.shape, jnp.float32),
-        compiler_params=params(64),
+        compiler_params=params(32),
         cost_estimate=cost(100_000, 600_000),
         name="middle",
     )(parts, emitted, mirror)
@@ -254,7 +282,7 @@
             jax.ShapeDtypeStruct(mirror.shape, jnp.float32),
             jax.ShapeDtypeStruct((count, cells // LANES, LANES), jnp.float32),
         ),
-        compiler_params=params(64),
+        compiler_params=params(32),
         cost_estimate=cost(10_000_000, 600_000),
         name="last",
     )(parts, emitted, mirror, site)
@@ -304,14 +332,14 @@
 def pack_y_kernel(nx, ny, t0, k0, t7, k7, low_ref, high_ref, down_ref, up_ref):
     upper = lax.broadcasted_iota(jnp.int32, down_ref.shape[1:], 0) < ROWS
 
-    def put(x, t_first, k_first, t_final, k_final):
+    def edge(x, t_first, k_first, t_final, k_final):
         down_ref[x] = jnp.where(upper, t_first, pltpu.roll(k_first, ROWS, 0))
         up_ref[x] = jnp.where(upper, pltpu.roll(t_final, ROWS, 0), k_final)
 
     for side, base in ((low_ref, 0), (high_ref, DEPTH + nx)):
         for p in range(DEPTH):
             t_at, k_at = p * ny, (DEPTH + p) * ny
-            put(
+            edge(
                 base + p,
                 side[t_at : t_at + 8, :],
                 side[k_at : k_at + 8, :],
@@ -319,7 +347,7 @@
                 side[k_at + ny - 8 : k_at + ny, :],
             )
     for x in range(nx):
-        put(DEPTH + x, t0[x], k0[x], t7[x], k7[x])
+        edge(DEPTH + x, t0[x], k0[x], t7[x], k7[x])
 
 
 def pack_y(temp, cond, low, high):
@@ -355,60 +383,44 @@
     return [slice(j * LANES, (j + 1) * LANES) for j in range(nz // LANES)]
 
 
-class Lagging:
-    def __init__(self, depth):
-        self.depth = depth
-        self.waiting = []
-
-    def add(self, store):
-        self.waiting.append(store)
-        if len(self.waiting) > self.depth:
-            self.waiting.pop(0)()
-
-    def finish(self):
-        for store in self.waiting:
-            store()
-        self.waiting = []
-
-
-def put(ref, index, value):
-    return lambda: ref.__setitem__(index, value)
-
-
 def prepare(cond, gx, gy, gz, gb):
     tall, wide, nz = cond.shape
     tiles = wide // 8
     lane = lax.broadcasted_iota(jnp.int32, (8, LANES), 1)
     half = 0.5 * step_size
 
-    @pl.loop(0, tall)
-    def _(x):
-        after = jnp.minimum(x + 1, tall - 1)
-        stores = Lagging(16)
-        for z in lane_tiles(nz):
-            last = z.stop == nz
-            for t in range(tiles):
-                rows = slice(8 * t, 8 * t + 8)
-                here = cond[x, rows, z]
-                stores.add(put(gx, (x, rows, z), half * (here + cond[after, rows, z])))
-                if t + 1 < tiles:
-                    beside = cond[x, 8 * t + 8 : 8 * t + 16, z]
-                else:
-                    beside = pltpu.roll(cond[x, :8, z], 7, 0)
-                stores.add(put(gy, (x, rows, z), half * (here + beside)))
-                turned = pltpu.roll(here, LANES - 1, 1)
-                if last:
-                    deeper = here
-                else:
-                    deeper = pltpu.roll(cond[x, rows, z.stop : z.stop + LANES], LANES - 1, 1)
-                deeper = jnp.where(lane < LANES - 1, turned, deeper)
-                stores.add(put(gz, (x, rows, z), half * (here + deeper)))
-                if z.start == 0:
-                    stores.add(put(gb, (x, rows), step_size * here))
+    together_planes = unrolled(0, tall, 2)
+
+    @pl.loop(0, tall, step=together_planes)
+    def _(base):
+        stores = Lagging(LAG)
+        for p in range(together_planes):
+            x = base + p
+            after = jnp.minimum(x + 1, tall - 1)
+            for z in lane_tiles(nz):
+                last = z.stop == nz
+                for t in range(tiles):
+                    rows = slice(8 * t, 8 * t + 8)
+                    here = cond[x, rows, z]
+                    stores.add(put(gx, (x, rows, z), half * (here + cond[after, rows, z])))
+                    if t + 1 < tiles:
+                        beside = cond[x, 8 * t + 8 : 8 * t + 16, z]
+                    else:
+                        beside = pltpu.roll(cond[x, :8, z], 7, 0)
+                    stores.add(put(gy, (x, rows, z), half * (here + beside)))
+                    turned = pltpu.roll(here, LANES - 1, 1)
+                    if last:
+                        deeper = here
+                    else:
+                        deeper = pltpu.roll(cond[x, rows, z.stop : z.stop + LANES], LANES - 1, 1)
+                    deeper = jnp.where(lane < LANES - 1, turned, deeper)
+                    stores.add(put(gz, (x, rows, z), half * (here + deeper)))
+                    if z.start == 0:
+                        stores.add(put(gb, (x, rows), step_size * here))
         stores.finish()
 
 
-def one_step(field, begin, end, target, gx, gy, gz, gb, carried):
+def one_step(field, begin, end, target, gx, gy, gz, gb):
     wide, nz = field.shape[1:]
     tiles = wide // 8
     lane = lax.broadcasted_iota(jnp.int32, (8, LANES), 1)
@@ -417,14 +429,12 @@
     keep_above = (sub < 7) | has_above
     keep_below = (sub < 7) | has_below
 
-    carried[...] = gx[begin - 1] * (field[begin] - field[begin - 1])
-
-    @pl.loop(begin, end)
-    def _(x):
+    spans = lane_tiles(nz)
+    count = len(spans)
+    together_planes = unrolled(begin, end, 4)
+
+    def plane_step(x, stores):
         here, across_y = {}, {}
-        stores = Lagging(16)
-        spans = lane_tiles(nz)
-        count = len(spans)
 
         def tile(t, j):
             if (t, j) not in here:
@@ -454,13 +464,18 @@
                 low_z = back[j - 1] if j else gb[x, rows, :] * now
                 low_z = jnp.where(lane > 0, back[j], low_z)
                 x_flux = gx[x, rows, spans[j]] * (field[x + 1, rows, spans[j]] - now)
-                low_x = carried[rows, spans[j]]
-                stores.add(put(carried, (rows, spans[j]), x_flux))
+                low_x = gx[x - 1, rows, spans[j]] * (now - field[x - 1, rows, spans[j]])
                 low_y = y_flux(t - 1, j) if t else pltpu.roll(y_flux(tiles - 1, j), 1, 0)
                 new = now + (x_flux - low_x) + (y_flux(t, j) - low_y) + (flux[j] - low_z)
                 if t:
                     new = jnp.where(keep_above if t <= ROWS else keep_below, new, 0.0)
                 stores.add(put(*target(x, t, spans[j]), new))
+
+    @pl.loop(begin, end, step=together_planes)
+    def _(base):
+        stores = Lagging(LAG)
+        for p in range(together_planes):
+            plane_step(base + p, stores)
         stores.finish()
 
 
@@ -490,7 +505,7 @@
 def first_round_kernel(
     t_ref, k_ref, low_ref, high_ref, below_ref, above_ref,
     out_ref, low_out, high_out, cond_out, thin_ref,
-    loaded, field, between, gx, gy, gz, gb, carried, sems,
+    loaded, field, between, gx, gy, gz, gb, sems,
 ):
     nx, ny, nz = t_ref.shape
     tall, wide = nx + 2 * DEPTH, ny + 2 * ROWS
@@ -560,7 +575,7 @@
 
     @pl.loop(0, tall)
     def _(x):
-        stores = Lagging(16)
+        stores = Lagging(LAG)
         for t in range(tiles):
             rows = pl.ds(t, 8, stride=tiles)
             for j, z in enumerate(spans):
@@ -573,24 +588,25 @@
     def target(x, t, z):
         return out_ref, (x - DEPTH, slice(8 * t, 8 * t + 8), z)
 
-    two_steps(field, between, gx, gy, gz, gb, carried, target)
+    two_steps(field, between, gx, gy, gz, gb, target)
     low_out[...] = out_ref[:DEPTH]
     high_out[...] = out_ref[nx - DEPTH :]
 
 
-def two_steps(field, between, gx, gy, gz, gb, carried, target):
+def two_steps(field, between, gx, gy, gz, gb, target):
     tall = field.shape[0]
     has_low, has_high, _, _ = neighbours()
-    for x in (1, tall - 2):
-        between[x] = jnp.zeros(field.shape[1:], jnp.float32)
-
     def inner(x, t, z):
         return between, (x, slice(8 * t, 8 * t + 8), z)
 
-    begin = jnp.where(has_low, 1, DEPTH)
-    end = jnp.where(has_high, tall - 1, tall - DEPTH)
-    one_step(field, begin, end, inner, gx, gy, gz, gb, carried)
-    one_step(between, DEPTH, tall - DEPTH, target, gx, gy, gz, gb, carried)
+    one_step(field, 1, tall - 1, inner, gx, gy, gz, gb)
+    for x, inside in ((1, has_low), (tall - 2, has_high)):
+
+        @pl.when(jnp.logical_not(inside))
+        def _():
+            between[x] = jnp.zeros(field.shape[1:], jnp.float32)
+
+    one_step(between, DEPTH, tall - DEPTH, target, gx, gy, gz, gb)
 
 
 def heat_scratch(tall, wide, nz):
@@ -602,7 +618,6 @@
         big,
         big,
         pltpu.VMEM((tall, wide, LANES), jnp.float32),
-        pltpu.VMEM((wide, nz), jnp.float32),
     ]
 
 
@@ -633,7 +648,7 @@
 
 def second_round_kernel(
     t_ref, low_ref, high_ref, k_ref, out_ref,
-    cond, field, between, gx, gy, gz, gb, carried, placed, sems,
+    cond, field, between, gx, gy, gz, gb, placed, sems,
 ):
     nx, wide, nz = t_ref.shape
     ny = out_ref.shape[1]
@@ -654,7 +669,7 @@
     def target(x, t, z):
         return placed, (x - DEPTH, z.start // LANES, pl.ds(t, 8, stride=tiles))
 
-    two_steps(field, between, gx, gy, gz, gb, carried, target)
+    two_steps(field, between, gx, gy, gz, gb, target)
 
     @pl.loop(0, nx)
     def _(x):
@@ -824,20 +839,20 @@
 
     whole = exchange(copies)
     send_low, send_high = pack_x(temp, cond)
-    whole, send_low, send_high = together(whole, send_low, send_high)
     low, high = both_ways(send_low, send_high, "slab")
+    whole = together(whole, send_low, send_high)[0]
     parts = exchange(sweep_terms(whole))
     send_down, send_up = pack_y(temp, cond, low, high)
-    parts, send_down, send_up = together(parts, send_down, send_up)
+    parts = together(parts, send_down, send_up)[0]
     below, above = both_ways(send_down, send_up, "pair")
     whole = exchange(middle(parts, emitted, mirror_fraction))
     middle_temp, send_low, send_high, strided_cond, thin = first_round(
         temp, cond, low, high, below, above
     )
-    whole, send_low, send_high = together(whole, send_low, send_high)
     low, high = both_ways(send_low, send_high, "slab")
-    parts = exchange(sweep_terms(whole))
-    parts, low, high = together(parts, low, high)
+    whole = together(whole, send_low, send_high)[0]
+    term, low, high = together(sweep_terms(whole), low, high)
+    parts = exchange(term)
     radiosity, source = last(parts, emitted, mirror_fraction, element_facing_site, nx * ny)
     everything = exchange(source)
     base = second_round(middle_temp, low, high, strided_cond, temp.shape)

time: 144 us -> 143 us (level)
  waiting for transfers between devices: 31.7 us -> 13.5 us
  blocking collectives: 0 us -> 16.8 us
  starting transfers between devices: 52.8 us -> 39.9 us
  Pallas kernels: 55.4 us -> 66.1 us
  local copies, waits for them, and re-layouts: 0.7 us -> 3.54 us
    all_to_all x0 -> x1, blocking collectives: none -> 16.8 us  [exchange(): lax.all_to_all(copies, ('slab', 'pair'), split_axis=0, concat_axis=0, til...]
    all_to_all x5 -> x4, starting transfers between devices: 38.2 us -> 26.1 us  [exchange(): lax.all_to_all(copies, ('slab', 'pair'), split_axis=0, concat_axis=0, til...]
    ppermute x3, waiting for transfers between devices: 20 us -> 11.6 us  [both_ways(): from_low = lax.ppermute(high, axis, forward)]
    all_to_all x5 -> x4, waiting for transfers between devices: 8.69 us -> 1.92 us  [exchange(): lax.all_to_all(copies, ('slab', 'pair'), split_axis=0, concat_axis=0, til...]
    pallas_call x1, Pallas kernels: 12.4 us -> 17.9 us  [second_round(): pl.pallas_call(second_round_kernel, out_shape=jax.ShapeDtypeStruct(shape,...]
    pallas_call x1, Pallas kernels: 16.3 us -> 21 us  [first_round(): pl.pallas_call(first_round_kernel, out_shape=(jax.ShapeDtypeStruct((nx, w...]
    ppermute x3, waiting for transfers between devices: 2.96 us -> 0.01 us  [both_ways(): from_high = lax.ppermute(low, axis, backward)]
    unnamed x0 -> x18, local copies, waits for them, and re-layouts: none -> 2.77 us
  transfers between devices with their start and end apart: 11 -> 10, of which waited for: 5 -> 3; matrix products, arithmetic and copies ran while one was open for 1% -> 1% of each run, Pallas kernels for 28% -> 42%
where the time goes in v5:
time: 143 us; the launch traced here: 142 us
  Pallas kernels  66.1 us (46%)
  starting transfers between devices  39.9 us (28%)
  blocking collectives  16.8 us (12%)
  waiting for transfers between devices  13.5 us (9%)
  local copies, waits for them, and re-layouts  3.54 us (2%)
  between operations  1.51 us (1%)
    all_to_all x4, starting transfers between devices, exchange(): lax.all_to_all(copies, ('slab', 'pair'), split_axis=0, concat_axis=0, til...  26.1 us
    pallas_call x1, Pallas kernels, first_round(): pl.pallas_call(first_round_kernel, out_shape=(jax.ShapeDtypeStruct((nx, w...  21 us
    pallas_call x1, Pallas kernels, second_round(): pl.pallas_call(second_round_kernel, out_shape=jax.ShapeDtypeStruct(shape,...  17.9 us
    all_to_all x1, blocking collectives, exchange(): lax.all_to_all(copies, ('slab', 'pair'), split_axis=0, concat_axis=0, til...  16.8 us
    pallas_call x2, Pallas kernels, tile_terms(): pl.pallas_call(tiles_kernel, out_shape=jax.ShapeDtypeStruct(whole.shape,...  14.7 us
    ppermute x3, waiting for transfers between devices, both_ways(): from_low = lax.ppermute(high, axis, forward)  11.6 us
    ppermute x3, starting transfers between devices, both_ways(): from_low = lax.ppermute(high, axis, forward)  10 us
    ppermute x3, starting transfers between devices, both_ways(): from_high = lax.ppermute(low, axis, backward)  3.85 us
  transfers between devices with their start and end apart: 10, of which 3 were waited for; matrix products, arithmetic and copies ran while one was open for 1% of the time, Pallas kernels for 42%

profile of v5, /device:TPU:0, one launch (start us, length us, event | category | flops | bytes accessed | tf_op | source)
XLA Modules:
  0.0 142.0 jit_solution(12195995278243194670)
XLA Ops:
  0.6 2.1 %emit.1 = (f32[16,128]{1,0:T(8,128)}, f32[32,16,128]{2,1,0:T(8,128)}) custom-call(f32[16,64,512]{2,1,0:T(8,128)} %t_ref, s32[16,128]{1,0:T(8,128)} %site_ref.3, f32[16,128]{1,0:T(8,128)} %mirror_ref.5), custom_call_target="tpu_custom_call" | custom-call | flops 10000 | bytes 900000 | tf_op jit(solution)/shard_map/emit/pallas_call | solution.py:101
  2.8 7.4 %all-to-all-start = ((f32[32,16,128]{2,1,0:T(8,128)}), f32[32,16,128]{2,1,0:T(8,128)}, u32[]{:S(2)}, u32[]{:S(2)}) async-start(f32[32,16,128]{2,1,0:T(8,128)} %get-tuple-element.24), calls=%async_computation | async-start | bytes 524288 | tf_op jit(solution)/shard_map/all_to_all | solution.py:800
  10.2 2.3 %pack_x.1 = (f32[272,512]{1,0:T(8,128)}, f32[272,512]{1,0:T(8,128)}) custom-call(f32[16,64,512]{2,1,0:T(8,128)} %t_ref, f32[16,64,512]{2,1,0:T(8,128)} %k_ref.1, f32[16,64,512]{2,1,0:T(8,128)} %k_ref.1, f32[16,64,512]{2,1,0:T(8,128)} %t_ref, f32[16,64,512]{2,1,0:T(8,128)} %k_ref.1, f32[16,64,512]{2,1,0:T(8,128)} %k_ref.1), custom_call_target="tpu_custom_call" | custom-call | bytes 2228224 | tf_op jit(solution)/shard_map/pack_x/pallas_call | solution.py:320
  12.5 4.4 %collective-permute-start = (f32[272,512]{1,0:T(8,128)}, f32[272,512]{1,0:T(8,128)}, u32[]{:S(2)}, u32[]{:S(2)}) collective-permute-start(f32[272,512]{1,0:T(8,128)} %get-tuple-element.27), channel_id=1, source_target_pairs={{0,4},{4,8},{8,12},{12,16},{16,20},{20,24},{24,28},{1,5},{5,9},{9,... | collective-permute-start | bytes 1671176 | tf_op jit(solution)/shard_map/ppermute | solution.py:811
  16.9 1.3 collective-permute-start.1
  18.9 1.9 %all-to-all-done = f32[32,16,128]{2,1,0:T(8,128)} async-done(((f32[32,16,128]{2,1,0:T(8,128)}), f32[32,16,128]{2,1,0:T(8,128)}, u32[]{:S(2)}, u32[]{:S(2)}) %all-to-all-start) | async-done | bytes 262176 | tf_op jit(solution)/shard_map/all_to_all | solution.py:800
  20.8 0.0 copy-start.2
  20.8 0.7 copy-done.2
  21.5 7.7 %tiles.2 = f32[512,128]{1,0:T(8,128)} custom-call(s32[1]{0:T(128)S(6)} %copy.11.live_ref, s32[2,256]{1,0:T(2,128)S(1)} %bitcast.24, s32[2,256]{1,0:T(2,128)S(1)} %bitcast.25, f32[512,128]{1,0:T(8,128)} %bitcast.1.whole_ref, f32[256,128,128]{2,1,0:T(8,128)} %tiles_ref.3), custom_call_target="tpu_custom_call" | custom-call | flops 134217728 | bytes 16777216 | tf_op jit(solution)/shard_map/tiles/pallas_call | solution.py:205
  29.2 6.7 %all-to-all-start.1 = ((f32[32,16,128]{2,1,0:T(8,128)}), f32[32,16,128]{2,1,0:T(8,128)}, u32[]{:S(2)}, u32[]{:S(2)}) async-start(f32[32,16,128]{2,1,0:T(8,128)} %bitcast.2), calls=%async_computation.1 | async-start | bytes 524288 | tf_op jit(solution)/shard_map/all_to_all | solution.py:800
  35.9 7.5 %collective-permute-done.low_ref = f32[272,512]{1,0:T(8,128)} collective-permute-done((f32[272,512]{1,0:T(8,128)}, f32[272,512]{1,0:T(8,128)}, u32[]{:S(2)}, u32[]{:S(2)}) %collective-permute-start) | collective-permute-done | bytes 557088 | tf_op jit(solution)/shard_map/ppermute | solution.py:811
  43.4 0.0 collective-permute-done.1.high_ref
  43.4 2.4 %pack_y.1 = (f32[20,8,512]{2,1,0:T(8,128)}, f32[20,8,512]{2,1,0:T(8,128)}) custom-call(f32[16,64,512]{2,1,0:T(8,128)} %t_ref, f32[16,64,512]{2,1,0:T(8,128)} %k_ref.1, f32[16,64,512]{2,1,0:T(8,128)} %t_ref, f32[16,64,512]{2,1,0:T(8,128)} %k_ref.1, f32[272,512]{1,0:T(8,128)} %collective-permute-done.low_ref, f32[272,512]{1,0:T(8,128)} %collective-permute-done.1.high_ref), custom_call_target="tpu_custom_call" | custom-call | bytes 1310720 | tf_op jit(solution)/shard_map/pack_y/pallas_call | solution.py:361
  45.8 2.0 %collective-permute-start.2 = (f32[20,8,512]{2,1,0:T(8,128)}, f32[20,8,512]{2,1,0:T(8,128)}, u32[]{:S(2)}, u32[]{:S(2)}) collective-permute-start(f32[20,8,512]{2,1,0:T(8,128)} %get-tuple-element.30), channel_id=1, source_target_pairs={{0,1},{1,2},{2,3},{4,5},{5,6},{6,7},{8,9},{9,10},{10,11},{12,13},{... | collective-permute-start | bytes 983048 | tf_op jit(solution)/shard_map/ppermute | solution.py:811
  47.8 1.3 collective-permute-start.3
  49.1 0.0 all-to-all-done.1.parts_ref
  49.1 0.0 copy-start
  49.1 0.7 copy-done
  49.8 0.0 copy-start.5
  49.8 0.7 copy-done.5
  50.5 1.7 %middle.1 = f32[32,16,128]{2,1,0:T(8,128)} custom-call(f32[32,16,128]{2,1,0:T(8,128)} %all-to-all-done.1.parts_ref, f32[16,128]{1,0:T(8,128)S(1)} %copy-done.5, f32[16,128]{1,0:T(8,128)S(1)} %copy-done), custom_call_target="tpu_custom_call" | custom-call | flops 100000 | bytes 600000 | tf_op jit(solution)/shard_map/middle/pallas_call | solution.py:238
  52.2 8.7 %all-to-all-start.2 = ((f32[32,16,128]{2,1,0:T(8,128)}), f32[32,16,128]{2,1,0:T(8,128)}, u32[]{:S(2)}, u32[]{:S(2)}) async-start(f32[32,16,128]{2,1,0:T(8,128)} %middle.1), calls=%async_computation.2 | async-start | bytes 524288 | tf_op jit(solution)/shard_map/all_to_all | solution.py:800
  60.9 0.0 collective-permute-done.2.below_ref
  60.9 0.0 collective-permute-done.3.above_ref
  60.9 21.0 %first_round.1 = (f32[16,72,512]{2,1,0:T(8,128)}, f32[2,72,512]{2,1,0:T(8,128)}, f32[2,72,512]{2,1,0:T(8,128)}, f32[20,72,512]{2,1,0:T(8,128)}, f32[24,8,128]{2,1,0:T(8,128)}) custom-call(f32[16,64,512]{2,1,0:T(8,128)} %t_ref, f32[16,64,512]{2,1,0:T(8,128)} %k_ref.1, f32[272,512]{1,0:T(8,128)} %collective-permute-done.low_ref, ...), custom_call_target="tpu_custom_call" | custom-call | flops 73728000 | bytes 25165824 | tf_op jit(solution)/shard_map/first_round/pallas_call | solution.py:630
  81.9 3.6 %collective-permute-start.4 = (f32[2,72,512]{2,1,0:T(8,128)}, f32[2,72,512]{2,1,0:T(8,128)S(1)}, u32[]{:S(2)}, u32[]{:S(2)}) collective-permute-start(f32[2,72,512]{2,1,0:T(8,128)} %get-tuple-element.34), channel_id=1, source_target_pairs={{0,4},{4,8},{8,12},{12,16},{16,20},{20,24},{24,28},{1,5},{5,9},{9,... | collective-permute-start | bytes 884744 | tf_op jit(solution)/shard_map/ppermute | solution.py:811
  85.5 1.3 collective-permute-start.5
  86.8 0.0 all-to-all-done.2
  86.8 0.0 copy-start.3
  86.9 0.7 copy-done.3
  87.5 0.0 copy-start.1
  87.5 0.0 copy-start.4
  87.5 0.0 copy-start.6
  87.5 7.0 %tiles.3 = f32[512,128]{1,0:T(8,128)S(1)} custom-call(s32[1]{0:T(128)S(6)} %copy.11.live_ref, s32[2,256]{1,0:T(2,128)S(1)} %bitcast.26, s32[2,256]{1,0:T(2,128)S(1)} %bitcast.27, f32[512,128]{1,0:T(8,128)} %bitcast.3.whole_ref, f32[256,128,128]{2,1,0:T(8,128)} %tiles_ref.3), custom_call_target="tpu_custom_call" | custom-call | flops 134217728 | bytes 16777216 | tf_op jit(solution)/shard_map/tiles/pallas_call | solution.py:205
  94.6 4.1 %collective-permute-done.4.low_ref = f32[2,72,512]{2,1,0:T(8,128)S(1)} collective-permute-done((f32[2,72,512]{2,1,0:T(8,128)}, f32[2,72,512]{2,1,0:T(8,128)S(1)}, u32[]{:S(2)}, u32[]{:S(2)}) %collective-permute-start.4) | collective-permute-done | bytes 294944 | tf_op jit(solution)/shard_map/ppermute | solution.py:811
  98.7 0.0 copy-start.7
  98.7 0.0 collective-permute-done.5.high_ref
  98.7 0.0 copy-start.8
  98.7 16.8 %all_to_all.25.parts_ref = f32[32,16,128]{2,1,0:T(8,128)S(1)} all-to-all(f32[32,16,128]{2,1,0:T(8,128)S(1)} %bitcast.23), channel_id=1, replica_groups=mesh['slab'=8,'pair'=4] {'slab','pair'}, dimensions={0} | all-to-all | bytes 524288 | tf_op jit(solution)/shard_map/all_to_all | solution.py:800
  115.5 0.0 copy-done.1
  115.5 0.0 copy-done.4
  115.5 0.0 copy-done.6
  115.5 1.2 last.1
  116.7 0.0 copy-done.7
  116.7 0.0 copy-done.8
  116.7 3.3 %all-to-all-start.4 = ((f32[32,8,128]{2,1,0:T(8,128)}), f32[32,8,128]{2,1,0:T(8,128)}, u32[]{:S(2)}, u32[]{:S(2)}) async-start(f32[32,8,128]{2,1,0:T(8,128)} %get-tuple-element.38), calls=%async_computation.4 | async-start | bytes 262144 | tf_op jit(solution)/shard_map/all_to_all | solution.py:800
  120.1 0.1 stack.79
  120.2 0.6 convert_element_type.3.flag_ref
  120.8 0.7 stack.69.near_ref
  121.4 17.9 %second_round.1.base_ref = f32[16,64,512]{2,1,0:T(8,128)} custom-call(f32[16,72,512]{2,1,0:T(8,128)} %get-tuple-element.40.t_ref, f32[2,72,512]{2,1,0:T(8,128)} %copy-done.7, f32[2,72,512]{2,1,0:T(8,128)} %copy-done.8, f32[20,72,512]{2,1,0:T(8,128)} %get-tuple-element.43.k_ref), custom_call_target="tpu_custom_call" | custom-call | flops 44236800 | bytes 18874368 | tf_op jit(solution)/shard_map/second_round/pallas_call | solution.py:684
  139.4 0.0 all-to-all-done.4.all_ref
  139.4 2.6 %add_source.1 = f32[16,64,512]{2,1,0:T(8,128)} custom-call(s32[9]{0:T(128)} %stack.69.near_ref, s32[9]{0:T(128)} %convert_element_type.3.flag_ref, f32[32,8,128]{2,1,0:T(8,128)} %all-to-all-done.4.all_ref, f32[24,8,128]{2,1,0:T(8,128)} %get-tuple-element.39.thin_ref, f32[16,64,512]{2,1,0:T(8,128)} %second_round.1.base_ref), custom_call_target="tpu_custom_call", output_to_operand_aliasing={{}: (4, {})} | custom-call | flops 1000000 | bytes 1048576 | tf_op jit(solution)/shard_map/add_source/pallas_call | solution.py:780
Async XLA Ops:
  2.8 18.0 %all-to-all-start = ((f32[32,16,128]{2,1,0:T(8,128)}), f32[32,16,128]{2,1,0:T(8,128)}, u32[]{:S(2)}, u32[]{:S(2)}) async-start(f32[32,16,128]{2,1,0:T(8,128)} %get-tuple-element.24), calls=%async_computation | async-start | bytes 524288 | tf_op jit(solution)/shard_map/all_to_all | solution.py:800
  12.5 30.8 %collective-permute-start = (f32[272,512]{1,0:T(8,128)}, f32[272,512]{1,0:T(8,128)}, u32[]{:S(2)}, u32[]{:S(2)}) collective-permute-start(f32[272,512]{1,0:T(8,128)} %get-tuple-element.27), channel_id=1, source_target_pairs={{0,4},{4,8},{8,12},{12,16},{16,20},{20,24},{24,28},{1,5},{5,9},{9,... | collective-permute-start | bytes 1671176 | tf_op jit(solution)/shard_map/ppermute | solution.py:811
  16.9 26.4 %collective-permute-start.1 = (f32[272,512]{1,0:T(8,128)}, f32[272,512]{1,0:T(8,128)}, u32[]{:S(2)}, u32[]{:S(2)}) collective-permute-start(f32[272,512]{1,0:T(8,128)} %get-tuple-element.26), channel_id=1, source_target_pairs={{4,0},{8,4},{12,8},{16,12},{20,16},{24,20},{28,24},{5,1},{9,5},{13... | collective-permute-start | bytes 1671176 | tf_op jit(solution)/shard_map/ppermute | solution.py:812
  20.8 0.7 copy-start.2
  29.2 19.9 %all-to-all-start.1 = ((f32[32,16,128]{2,1,0:T(8,128)}), f32[32,16,128]{2,1,0:T(8,128)}, u32[]{:S(2)}, u32[]{:S(2)}) async-start(f32[32,16,128]{2,1,0:T(8,128)} %bitcast.2), calls=%async_computation.1 | async-start | bytes 524288 | tf_op jit(solution)/shard_map/all_to_all | solution.py:800
  45.8 15.1 %collective-permute-start.2 = (f32[20,8,512]{2,1,0:T(8,128)}, f32[20,8,512]{2,1,0:T(8,128)}, u32[]{:S(2)}, u32[]{:S(2)}) collective-permute-start(f32[20,8,512]{2,1,0:T(8,128)} %get-tuple-element.30), channel_id=1, source_target_pairs={{0,1},{1,2},{2,3},{4,5},{5,6},{6,7},{8,9},{9,10},{10,11},{12,13},{... | collective-permute-start | bytes 983048 | tf_op jit(solution)/shard_map/ppermute | solution.py:811
  47.8 13.1 %collective-permute-start.3 = (f32[20,8,512]{2,1,0:T(8,128)}, f32[20,8,512]{2,1,0:T(8,128)}, u32[]{:S(2)}, u32[]{:S(2)}) collective-permute-start(f32[20,8,512]{2,1,0:T(8,128)} %get-tuple-element.29), channel_id=1, source_target_pairs={{1,0},{2,1},{3,2},{5,4},{6,5},{7,6},{9,8},{10,9},{11,10},{13,12},{... | collective-permute-start | bytes 983048 | tf_op jit(solution)/shard_map/ppermute | solution.py:812
  49.1 0.7 copy-start
  49.8 0.7 copy-start.5
  52.2 34.6 %all-to-all-start.2 = ((f32[32,16,128]{2,1,0:T(8,128)}), f32[32,16,128]{2,1,0:T(8,128)}, u32[]{:S(2)}, u32[]{:S(2)}) async-start(f32[32,16,128]{2,1,0:T(8,128)} %middle.1), calls=%async_computation.2 | async-start | bytes 524288 | tf_op jit(solution)/shard_map/all_to_all | solution.py:800
  81.9 16.8 %collective-permute-start.4 = (f32[2,72,512]{2,1,0:T(8,128)}, f32[2,72,512]{2,1,0:T(8,128)S(1)}, u32[]{:S(2)}, u32[]{:S(2)}) collective-permute-start(f32[2,72,512]{2,1,0:T(8,128)} %get-tuple-element.34), channel_id=1, source_target_pairs={{0,4},{4,8},{8,12},{12,16},{16,20},{20,24},{24,28},{1,5},{5,9},{9,... | collective-permute-start | bytes 884744 | tf_op jit(solution)/shard_map/ppermute | solution.py:811
  85.5 13.2 %collective-permute-start.5 = (f32[2,72,512]{2,1,0:T(8,128)}, f32[2,72,512]{2,1,0:T(8,128)S(1)}, u32[]{:S(2)}, u32[]{:S(2)}) collective-permute-start(f32[2,72,512]{2,1,0:T(8,128)} %get-tuple-element.33), channel_id=1, source_target_pairs={{4,0},{8,4},{12,8},{16,12},{20,16},{24,20},{28,24},{5,1},{9,5},{13... | collective-permute-start | bytes 884744 | tf_op jit(solution)/shard_map/ppermute | solution.py:812
  86.8 0.7 copy-start.3
  87.5 28.0 %copy-start.1 = (f32[16,128]{1,0:T(8,128)S(1)}, f32[16,128]{1,0:T(8,128)}, u32[]{:S(2)}) copy-start(f32[16,128]{1,0:T(8,128)} %mirror_ref.5) | copy-start | bytes 24580
  87.5 28.0 %copy-start.4 = (s32[16,128]{1,0:T(8,128)S(1)}, s32[16,128]{1,0:T(8,128)}, u32[]{:S(2)}) copy-start(s32[16,128]{1,0:T(8,128)} %site_ref.3) | copy-start | bytes 24580
  87.5 28.0 %copy-start.6 = (f32[16,128]{1,0:T(8,128)S(1)}, f32[16,128]{1,0:T(8,128)}, u32[]{:S(2)}) copy-start(f32[16,128]{1,0:T(8,128)} %get-tuple-element.32.emitted_ref) | copy-start | bytes 24580
  98.7 18.0 %copy-start.7 = (f32[2,72,512]{2,1,0:T(8,128)}, f32[2,72,512]{2,1,0:T(8,128)S(1)}, u32[]{:S(2)}) copy-start(f32[2,72,512]{2,1,0:T(8,128)S(1)} %collective-permute-done.4.low_ref) | copy-start | bytes 884740
  98.7 18.0 %copy-start.8 = (f32[2,72,512]{2,1,0:T(8,128)}, f32[2,72,512]{2,1,0:T(8,128)S(1)}, u32[]{:S(2)}) copy-start(f32[2,72,512]{2,1,0:T(8,128)S(1)} %collective-permute-done.5.high_ref) | copy-start | bytes 884740
  116.7 22.7 %all-to-all-start.4 = ((f32[32,8,128]{2,1,0:T(8,128)}), f32[32,8,128]{2,1,0:T(8,128)}, u32[]{:S(2)}, u32[]{:S(2)}) async-start(f32[32,8,128]{2,1,0:T(8,128)} %get-tuple-element.38), calls=%async_computation.4 | async-start | bytes 262144 | tf_op jit(solution)/shard_map/all_to_all | solution.py:800

commit v6 on v4

--- a/solution.py
+++ b/solution.py
@@ -15,6 +15,7 @@
 ROWS = STEPS
 LANES = 128
 CHUNK = 16
+LAG = 12
 
 step_size = 0.07
 
@@ -38,6 +39,26 @@
         x = x - part.astype(jnp.float32)
     out.append(x.astype(jnp.bfloat16))
     return out
+
+
+class Lagging:
+    def __init__(self, depth):
+        self.depth = depth
+        self.waiting = []
+
+    def add(self, store):
+        self.waiting.append(store)
+        if len(self.waiting) > self.depth:
+            self.waiting.pop(0)()
+
+    def finish(self):
+        for store in self.waiting:
+            store()
+        self.waiting = []
+
+
+def put(ref, index, value):
+    return lambda: ref.__setitem__(index, value)
 
 
 def emit_kernel(temp_ref, site_ref, mirror_ref, emitted_ref, copies_ref):
@@ -118,6 +139,7 @@
     @pl.loop(0, chunks)
     def _(c):
         chunk_copy(c).wait()
+        stores = Lagging(4 * CHUNK)
         for u in range(0, CHUNK, 2):
             t = c * CHUNK + u
             high_a, low_a = parts_of(held[t], 2)
@@ -149,8 +171,10 @@
                 preferred_element_type=jnp.float32,
             )
             for side, result in ((0, first), (1, second)):
-                terms[side, pl.ds(t, 1), :] = result[0:1, :BLK] + result[1:2, :BLK]
-                terms[side, pl.ds(t + 1, 1), :] = result[8:9, BLK:] + result[9:10, BLK:]
+                for v, (top_row, cols) in enumerate(((0, slice(0, BLK)), (8, slice(BLK, 2 * BLK)))):
+                    row = result[top_row : top_row + 1, cols] + result[top_row + 1 : top_row + 2, cols]
+                    stores.add(put(terms, (side, pl.ds(t + v, 1)), row))
+        stores.finish()
 
     used = lax.broadcasted_iota(jnp.int32, (slots, BLK), 0) < live
     used_lane = lax.broadcasted_iota(jnp.int32, (1, slots), 1) < live
@@ -184,7 +208,7 @@
             pltpu.VMEM((2, slots, BLK), jnp.float32),
             pltpu.SemaphoreType.DMA((slots // CHUNK,)),
         ],
-        compiler_params=params(64),
+        compiler_params=params(50),
         cost_estimate=cost(slots * BLK * BLK * 32, slots * BLK * BLK * 4),
         name="tiles",
     )(live, couples, couples, whole, tiles)
@@ -210,7 +234,7 @@
     return pl.pallas_call(
         middle_kernel,
         out_shape=jax.ShapeDtypeStruct(parts.shape, jnp.float32),
-        compiler_params=params(64),
+        compiler_params=params(32),
         cost_estimate=cost(100_000, 600_000),
         name="middle",
     )(parts, emitted, mirror)
@@ -245,8 +269,7 @@
         source_ref[d] = source
 
 
-def last(parts, emitted, mirror, site, cells):
-    count = parts.shape[0]
+def last(parts, emitted, mirror, site, cells, count):
     weight = cells / (mirror.shape[0] * BLK * 1.0)
     return pl.pallas_call(
         functools.partial(last_kernel, step_size * weight),
@@ -254,7 +277,7 @@
             jax.ShapeDtypeStruct(mirror.shape, jnp.float32),
             jax.ShapeDtypeStruct((count, cells // LANES, LANES), jnp.float32),
         ),
-        compiler_params=params(64),
+        compiler_params=params(32),
         cost_estimate=cost(10_000_000, 600_000),
         name="last",
     )(parts, emitted, mirror, site)
@@ -304,14 +327,14 @@
 def pack_y_kernel(nx, ny, t0, k0, t7, k7, low_ref, high_ref, down_ref, up_ref):
     upper = lax.broadcasted_iota(jnp.int32, down_ref.shape[1:], 0) < ROWS
 
-    def put(x, t_first, k_first, t_final, k_final):
+    def edge(x, t_first, k_first, t_final, k_final):
         down_ref[x] = jnp.where(upper, t_first, pltpu.roll(k_first, ROWS, 0))
         up_ref[x] = jnp.where(upper, pltpu.roll(t_final, ROWS, 0), k_final)
 
     for side, base in ((low_ref, 0), (high_ref, DEPTH + nx)):
         for p in range(DEPTH):
             t_at, k_at = p * ny, (DEPTH + p) * ny
-            put(
+            edge(
                 base + p,
                 side[t_at : t_at + 8, :],
                 side[k_at : k_at + 8, :],
@@ -319,7 +342,7 @@
                 side[k_at + ny - 8 : k_at + ny, :],
             )
     for x in range(nx):
-        put(DEPTH + x, t0[x], k0[x], t7[x], k7[x])
+        edge(DEPTH + x, t0[x], k0[x], t7[x], k7[x])
 
 
 def pack_y(temp, cond, low, high):
@@ -355,26 +378,6 @@
     return [slice(j * LANES, (j + 1) * LANES) for j in range(nz // LANES)]
 
 
-class Lagging:
-    def __init__(self, depth):
-        self.depth = depth
-        self.waiting = []
-
-    def add(self, store):
-        self.waiting.append(store)
-        if len(self.waiting) > self.depth:
-            self.waiting.pop(0)()
-
-    def finish(self):
-        for store in self.waiting:
-            store()
-        self.waiting = []
-
-
-def put(ref, index, value):
-    return lambda: ref.__setitem__(index, value)
-
-
 def prepare(cond, gx, gy, gz, gb):
     tall, wide, nz = cond.shape
     tiles = wide // 8
@@ -384,7 +387,7 @@
     @pl.loop(0, tall)
     def _(x):
         after = jnp.minimum(x + 1, tall - 1)
-        stores = Lagging(16)
+        stores = Lagging(LAG)
         for z in lane_tiles(nz):
             last = z.stop == nz
             for t in range(tiles):
@@ -422,7 +425,7 @@
     @pl.loop(begin, end)
     def _(x):
         here, across_y = {}, {}
-        stores = Lagging(16)
+        stores = Lagging(LAG)
         spans = lane_tiles(nz)
         count = len(spans)
 
@@ -560,7 +563,7 @@
 
     @pl.loop(0, tall)
     def _(x):
-        stores = Lagging(16)
+        stores = Lagging(LAG)
         for t in range(tiles):
             rows = pl.ds(t, 8, stride=tiles)
             for j, z in enumerate(spans):
@@ -682,18 +685,24 @@
     )(temp, low, high, cond)
 
 
-def source_kernel(ny, near_ref, flag_ref, all_ref, thin_ref, base_ref, out_ref):
+def source_kernel(ny, all_ref, thin_ref, base_ref, out_ref):
     tall = thin_ref.shape[0]
     nx = tall - 2 * HALO
     sheets = all_ref.shape[1]
     sub = lax.broadcasted_iota(jnp.int32, (8, LANES), 0)
     y_lane = lax.broadcasted_iota(jnp.int32, (8, LANES), 1)
 
-    def sheet(k):
-        return all_ref[near_ref[k]] * flag_ref[k].astype(jnp.float32)
-
-    def rows_of(slab):
-        low, own, high = (sheet(3 * slab + k) for k in range(3))
+    slabs, pairs = lax.axis_size("slab"), lax.axis_size("pair")
+
+    def sheet(down, across):
+        slab = lax.axis_index("slab") + down
+        pair = lax.axis_index("pair") + across
+        inside = (slab >= 0) & (slab < slabs) & (pair >= 0) & (pair < pairs)
+        found = all_ref[jnp.where(inside, slab * pairs + pair, 0)]
+        return jnp.where(inside, found, 0.0)
+
+    def rows_of(down):
+        low, own, high = (sheet(down, across) for across in (-1, 0, 1))
         out = []
         for half in range(2):
             if half == 0:
@@ -713,7 +722,7 @@
             )
         return out
 
-    lines = [rows_of(s) for s in range(3)]
+    lines = [rows_of(down) for down in (-1, 0, 1)]
     source = []
     for x in range(-HALO, nx + HALO):
         which, local = (x + nx) // nx, x % nx
@@ -758,31 +767,41 @@
         out_ref[x] = base_ref[x] + jnp.where(lane < STEPS, piece, 0.0)
 
 
-def add_source(near, flag, everything, thin, base):
+def add_source(everything, thin, base):
     nx, ny, nz = base.shape
-    smem = pl.BlockSpec(memory_space=pltpu.SMEM)
     block = pl.BlockSpec((nx, ny, LANES), lambda i: (0, 0, 0))
     return pl.pallas_call(
         functools.partial(source_kernel, ny),
         grid=(1,),
         out_shape=jax.ShapeDtypeStruct(base.shape, jnp.float32),
         in_specs=[
-            smem,
-            smem,
             pl.BlockSpec(everything.shape, lambda i: (0, 0, 0)),
             pl.BlockSpec(thin.shape, lambda i: (0, 0, 0)),
             block,
         ],
         out_specs=block,
-        input_output_aliases={4: 0},
+        input_output_aliases={2: 0},
         compiler_params=params(64),
         cost_estimate=cost(1_000_000, 2 * nx * ny * LANES * 4),
         name="add_source",
-    )(near, flag, everything, thin, base)
-
-
-def exchange(copies):
-    return lax.all_to_all(copies, ("slab", "pair"), split_axis=0, concat_axis=0, tiled=True)
+    )(everything, thin, base)
+
+
+def swap(rows, axis):
+    return lax.all_to_all(rows, axis, split_axis=0, concat_axis=0, tiled=True)
+
+
+def gather(copies):
+    column = swap(copies, "slab")
+    pairs = lax.axis_size("pair")
+    everyone = jnp.broadcast_to(column[None], (pairs,) + column.shape)
+    return swap(everyone, "pair")
+
+
+def reduce_pairs(term):
+    pairs, slabs = lax.axis_size("pair"), lax.axis_size("slab")
+    parts = swap(term, "pair").reshape(pairs, slabs, -1, BLK)
+    return swap(parts.sum(axis=0), "slab")
 
 
 def together(*arrays):
@@ -812,47 +831,42 @@
     count = slabs * pairs
     blocks = mirror_fraction.shape[0]
     couples = tile_block_couples.T
+    owner, local = couples // blocks, couples % blocks
+    couples = ((owner % pairs) * slabs + owner // pairs) * blocks + local
 
     temp, cond = initial_warmth, heat_passing_coefficient
-    emitted, copies = emit(temp, element_facing_site, mirror_fraction, count)
+    emitted, copies = emit(temp, element_facing_site, mirror_fraction, slabs)
     temp, copies = together(temp, copies)
 
     def sweep_terms(whole):
         whole = whole.reshape(count * blocks, BLK)
         term = tile_terms(whole, couples, active_slot_count, view_factor_blocks)
-        return term.reshape(count, blocks, BLK)
-
-    whole = exchange(copies)
+        return term.reshape(pairs, slabs * blocks, BLK)
+
+    whole = gather(copies)
     send_low, send_high = pack_x(temp, cond)
-    whole, send_low, send_high = together(whole, send_low, send_high)
     low, high = both_ways(send_low, send_high, "slab")
-    parts = exchange(sweep_terms(whole))
+    whole = together(whole, send_low, send_high)[0]
+    parts = reduce_pairs(sweep_terms(whole))
     send_down, send_up = pack_y(temp, cond, low, high)
-    parts, send_down, send_up = together(parts, send_down, send_up)
+    parts = together(parts, send_down, send_up)[0]
     below, above = both_ways(send_down, send_up, "pair")
-    whole = exchange(middle(parts, emitted, mirror_fraction))
+    whole = gather(middle(parts, emitted, mirror_fraction))
     middle_temp, send_low, send_high, strided_cond, thin = first_round(
         temp, cond, low, high, below, above
     )
-    whole, send_low, send_high = together(whole, send_low, send_high)
     low, high = both_ways(send_low, send_high, "slab")
-    parts = exchange(sweep_terms(whole))
-    parts, low, high = together(parts, low, high)
-    radiosity, source = last(parts, emitted, mirror_fraction, element_facing_site, nx * ny)
-    everything = exchange(source)
+    whole = together(whole, send_low, send_high)[0]
+    term, low, high = together(sweep_terms(whole), low, high)
+    parts = reduce_pairs(term)
     base = second_round(middle_temp, low, high, strided_cond, temp.shape)
-
-    slab, pair = lax.axis_index("slab"), lax.axis_index("pair")
-    near, flag = [], []
-    for ds in (-1, 0, 1):
-        for dp in (-1, 0, 1):
-            s, p = slab + ds, pair + dp
-            inside = (s >= 0) & (s < slabs) & (p >= 0) & (p < pairs)
-            near.append(jnp.where(inside, s * pairs + p, 0))
-            flag.append(inside)
-    near = jnp.stack(near).astype(jnp.int32)
-    flag = jnp.stack(flag).astype(jnp.int32)
-    warmed_liner = add_source(near, flag, everything, thin, base)
+    parts = together(parts, base)[0]
+    radiosity, source = last(parts, emitted, mirror_fraction, element_facing_site, nx * ny, count)
+    everything = lax.all_to_all(
+        source, ("slab", "pair"), split_axis=0, concat_axis=0, tiled=True
+    )
+
+    warmed_liner = add_source(everything, thin, base)
     return (radiosity, warmed_liner)
 
 

time: 144 us -> 175 us (1.22)
  blocking collectives: 0 us -> 47.8 us
  waiting for transfers between devices: 31.7 us -> 20.3 us
  starting transfers between devices: 52.8 us -> 46.4 us
  local copies, waits for them, and re-layouts: 0.7 us -> 6.45 us
  Pallas kernels: 55.4 us -> 50.1 us
    all_to_all x0 -> x4, blocking collectives: none -> 47.8 us  [the longest x3 34.6 us: swap(): return lax.all_to_all(rows, axis, split_axis=0, concat_axis=0, tiled=True)]
    ppermute x3, waiting for transfers between devices: 20 us -> 0.01 us  [both_ways(): from_low = lax.ppermute(high, axis, forward)]
    all_to_all x5, waiting for transfers between devices: 8.69 us -> 20.3 us  [swap(): return lax.all_to_all(rows, axis, split_axis=0, concat_axis=0, tiled=True)]
    all_to_all x5, starting transfers between devices: 38.2 us -> 28.5 us  [swap(): return lax.all_to_all(rows, axis, split_axis=0, concat_axis=0, tiled=True)]
    unnamed x0 -> x18, local copies, waits for them, and re-layouts: none -> 4.88 us
    pallas_call x2, Pallas kernels: 13.3 us -> 9.59 us  [tile_terms(): pl.pallas_call(tiles_kernel, out_shape=jax.ShapeDtypeStruct(whole.shape,...]
    ppermute x3, starting transfers between devices: 10.8 us -> 14.1 us  [both_ways(): from_low = lax.ppermute(high, axis, forward)]
    ppermute x3, waiting for transfers between devices: 2.96 us -> 0.01 us  [both_ways(): from_high = lax.ppermute(low, axis, backward)]
  transfers between devices with their start and end apart: 11 -> 11, of which waited for: 5 -> 2; matrix products, arithmetic and copies ran while one was open for 1% -> 2% of each run, Pallas kernels for 28% -> 24%
where the time goes in v6:
time: 175 us
  Pallas kernels  50.1 us (29%)
  blocking collectives  47.8 us (27%)
  starting transfers between devices  46.4 us (27%)
  waiting for transfers between devices  20.3 us (12%)
  local copies, waits for them, and re-layouts  6.45 us (4%)
  other arithmetic  2.33 us (1%)
    all_to_all x3, blocking collectives, swap(): return lax.all_to_all(rows, axis, split_axis=0, concat_axis=0, tiled=True)  34.6 us
    all_to_all x5, starting transfers between devices, swap(): return lax.all_to_all(rows, axis, split_axis=0, concat_axis=0, tiled=True)  28.5 us
    all_to_all x5, waiting for transfers between devices, swap(): return lax.all_to_all(rows, axis, split_axis=0, concat_axis=0, tiled=True)  20.3 us
    pallas_call x1, Pallas kernels, first_round(): pl.pallas_call(first_round_kernel, out_shape=(jax.ShapeDtypeStruct((nx, w...  16.3 us
    ppermute x3, starting transfers between devices, both_ways(): from_low = lax.ppermute(high, axis, forward)  14.1 us
    all_to_all x1, blocking collectives, shards(): lax.all_to_all(source, ('slab', 'pair'), split_axis=0, concat_axis=0, til...  13.2 us
    pallas_call x1, Pallas kernels, second_round(): pl.pallas_call(second_round_kernel, out_shape=jax.ShapeDtypeStruct(shape,...  12.4 us
    pallas_call x2, Pallas kernels, tile_terms(): pl.pallas_call(tiles_kernel, out_shape=jax.ShapeDtypeStruct(whole.shape,...  9.59 us
  transfers between devices with their start and end apart: 11, of which 2 were waited for; matrix products, arithmetic and copies ran while one was open for 2% of the time, Pallas kernels for 24%

profile of v6, /device:TPU:0, one launch (start us, length us, event | category | flops | bytes accessed | tf_op | source)
XLA Modules:
  0.0 174.9 jit_solution(18074145228081781566)
XLA Ops:
  0.6 2.1 %emit.1 = (f32[16,128]{1,0:T(8,128)}, f32[8,16,128]{2,1,0:T(8,128)}) custom-call(f32[16,64,512]{2,1,0:T(8,128)} %t_ref, s32[16,128]{1,0:T(8,128)} %site_ref.3, f32[16,128]{1,0:T(8,128)} %mirror_ref.5), custom_call_target="tpu_custom_call" | custom-call | flops 10000 | bytes 900000 | tf_op jit(solution)/shard_map/emit/pallas_call | solution.py:97
  2.7 2.3 %pack_x.1 = (f32[272,512]{1,0:T(8,128)}, f32[272,512]{1,0:T(8,128)}) custom-call(f32[16,64,512]{2,1,0:T(8,128)} %t_ref, f32[16,64,512]{2,1,0:T(8,128)} %k_ref.1, f32[16,64,512]{2,1,0:T(8,128)} %k_ref.1, f32[16,64,512]{2,1,0:T(8,128)} %t_ref, f32[16,64,512]{2,1,0:T(8,128)} %k_ref.1, f32[16,64,512]{2,1,0:T(8,128)} %k_ref.1), custom_call_target="tpu_custom_call" | custom-call | bytes 2228224 | tf_op jit(solution)/shard_map/pack_x/pallas_call | solution.py:315
  5.0 5.7 %collective-permute-start = (f32[272,512]{1,0:T(8,128)}, f32[272,512]{1,0:T(8,128)}, u32[]{:S(2)}, u32[]{:S(2)}) collective-permute-start(f32[272,512]{1,0:T(8,128)} %get-tuple-element.28), channel_id=1, source_target_pairs={{0,4},{4,8},{8,12},{12,16},{16,20},{20,24},{24,28},{1,5},{5,9},{9,... | collective-permute-start | bytes 1671176 | tf_op jit(solution)/shard_map/ppermute | solution.py:815
  10.7 1.3 collective-permute-start.1
  11.9 7.0 %all-to-all-start = ((f32[8,16,128]{2,1,0:T(8,128)}), f32[8,16,128]{2,1,0:T(8,128)S(1)}, u32[]{:S(2)}, u32[]{:S(2)}) async-start(f32[8,16,128]{2,1,0:T(8,128)} %get-tuple-element.25), calls=%async_computation | async-start | bytes 131072 | tf_op jit(solution)/shard_map/all_to_all | solution.py:791
  19.6 15.0 %all-to-all-done = f32[8,16,128]{2,1,0:T(8,128)S(1)} async-done(((f32[8,16,128]{2,1,0:T(8,128)}), f32[8,16,128]{2,1,0:T(8,128)S(1)}, u32[]{:S(2)}, u32[]{:S(2)}) %all-to-all-start) | async-done | bytes 65568 | tf_op jit(solution)/shard_map/all_to_all | solution.py:791
  34.6 0.7 broadcast_in_dim.4
  35.3 3.4 %all-to-all-start.1 = ((f32[4,8,16,128]{3,2,1,0:T(8,128)}), f32[4,8,16,128]{3,2,1,0:T(8,128)S(1)}, u32[]{:S(2)}, u32[]{:S(2)}) async-start(f32[4,8,16,128]{3,2,1,0:T(8,128)} %broadcast_in_dim.4), calls=%async_computation.1 | async-start | bytes 524288 | tf_op jit(solution)/shard_map/all_to_all | solution.py:791
  38.7 0.7 fusion.2.pairs_ref.lanes_ref
  39.4 0.0 copy-start.2
  39.4 5.3 %all-to-all-done.1 = f32[4,8,16,128]{3,2,1,0:T(8,128)S(1)} async-done(((f32[4,8,16,128]{3,2,1,0:T(8,128)}), f32[4,8,16,128]{3,2,1,0:T(8,128)S(1)}, u32[]{:S(2)}, u32[]{:S(2)}) %all-to-all-start.1) | async-done | bytes 262176 | tf_op jit(solution)/shard_map/all_to_all | solution.py:791
  44.7 5.1 %tiles.2 = f32[512,128]{1,0:T(8,128)} custom-call(s32[1]{0:T(128)S(6)} %copy.11.live_ref, s32[2,256]{1,0:T(2,128)S(1)} %fusion.2.pairs_ref.lanes_ref, s32[2,256]{1,0:T(2,128)S(1)} %fusion.2.pairs_ref.lanes_ref, f32[512,128]{1,0:T(8,128)S(1)} %bitcast.21, f32[256,128,128]{2,1,0:T(8,128)} %tiles_ref.3), custom_call_target="tpu_custom_call" | custom-call | flops 134217728 | bytes 16777216 | tf_op jit(solution)/shard_map/tiles/pallas_call | solution.py:201
  49.9 0.0 copy-done.2
  49.9 4.1 %all-to-all-start.2 = ((f32[4,128,128]{2,1,0:T(8,128)}), f32[4,128,128]{2,1,0:T(8,128)}, u32[]{:S(2)}, u32[]{:S(2)}) async-start(f32[4,128,128]{2,1,0:T(8,128)} %bitcast.2), calls=%async_computation.2 | async-start | bytes 524288 | tf_op jit(solution)/shard_map/all_to_all | solution.py:791
  53.9 0.0 collective-permute-done.low_ref
  54.0 0.0 collective-permute-done.1.high_ref
  54.0 2.5 %pack_y.1 = (f32[20,8,512]{2,1,0:T(8,128)}, f32[20,8,512]{2,1,0:T(8,128)}) custom-call(f32[16,64,512]{2,1,0:T(8,128)} %t_ref, f32[16,64,512]{2,1,0:T(8,128)} %k_ref.1, f32[16,64,512]{2,1,0:T(8,128)} %t_ref, f32[16,64,512]{2,1,0:T(8,128)} %k_ref.1, f32[272,512]{1,0:T(8,128)} %collective-permute-done.low_ref, f32[272,512]{1,0:T(8,128)} %collective-permute-done.1.high_ref), custom_call_target="tpu_custom_call" | custom-call | bytes 1310720 | tf_op jit(solution)/shard_map/pack_y/pallas_call | solution.py:356
  56.4 4.4 %collective-permute-start.2 = (f32[20,8,512]{2,1,0:T(8,128)}, f32[20,8,512]{2,1,0:T(8,128)}, u32[]{:S(2)}, u32[]{:S(2)}) collective-permute-start(f32[20,8,512]{2,1,0:T(8,128)} %get-tuple-element.31), channel_id=1, source_target_pairs={{0,1},{1,2},{2,3},{4,5},{5,6},{6,7},{8,9},{9,10},{10,11},{12,13},{... | collective-permute-start | bytes 983048 | tf_op jit(solution)/shard_map/ppermute | solution.py:815
  60.8 1.3 collective-permute-start.3
  62.1 0.0 all-to-all-done.2
  62.1 1.0 reduce_sum.22
  63.1 15.7 %all_to_all.45.parts_ref = f32[8,16,128]{2,1,0:T(8,128)S(1)} all-to-all(f32[8,16,128]{2,1,0:T(8,128)S(1)} %bitcast.23), channel_id=1, replica_groups=mesh['slab'=8,'pair'=4] {'slab'}, dimensions={0} | all-to-all | bytes 131072 | tf_op jit(solution)/shard_map/all_to_all | solution.py:791
  78.8 0.0 copy-start
  78.8 0.7 copy-done
  79.5 0.0 copy-start.5
  79.5 0.7 copy-done.5
  80.2 0.6 middle.1
  80.9 4.0 %all-to-all-start.4 = ((f32[8,16,128]{2,1,0:T(8,128)}), f32[8,16,128]{2,1,0:T(8,128)}, u32[]{:S(2)}, u32[]{:S(2)}) async-start(f32[8,16,128]{2,1,0:T(8,128)} %middle.1), calls=%async_computation.4 | async-start | bytes 131072 | tf_op jit(solution)/shard_map/all_to_all | solution.py:791
  84.9 0.0 collective-permute-done.2.below_ref
  84.9 0.0 collective-permute-done.3.above_ref
  84.9 16.3 %first_round.1 = (f32[16,72,512]{2,1,0:T(8,128)}, f32[2,72,512]{2,1,0:T(8,128)}, f32[2,72,512]{2,1,0:T(8,128)}, f32[20,72,512]{2,1,0:T(8,128)}, f32[24,8,128]{2,1,0:T(8,128)}) custom-call(f32[16,64,512]{2,1,0:T(8,128)} %t_ref, f32[16,64,512]{2,1,0:T(8,128)} %k_ref.1, f32[272,512]{1,0:T(8,128)} %collective-permute-done.low_ref, ...), custom_call_target="tpu_custom_call" | custom-call | flops 73728000 | bytes 25165824 | tf_op jit(solution)/shard_map/first_round/pallas_call | solution.py:618
  101.2 4.0 %collective-permute-start.4 = (f32[2,72,512]{2,1,0:T(8,128)}, f32[2,72,512]{2,1,0:T(8,128)S(1)}, u32[]{:S(2)}, u32[]{:S(2)}) collective-permute-start(f32[2,72,512]{2,1,0:T(8,128)} %get-tuple-element.35), channel_id=1, source_target_pairs={{0,4},{4,8},{8,12},{12,16},{16,20},{20,24},{24,28},{1,5},{5,9},{9,... | collective-permute-start | bytes 884744 | tf_op jit(solution)/shard_map/ppermute | solution.py:815
  105.1 1.3 collective-permute-start.5
  106.4 0.0 all-to-all-done.4
  106.4 0.9 broadcast_in_dim.5
  107.3 10.1 %all_to_all.46 = f32[4,8,16,128]{3,2,1,0:T(8,128)S(1)} all-to-all(f32[4,8,16,128]{3,2,1,0:T(8,128)S(1)} %broadcast_in_dim.5), channel_id=1, replica_groups=mesh['slab'=8,'pair'=4] {'pair'}, dimensions={0} | all-to-all | bytes 524288 | tf_op jit(solution)/shard_map/all_to_all | solution.py:791
  117.4 0.0 copy-start.3
  117.4 0.7 copy-done.3
  118.1 4.4 %tiles.3 = f32[512,128]{1,0:T(8,128)S(1)} custom-call(s32[1]{0:T(128)S(6)} %copy.11.live_ref, s32[2,256]{1,0:T(2,128)S(1)} %copy-done.3, s32[2,256]{1,0:T(2,128)S(1)} %copy-done.3, f32[512,128]{1,0:T(8,128)S(1)} %bitcast.22, f32[256,128,128]{2,1,0:T(8,128)} %tiles_ref.3), custom_call_target="tpu_custom_call" | custom-call | flops 134217728 | bytes 16777216 | tf_op jit(solution)/shard_map/tiles/pallas_call | solution.py:201
  122.6 0.0 collective-permute-done.4.low_ref
  122.6 0.0 copy-start.7
  122.6 0.0 collective-permute-done.5.high_ref
  122.6 0.7 copy-done.7
  123.3 0.0 copy-start.8
  123.3 8.7 %all_to_all.47 = f32[4,128,128]{2,1,0:T(8,128)S(1)} all-to-all(f32[4,128,128]{2,1,0:T(8,128)S(1)} %bitcast.20), channel_id=1, replica_groups=mesh['slab'=8,'pair'=4] {'pair'}, dimensions={0} | all-to-all | bytes 524288 | tf_op jit(solution)/shard_map/all_to_all | solution.py:791
  132.0 0.7 reduce_sum.24
  132.7 0.0 copy-done.8
  132.7 10.1 %all-to-all-start.7 = ((f32[8,16,128]{2,1,0:T(8,128)}), f32[8,16,128]{2,1,0:T(8,128)}, u32[]{:S(2)}, u32[]{:S(2)}) async-start(f32[8,16,128]{2,1,0:T(8,128)} %bitcast.6), calls=%async_computation.7 | async-start | bytes 131072 | tf_op jit(solution)/shard_map/all_to_all | solution.py:791
  142.8 12.4 %second_round.1.base_ref = f32[16,64,512]{2,1,0:T(8,128)} custom-call(f32[16,72,512]{2,1,0:T(8,128)} %get-tuple-element.38.t_ref, f32[2,72,512]{2,1,0:T(8,128)} %copy-done.7, f32[2,72,512]{2,1,0:T(8,128)} %copy-done.8, f32[20,72,512]{2,1,0:T(8,128)} %get-tuple-element.41.k_ref), custom_call_target="tpu_custom_call" | custom-call | flops 44236800 | bytes 18874368 | tf_op jit(solution)/shard_map/second_round/pallas_call | solution.py:672
  155.2 0.0 all-to-all-done.7.parts_ref
  155.2 0.0 copy-start.1
  155.2 0.7 copy-done.1
  155.9 0.0 copy-start.4
  155.9 0.7 copy-done.4
  156.6 0.0 copy-start.6
  156.6 0.7 copy-done.6
  157.3 1.8 %last.1 = (f32[16,128]{1,0:T(8,128)}, f32[32,8,128]{2,1,0:T(8,128)S(1)}) custom-call(f32[8,16,128]{2,1,0:T(8,128)} %all-to-all-done.7.parts_ref, f32[16,128]{1,0:T(8,128)S(1)} %copy-done.6, f32[16,128]{1,0:T(8,128)S(1)} %copy-done.1, s32[16,128]{1,0:T(8,128)S(1)} %copy-done.4), custom_call_target="tpu_custom_call" | custom-call | flops 10000000 | bytes 600000 | tf_op jit(solution)/shard_map/last/pallas_call | solution.py:274
  159.1 13.2 %all_to_all.48.all_ref = f32[32,8,128]{2,1,0:T(8,128)} all-to-all(f32[32,8,128]{2,1,0:T(8,128)S(1)} %get-tuple-element.44), channel_id=1, replica_groups=mesh['slab'=8,'pair'=4] {'slab','pair'}, dimensions={0} | all-to-all | bytes 262144 | tf_op jit(solution)/shard_map/all_to_all | solution.py:865
  172.3 2.6 %add_source.1 = f32[16,64,512]{2,1,0:T(8,128)} custom-call(f32[32,8,128]{2,1,0:T(8,128)} %all_to_all.48.all_ref, f32[24,8,128]{2,1,0:T(8,128)} %get-tuple-element.45.thin_ref, f32[16,64,512]{2,1,0:T(8,128)} %second_round.1.base_ref), custom_call_target="tpu_custom_call", output_to_operand_aliasing={{}: (2, {})} | custom-call | flops 1000000 | bytes 1048576 | tf_op jit(solution)/shard_map/add_source/pallas_call | solution.py:773
Async XLA Ops:
  5.0 49.0 %collective-permute-start = (f32[272,512]{1,0:T(8,128)}, f32[272,512]{1,0:T(8,128)}, u32[]{:S(2)}, u32[]{:S(2)}) collective-permute-start(f32[272,512]{1,0:T(8,128)} %get-tuple-element.28), channel_id=1, source_target_pairs={{0,4},{4,8},{8,12},{12,16},{16,20},{20,24},{24,28},{1,5},{5,9},{9,... | collective-permute-start | bytes 1671176 | tf_op jit(solution)/shard_map/ppermute | solution.py:815
  10.7 43.3 %collective-permute-start.1 = (f32[272,512]{1,0:T(8,128)}, f32[272,512]{1,0:T(8,128)}, u32[]{:S(2)}, u32[]{:S(2)}) collective-permute-start(f32[272,512]{1,0:T(8,128)} %get-tuple-element.27), channel_id=1, source_target_pairs={{4,0},{8,4},{12,8},{16,12},{20,16},{24,20},{28,24},{5,1},{9,5},{13... | collective-permute-start | bytes 1671176 | tf_op jit(solution)/shard_map/ppermute | solution.py:816
  11.9 22.6 %all-to-all-start = ((f32[8,16,128]{2,1,0:T(8,128)}), f32[8,16,128]{2,1,0:T(8,128)S(1)}, u32[]{:S(2)}, u32[]{:S(2)}) async-start(f32[8,16,128]{2,1,0:T(8,128)} %get-tuple-element.25), calls=%async_computation | async-start | bytes 131072 | tf_op jit(solution)/shard_map/all_to_all | solution.py:791
  35.3 9.4 %all-to-all-start.1 = ((f32[4,8,16,128]{3,2,1,0:T(8,128)}), f32[4,8,16,128]{3,2,1,0:T(8,128)S(1)}, u32[]{:S(2)}, u32[]{:S(2)}) async-start(f32[4,8,16,128]{3,2,1,0:T(8,128)} %broadcast_in_dim.4), calls=%async_computation.1 | async-start | bytes 524288 | tf_op jit(solution)/shard_map/all_to_all | solution.py:791
  39.4 10.5 %copy-start.2 = (s32[2,256]{1,0:T(2,128)}, s32[2,256]{1,0:T(2,128)S(1)}, u32[]{:S(2)}) copy-start(s32[2,256]{1,0:T(2,128)S(1)} %fusion.2.pairs_ref.lanes_ref) | copy-start | bytes 6148
  49.9 12.3 %all-to-all-start.2 = ((f32[4,128,128]{2,1,0:T(8,128)}), f32[4,128,128]{2,1,0:T(8,128)}, u32[]{:S(2)}, u32[]{:S(2)}) async-start(f32[4,128,128]{2,1,0:T(8,128)} %bitcast.2), calls=%async_computation.2 | async-start | bytes 524288 | tf_op jit(solution)/shard_map/all_to_all | solution.py:791
  56.4 28.4 %collective-permute-start.2 = (f32[20,8,512]{2,1,0:T(8,128)}, f32[20,8,512]{2,1,0:T(8,128)}, u32[]{:S(2)}, u32[]{:S(2)}) collective-permute-start(f32[20,8,512]{2,1,0:T(8,128)} %get-tuple-element.31), channel_id=1, source_target_pairs={{0,1},{1,2},{2,3},{4,5},{5,6},{6,7},{8,9},{9,10},{10,11},{12,13},{... | collective-permute-start | bytes 983048 | tf_op jit(solution)/shard_map/ppermute | solution.py:815
  60.8 24.0 %collective-permute-start.3 = (f32[20,8,512]{2,1,0:T(8,128)}, f32[20,8,512]{2,1,0:T(8,128)}, u32[]{:S(2)}, u32[]{:S(2)}) collective-permute-start(f32[20,8,512]{2,1,0:T(8,128)} %get-tuple-element.30), channel_id=1, source_target_pairs={{1,0},{2,1},{3,2},{5,4},{6,5},{7,6},{9,8},{10,9},{11,10},{13,12},{... | collective-permute-start | bytes 983048 | tf_op jit(solution)/shard_map/ppermute | solution.py:816
  78.8 0.7 copy-start
  79.5 0.7 copy-start.5
  80.9 25.6 %all-to-all-start.4 = ((f32[8,16,128]{2,1,0:T(8,128)}), f32[8,16,128]{2,1,0:T(8,128)}, u32[]{:S(2)}, u32[]{:S(2)}) async-start(f32[8,16,128]{2,1,0:T(8,128)} %middle.1), calls=%async_computation.4 | async-start | bytes 131072 | tf_op jit(solution)/shard_map/all_to_all | solution.py:791
  101.2 21.4 %collective-permute-start.4 = (f32[2,72,512]{2,1,0:T(8,128)}, f32[2,72,512]{2,1,0:T(8,128)S(1)}, u32[]{:S(2)}, u32[]{:S(2)}) collective-permute-start(f32[2,72,512]{2,1,0:T(8,128)} %get-tuple-element.35), channel_id=1, source_target_pairs={{0,4},{4,8},{8,12},{12,16},{16,20},{20,24},{24,28},{1,5},{5,9},{9,... | collective-permute-start | bytes 884744 | tf_op jit(solution)/shard_map/ppermute | solution.py:815
  105.1 17.5 %collective-permute-start.5 = (f32[2,72,512]{2,1,0:T(8,128)}, f32[2,72,512]{2,1,0:T(8,128)S(1)}, u32[]{:S(2)}, u32[]{:S(2)}) collective-permute-start(f32[2,72,512]{2,1,0:T(8,128)} %get-tuple-element.34), channel_id=1, source_target_pairs={{4,0},{8,4},{12,8},{16,12},{20,16},{24,20},{28,24},{5,1},{9,5},{13... | collective-permute-start | bytes 884744 | tf_op jit(solution)/shard_map/ppermute | solution.py:816
  117.4 0.7 copy-start.3
  122.6 0.7 copy-start.7
  123.3 9.4 %copy-start.8 = (f32[2,72,512]{2,1,0:T(8,128)}, f32[2,72,512]{2,1,0:T(8,128)S(1)}, u32[]{:S(2)}) copy-start(f32[2,72,512]{2,1,0:T(8,128)S(1)} %collective-permute-done.5.high_ref) | copy-start | bytes 884740
  132.7 22.5 %all-to-all-start.7 = ((f32[8,16,128]{2,1,0:T(8,128)}), f32[8,16,128]{2,1,0:T(8,128)}, u32[]{:S(2)}, u32[]{:S(2)}) async-start(f32[8,16,128]{2,1,0:T(8,128)} %bitcast.6), calls=%async_computation.7 | async-start | bytes 131072 | tf_op jit(solution)/shard_map/all_to_all | solution.py:791
  155.2 0.7 copy-start.1
  155.9 0.7 copy-start.4
  156.6 0.7 copy-start.6

commit v7 on v6

--- a/solution.py
+++ b/solution.py
@@ -787,21 +787,8 @@
     )(everything, thin, base)
 
 
-def swap(rows, axis):
-    return lax.all_to_all(rows, axis, split_axis=0, concat_axis=0, tiled=True)
-
-
-def gather(copies):
-    column = swap(copies, "slab")
-    pairs = lax.axis_size("pair")
-    everyone = jnp.broadcast_to(column[None], (pairs,) + column.shape)
-    return swap(everyone, "pair")
-
-
-def reduce_pairs(term):
-    pairs, slabs = lax.axis_size("pair"), lax.axis_size("slab")
-    parts = swap(term, "pair").reshape(pairs, slabs, -1, BLK)
-    return swap(parts.sum(axis=0), "slab")
+def exchange(rows):
+    return lax.all_to_all(rows, ("slab", "pair"), split_axis=0, concat_axis=0, tiled=True)
 
 
 def together(*arrays):
@@ -831,40 +818,36 @@
     count = slabs * pairs
     blocks = mirror_fraction.shape[0]
     couples = tile_block_couples.T
-    owner, local = couples // blocks, couples % blocks
-    couples = ((owner % pairs) * slabs + owner // pairs) * blocks + local
 
     temp, cond = initial_warmth, heat_passing_coefficient
-    emitted, copies = emit(temp, element_facing_site, mirror_fraction, slabs)
+    emitted, copies = emit(temp, element_facing_site, mirror_fraction, count)
     temp, copies = together(temp, copies)
 
     def sweep_terms(whole):
         whole = whole.reshape(count * blocks, BLK)
         term = tile_terms(whole, couples, active_slot_count, view_factor_blocks)
-        return term.reshape(pairs, slabs * blocks, BLK)
-
-    whole = gather(copies)
+        return term.reshape(count, blocks, BLK)
+
+    whole = exchange(copies)
     send_low, send_high = pack_x(temp, cond)
     low, high = both_ways(send_low, send_high, "slab")
     whole = together(whole, send_low, send_high)[0]
-    parts = reduce_pairs(sweep_terms(whole))
+    parts = exchange(sweep_terms(whole))
+    copies, low, high = together(middle(parts, emitted, mirror_fraction), low, high)
+    whole = exchange(copies)
     send_down, send_up = pack_y(temp, cond, low, high)
-    parts = together(parts, send_down, send_up)[0]
     below, above = both_ways(send_down, send_up, "pair")
-    whole = gather(middle(parts, emitted, mirror_fraction))
     middle_temp, send_low, send_high, strided_cond, thin = first_round(
         temp, cond, low, high, below, above
     )
     low, high = both_ways(send_low, send_high, "slab")
     whole = together(whole, send_low, send_high)[0]
     term, low, high = together(sweep_terms(whole), low, high)
-    parts = reduce_pairs(term)
+    parts = exchange(term)
     base = second_round(middle_temp, low, high, strided_cond, temp.shape)
     parts = together(parts, base)[0]
     radiosity, source = last(parts, emitted, mirror_fraction, element_facing_site, nx * ny, count)
-    everything = lax.all_to_all(
-        source, ("slab", "pair"), split_axis=0, concat_axis=0, tiled=True
-    )
+    everything = exchange(source)
 
     warmed_liner = add_source(everything, thin, base)
     return (radiosity, warmed_liner)

time: 175 us -> 133 us (0.76)
  blocking collectives: 47.8 us -> 33.5 us
  waiting for transfers between devices: 20.3 us -> 7.29 us
  starting transfers between devices: 46.4 us -> 35.6 us
  other arithmetic: 2.33 us -> 0 us
  local copies, waits for them, and re-layouts: 6.45 us -> 4.16 us
    all_to_all x5 -> x3, waiting for transfers between devices: 20.3 us -> 0.97 us  [exchange(): lax.all_to_all(rows, ('slab', 'pair'), split_axis=0, concat_axis=0, tiled...]
    all_to_all x4 -> x2, blocking collectives: 47.8 us -> 33.5 us  [exchange(): lax.all_to_all(rows, ('slab', 'pair'), split_axis=0, concat_axis=0, tiled...]
    all_to_all x5 -> x3, starting transfers between devices: 28.5 us -> 18.5 us  [exchange(): lax.all_to_all(rows, ('slab', 'pair'), split_axis=0, concat_axis=0, tiled...]
    ppermute x3, waiting for transfers between devices: 0.01 us -> 6.31 us  [both_ways(): from_low = lax.ppermute(high, axis, forward)]
    unnamed x18 -> x16, local copies, waits for them, and re-layouts: 4.88 us -> 4.16 us
  transfers between devices with their start and end apart: 11 -> 9, of which waited for: 2 -> 2; matrix products, arithmetic and copies ran while one was open for 2% -> 0% of each run, Pallas kernels for 24% -> 31%
where the time goes in v7:
time: 133 us; the launch traced here: 131 us
  Pallas kernels  49.5 us (37%)
  starting transfers between devices  35.6 us (27%)
  blocking collectives  33.5 us (25%)
  waiting for transfers between devices  7.29 us (5%)
  local copies, waits for them, and re-layouts  4.16 us (3%)
  between operations  1.43 us (1%)
    all_to_all x2, blocking collectives, exchange(): lax.all_to_all(rows, ('slab', 'pair'), split_axis=0, concat_axis=0, tiled...  33.5 us
    all_to_all x3, starting transfers between devices, exchange(): lax.all_to_all(rows, ('slab', 'pair'), split_axis=0, concat_axis=0, tiled...  18.5 us
    pallas_call x1, Pallas kernels, first_round(): pl.pallas_call(first_round_kernel, out_shape=(jax.ShapeDtypeStruct((nx, w...  16.3 us
    ppermute x3, starting transfers between devices, both_ways(): from_low = lax.ppermute(high, axis, forward)  13.2 us
    pallas_call x1, Pallas kernels, second_round(): pl.pallas_call(second_round_kernel, out_shape=jax.ShapeDtypeStruct(shape,...  12.4 us
    pallas_call x2, Pallas kernels, tile_terms(): pl.pallas_call(tiles_kernel, out_shape=jax.ShapeDtypeStruct(whole.shape,...  9.31 us
    ppermute x3, waiting for transfers between devices, both_ways(): from_low = lax.ppermute(high, axis, forward)  6.31 us
    unnamed x16, local copies, waits for them, and re-layouts  4.16 us
  transfers between devices with their start and end apart: 9, of which 2 were waited for; matrix products, arithmetic and copies ran while one was open for 0% of the time, Pallas kernels for 31%

profile of v7, /device:TPU:0, one launch (start us, length us, event | category | flops | bytes accessed | tf_op | source)
XLA Modules:
  0.0 131.4 jit_solution(11456973261139947701)
XLA Ops:
  0.6 2.1 %emit.1 = (f32[16,128]{1,0:T(8,128)}, f32[32,16,128]{2,1,0:T(8,128)}) custom-call(f32[16,64,512]{2,1,0:T(8,128)} %t_ref, s32[16,128]{1,0:T(8,128)} %site_ref.3, f32[16,128]{1,0:T(8,128)} %mirror_ref.5), custom_call_target="tpu_custom_call" | custom-call | flops 10000 | bytes 900000 | tf_op jit(solution)/shard_map/emit/pallas_call | solution.py:97
  2.8 7.4 %all-to-all-start = ((f32[32,16,128]{2,1,0:T(8,128)}), f32[32,16,128]{2,1,0:T(8,128)}, u32[]{:S(2)}, u32[]{:S(2)}) async-start(f32[32,16,128]{2,1,0:T(8,128)} %get-tuple-element.27), calls=%async_computation | async-start | bytes 524288 | tf_op jit(solution)/shard_map/all_to_all | solution.py:791
  10.2 2.3 %pack_x.1 = (f32[272,512]{1,0:T(8,128)}, f32[272,512]{1,0:T(8,128)}) custom-call(f32[16,64,512]{2,1,0:T(8,128)} %t_ref, f32[16,64,512]{2,1,0:T(8,128)} %k_ref.1, f32[16,64,512]{2,1,0:T(8,128)} %k_ref.1, f32[16,64,512]{2,1,0:T(8,128)} %t_ref, f32[16,64,512]{2,1,0:T(8,128)} %k_ref.1, f32[16,64,512]{2,1,0:T(8,128)} %k_ref.1), custom_call_target="tpu_custom_call" | custom-call | bytes 2228224 | tf_op jit(solution)/shard_map/pack_x/pallas_call | solution.py:315
  12.5 1.3 collective-permute-start.1
  13.8 5.4 %collective-permute-start = (f32[272,512]{1,0:T(8,128)}, f32[272,512]{1,0:T(8,128)}, u32[]{:S(2)}, u32[]{:S(2)}) collective-permute-start(f32[272,512]{1,0:T(8,128)} %get-tuple-element.30), channel_id=1, source_target_pairs={{0,4},{4,8},{8,12},{12,16},{16,20},{20,24},{24,28},{1,5},{5,9},{9,... | collective-permute-start | bytes 1671176 | tf_op jit(solution)/shard_map/ppermute | solution.py:802
  19.8 1.0 all-to-all-done
  20.8 0.0 copy-start.3
  20.8 0.7 copy-done.3
  21.5 0.0 copy-start.1
  21.5 0.0 copy-start.6
  21.5 4.3 %tiles.2 = f32[512,128]{1,0:T(8,128)S(1)} custom-call(s32[1]{0:T(128)S(6)} %copy.11.live_ref, s32[2,256]{1,0:T(2,128)S(1)} %bitcast.6, s32[2,256]{1,0:T(2,128)S(1)} %bitcast.7, f32[512,128]{1,0:T(8,128)} %bitcast.1.whole_ref, f32[256,128,128]{2,1,0:T(8,128)} %tiles_ref.3), custom_call_target="tpu_custom_call" | custom-call | flops 134217728 | bytes 16777216 | tf_op jit(solution)/shard_map/tiles/pallas_call | solution.py:201
  25.8 19.6 %all_to_all.25.parts_ref = f32[32,16,128]{2,1,0:T(8,128)S(1)} all-to-all(f32[32,16,128]{2,1,0:T(8,128)S(1)} %bitcast.5), channel_id=1, replica_groups=mesh['slab'=8,'pair'=4] {'slab','pair'}, dimensions={0} | all-to-all | bytes 524288 | tf_op jit(solution)/shard_map/all_to_all | solution.py:791
  45.4 0.0 copy-done.1
  45.4 0.0 copy-done.6
  45.4 0.1 middle.1
  45.4 0.0 copy-start
  45.4 0.7 copy-done
  46.1 0.0 collective-permute-done.1.high_ref
  46.1 0.0 collective-permute-done.low_ref
  46.1 2.5 %pack_y.1 = (f32[20,8,512]{2,1,0:T(8,128)}, f32[20,8,512]{2,1,0:T(8,128)}) custom-call(f32[16,64,512]{2,1,0:T(8,128)} %t_ref, f32[16,64,512]{2,1,0:T(8,128)} %k_ref.1, f32[16,64,512]{2,1,0:T(8,128)} %t_ref, f32[16,64,512]{2,1,0:T(8,128)} %k_ref.1, f32[272,512]{1,0:T(8,128)} %collective-permute-done.low_ref, f32[272,512]{1,0:T(8,128)} %collective-permute-done.1.high_ref), custom_call_target="tpu_custom_call" | custom-call | bytes 1310720 | tf_op jit(solution)/shard_map/pack_y/pallas_call | solution.py:356
  48.6 2.5 %collective-permute-start.2 = (f32[20,8,512]{2,1,0:T(8,128)}, f32[20,8,512]{2,1,0:T(8,128)}, u32[]{:S(2)}, u32[]{:S(2)}) collective-permute-start(f32[20,8,512]{2,1,0:T(8,128)} %get-tuple-element.36), channel_id=1, source_target_pairs={{0,1},{1,2},{2,3},{4,5},{5,6},{6,7},{8,9},{9,10},{10,11},{12,13},{... | collective-permute-start | bytes 983048 | tf_op jit(solution)/shard_map/ppermute | solution.py:802
  51.1 1.3 collective-permute-start.3
  52.4 6.1 %all-to-all-start.2 = ((f32[32,16,128]{2,1,0:T(8,128)}), f32[32,16,128]{2,1,0:T(8,128)}, u32[]{:S(2)}, u32[]{:S(2)}) async-start(f32[32,16,128]{2,1,0:T(8,128)} %copy-done), calls=%async_computation.2 | async-start | bytes 524288 | tf_op jit(solution)/shard_map/all_to_all | solution.py:791
  58.6 0.0 collective-permute-done.2.below_ref
  58.6 0.0 collective-permute-done.3.above_ref
  58.6 16.3 %first_round.1 = (f32[16,72,512]{2,1,0:T(8,128)}, f32[2,72,512]{2,1,0:T(8,128)}, f32[2,72,512]{2,1,0:T(8,128)}, f32[20,72,512]{2,1,0:T(8,128)}, f32[24,8,128]{2,1,0:T(8,128)}) custom-call(f32[16,64,512]{2,1,0:T(8,128)} %t_ref, f32[16,64,512]{2,1,0:T(8,128)} %k_ref.1, f32[272,512]{1,0:T(8,128)} %collective-permute-done.low_ref, ...), custom_call_target="tpu_custom_call" | custom-call | flops 73728000 | bytes 25165824 | tf_op jit(solution)/shard_map/first_round/pallas_call | solution.py:618
  74.9 1.3 collective-permute-start.5
  76.2 5.3 %collective-permute-start.4 = (f32[2,72,512]{2,1,0:T(8,128)}, f32[2,72,512]{2,1,0:T(8,128)}, u32[]{:S(2)}, u32[]{:S(2)}) collective-permute-start(f32[2,72,512]{2,1,0:T(8,128)} %get-tuple-element.39), channel_id=1, source_target_pairs={{0,4},{4,8},{8,12},{12,16},{16,20},{20,24},{24,28},{1,5},{5,9},{9,... | collective-permute-start | bytes 884744 | tf_op jit(solution)/shard_map/ppermute | solution.py:802
  81.5 0.0 all-to-all-done.2
  81.5 0.0 copy-start.4
  81.5 0.7 copy-done.4
  82.1 5.0 %tiles.3 = f32[512,128]{1,0:T(8,128)} custom-call(s32[1]{0:T(128)S(6)} %copy.11.live_ref, s32[2,256]{1,0:T(2,128)S(1)} %bitcast.8, s32[2,256]{1,0:T(2,128)S(1)} %bitcast.9, f32[512,128]{1,0:T(8,128)} %bitcast.3.whole_ref, f32[256,128,128]{2,1,0:T(8,128)} %tiles_ref.3), custom_call_target="tpu_custom_call" | custom-call | flops 134217728 | bytes 16777216 | tf_op jit(solution)/shard_map/tiles/pallas_call | solution.py:201
  87.1 0.0 collective-permute-done.5.high_ref
  87.2 6.3 %collective-permute-done.4.low_ref = f32[2,72,512]{2,1,0:T(8,128)} collective-permute-done((f32[2,72,512]{2,1,0:T(8,128)}, f32[2,72,512]{2,1,0:T(8,128)}, u32[]{:S(2)}, u32[]{:S(2)}) %collective-permute-start.4) | collective-permute-done | bytes 294944 | tf_op jit(solution)/shard_map/ppermute | solution.py:802
  93.5 5.0 %all-to-all-start.3 = ((f32[32,16,128]{2,1,0:T(8,128)}), f32[32,16,128]{2,1,0:T(8,128)}, u32[]{:S(2)}, u32[]{:S(2)}) async-start(f32[32,16,128]{2,1,0:T(8,128)} %bitcast.4), calls=%async_computation.3 | async-start | bytes 524288 | tf_op jit(solution)/shard_map/all_to_all | solution.py:791
  98.5 12.4 %second_round.1.base_ref = f32[16,64,512]{2,1,0:T(8,128)} custom-call(f32[16,72,512]{2,1,0:T(8,128)} %get-tuple-element.42.t_ref, f32[2,72,512]{2,1,0:T(8,128)} %collective-permute-done.4.low_ref, f32[2,72,512]{2,1,0:T(8,128)} %collective-permute-done.5.high_ref, f32[20,72,512]{2,1,0:T(8,128)} %get-tuple-element.45.k_ref), custom_call_target="tpu_custom_call" | custom-call | flops 44236800 | bytes 18874368 | tf_op jit(solution)/shard_map/second_round/pallas_call | solution.py:672
  110.9 0.0 all-to-all-done.3.parts_ref
  110.9 0.0 copy-start.2
  110.9 0.7 copy-done.2
  111.6 0.0 copy-start.5
  111.6 0.7 copy-done.5
  112.3 0.0 copy-start.7
  112.3 0.7 copy-done.7
  113.0 2.0 %last.1 = (f32[16,128]{1,0:T(8,128)}, f32[32,8,128]{2,1,0:T(8,128)S(1)}) custom-call(f32[32,16,128]{2,1,0:T(8,128)} %all-to-all-done.3.parts_ref, f32[16,128]{1,0:T(8,128)S(1)} %copy-done.7, f32[16,128]{1,0:T(8,128)S(1)} %copy-done.2, s32[16,128]{1,0:T(8,128)S(1)} %copy-done.5), custom_call_target="tpu_custom_call" | custom-call | flops 10000000 | bytes 600000 | tf_op jit(solution)/shard_map/last/pallas_call | solution.py:274
  114.9 13.9 %all_to_all.26.all_ref = f32[32,8,128]{2,1,0:T(8,128)} all-to-all(f32[32,8,128]{2,1,0:T(8,128)S(1)} %get-tuple-element.48), channel_id=1, replica_groups=mesh['slab'=8,'pair'=4] {'slab','pair'}, dimensions={0} | all-to-all | bytes 262144 | tf_op jit(solution)/shard_map/all_to_all | solution.py:791
  128.8 2.6 %add_source.1 = f32[16,64,512]{2,1,0:T(8,128)} custom-call(f32[32,8,128]{2,1,0:T(8,128)} %all_to_all.26.all_ref, f32[24,8,128]{2,1,0:T(8,128)} %get-tuple-element.49.thin_ref, f32[16,64,512]{2,1,0:T(8,128)} %second_round.1.base_ref), custom_call_target="tpu_custom_call", output_to_operand_aliasing={{}: (2, {})} | custom-call | flops 1000000 | bytes 1048576 | tf_op jit(solution)/shard_map/add_source/pallas_call | solution.py:773
Async XLA Ops:
  2.8 18.0 %all-to-all-start = ((f32[32,16,128]{2,1,0:T(8,128)}), f32[32,16,128]{2,1,0:T(8,128)}, u32[]{:S(2)}, u32[]{:S(2)}) async-start(f32[32,16,128]{2,1,0:T(8,128)} %get-tuple-element.27), calls=%async_computation | async-start | bytes 524288 | tf_op jit(solution)/shard_map/all_to_all | solution.py:791
  12.5 33.6 %collective-permute-start.1 = (f32[272,512]{1,0:T(8,128)}, f32[272,512]{1,0:T(8,128)}, u32[]{:S(2)}, u32[]{:S(2)}) collective-permute-start(f32[272,512]{1,0:T(8,128)} %get-tuple-element.29), channel_id=1, source_target_pairs={{4,0},{8,4},{12,8},{16,12},{20,16},{24,20},{28,24},{5,1},{9,5},{13... | collective-permute-start | bytes 1671176 | tf_op jit(solution)/shard_map/ppermute | solution.py:803
  13.8 32.4 %collective-permute-start = (f32[272,512]{1,0:T(8,128)}, f32[272,512]{1,0:T(8,128)}, u32[]{:S(2)}, u32[]{:S(2)}) collective-permute-start(f32[272,512]{1,0:T(8,128)} %get-tuple-element.30), channel_id=1, source_target_pairs={{0,4},{4,8},{8,12},{12,16},{16,20},{20,24},{24,28},{1,5},{5,9},{9,... | collective-permute-start | bytes 1671176 | tf_op jit(solution)/shard_map/ppermute | solution.py:802
  20.8 0.7 copy-start.3
  21.5 23.9 %copy-start.1 = (f32[16,128]{1,0:T(8,128)S(1)}, f32[16,128]{1,0:T(8,128)}, u32[]{:S(2)}) copy-start(f32[16,128]{1,0:T(8,128)} %mirror_ref.5) | copy-start | bytes 24580
  21.5 23.9 %copy-start.6 = (f32[16,128]{1,0:T(8,128)S(1)}, f32[16,128]{1,0:T(8,128)}, u32[]{:S(2)}) copy-start(f32[16,128]{1,0:T(8,128)} %get-tuple-element.32.emitted_ref) | copy-start | bytes 24580
  45.4 0.7 copy-start
  48.6 10.0 %collective-permute-start.2 = (f32[20,8,512]{2,1,0:T(8,128)}, f32[20,8,512]{2,1,0:T(8,128)}, u32[]{:S(2)}, u32[]{:S(2)}) collective-permute-start(f32[20,8,512]{2,1,0:T(8,128)} %get-tuple-element.36), channel_id=1, source_target_pairs={{0,1},{1,2},{2,3},{4,5},{5,6},{6,7},{8,9},{9,10},{10,11},{12,13},{... | collective-permute-start | bytes 983048 | tf_op jit(solution)/shard_map/ppermute | solution.py:802
  51.1 7.4 %collective-permute-start.3 = (f32[20,8,512]{2,1,0:T(8,128)}, f32[20,8,512]{2,1,0:T(8,128)}, u32[]{:S(2)}, u32[]{:S(2)}) collective-permute-start(f32[20,8,512]{2,1,0:T(8,128)} %get-tuple-element.37), channel_id=1, source_target_pairs={{1,0},{2,1},{3,2},{5,4},{6,5},{7,6},{9,8},{10,9},{11,10},{13,12},{... | collective-permute-start | bytes 983048 | tf_op jit(solution)/shard_map/ppermute | solution.py:803
  52.4 29.0 %all-to-all-start.2 = ((f32[32,16,128]{2,1,0:T(8,128)}), f32[32,16,128]{2,1,0:T(8,128)}, u32[]{:S(2)}, u32[]{:S(2)}) async-start(f32[32,16,128]{2,1,0:T(8,128)} %copy-done), calls=%async_computation.2 | async-start | bytes 524288 | tf_op jit(solution)/shard_map/all_to_all | solution.py:791
  74.9 12.3 %collective-permute-start.5 = (f32[2,72,512]{2,1,0:T(8,128)}, f32[2,72,512]{2,1,0:T(8,128)}, u32[]{:S(2)}, u32[]{:S(2)}) collective-permute-start(f32[2,72,512]{2,1,0:T(8,128)} %get-tuple-element.38), channel_id=1, source_target_pairs={{4,0},{8,4},{12,8},{16,12},{20,16},{24,20},{28,24},{5,1},{9,5},{13... | collective-permute-start | bytes 884744 | tf_op jit(solution)/shard_map/ppermute | solution.py:803
  76.2 17.3 %collective-permute-start.4 = (f32[2,72,512]{2,1,0:T(8,128)}, f32[2,72,512]{2,1,0:T(8,128)}, u32[]{:S(2)}, u32[]{:S(2)}) collective-permute-start(f32[2,72,512]{2,1,0:T(8,128)} %get-tuple-element.39), channel_id=1, source_target_pairs={{0,4},{4,8},{8,12},{12,16},{16,20},{20,24},{24,28},{1,5},{5,9},{9,... | collective-permute-start | bytes 884744 | tf_op jit(solution)/shard_map/ppermute | solution.py:802
  81.5 0.7 copy-start.4
  93.5 17.4 %all-to-all-start.3 = ((f32[32,16,128]{2,1,0:T(8,128)}), f32[32,16,128]{2,1,0:T(8,128)}, u32[]{:S(2)}, u32[]{:S(2)}) async-start(f32[32,16,128]{2,1,0:T(8,128)} %bitcast.4), calls=%async_computation.3 | async-start | bytes 524288 | tf_op jit(solution)/shard_map/all_to_all | solution.py:791
  110.9 0.7 copy-start.2
  111.6 0.7 copy-start.5
  112.3 0.7 copy-start.7

commit v8 on v7

--- a/solution.py
+++ b/solution.py
@@ -11,7 +11,6 @@
 SWEEPS = 2
 STEPS = 4
 HALO = STEPS
-DEPTH = STEPS // 2
 ROWS = STEPS
 LANES = 128
 CHUNK = 16
@@ -208,7 +207,7 @@
             pltpu.VMEM((2, slots, BLK), jnp.float32),
             pltpu.SemaphoreType.DMA((slots // CHUNK,)),
         ],
-        compiler_params=params(50),
+        compiler_params=params(64),
         cost_estimate=cost(slots * BLK * BLK * 32, slots * BLK * BLK * 4),
         name="tiles",
     )(live, couples, couples, whole, tiles)
@@ -234,7 +233,7 @@
     return pl.pallas_call(
         middle_kernel,
         out_shape=jax.ShapeDtypeStruct(parts.shape, jnp.float32),
-        compiler_params=params(32),
+        compiler_params=params(64),
         cost_estimate=cost(100_000, 600_000),
         name="middle",
     )(parts, emitted, mirror)
@@ -277,92 +276,72 @@
             jax.ShapeDtypeStruct(mirror.shape, jnp.float32),
             jax.ShapeDtypeStruct((count, cells // LANES, LANES), jnp.float32),
         ),
-        compiler_params=params(32),
+        compiler_params=params(64),
         cost_estimate=cost(10_000_000, 600_000),
         name="last",
     )(parts, emitted, mirror, site)
 
 
-def first_planes(depth, ny, nz):
-    return pl.BlockSpec((depth, ny, nz), lambda i: (0, 0, 0))
-
-
-def pack_x_kernel(t_low, k_low, k_low_thin, t_high, k_high, k_high_thin, low_ref, high_ref):
-    ny, nz = t_low.shape[1:]
-    tail = 2 * DEPTH * ny
-    piece = ny * LANES // nz
-    for send, temp, cond, thin, at in (
-        (low_ref, t_low, k_low, k_low_thin, DEPTH),
-        (high_ref, t_high, k_high, k_high_thin, k_high_thin.shape[0] - DEPTH - 1),
+def pack_y_kernel(t0, k0, t7, k7, down_ref, up_ref):
+    upper = lax.broadcasted_iota(jnp.int32, down_ref.shape[1:], 0) < ROWS
+    for x in range(down_ref.shape[0]):
+        down_ref[x] = jnp.where(upper, t0[x], pltpu.roll(k0[x], ROWS, 0))
+        up_ref[x] = jnp.where(upper, pltpu.roll(t7[x], ROWS, 0), k7[x])
+
+
+def pack_y(temp, cond):
+    nx, ny, nz = temp.shape
+    first = pl.BlockSpec((nx, 8, nz), lambda i: (0, 0, 0))
+    final = pl.BlockSpec((nx, 8, nz), lambda i: (0, ny // 8 - 1, 0))
+    shape = jax.ShapeDtypeStruct((nx, 8, nz), jnp.float32)
+    return pl.pallas_call(
+        pack_y_kernel,
+        grid=(1,),
+        out_shape=(shape, shape),
+        in_specs=[first, first, final, final],
+        out_specs=(first, first),
+        compiler_params=params(64),
+        cost_estimate=cost(0, 4 * nx * 8 * nz * 4),
+        name="pack_y",
+    )(temp, cond, temp, cond)
+
+
+def pack_x_kernel(first, final, below0, above0, below1, above1, low_ref, high_ref):
+    ny, nz = first.shape[1:]
+    upper = lax.broadcasted_iota(jnp.int32, (8, nz), 0) < ROWS
+    for send, temp, below, above in (
+        (low_ref, first, below0, above0),
+        (high_ref, final, below1, above1),
     ):
-        for p in range(DEPTH):
-            send[p * ny : p * ny + ny, :] = temp[p]
-            send[(DEPTH + p) * ny : (DEPTH + p + 1) * ny, :] = cond[p]
-        for j in range(nz // LANES):
-            send[tail:, j * LANES : (j + 1) * LANES] = thin[at, j * piece : (j + 1) * piece, :]
-
-
-def pack_x(temp, cond):
+        for p in range(HALO):
+            send[p, :ny] = temp[p]
+            send[p, ny : ny + 8] = jnp.where(upper, above[p], pltpu.roll(below[p], ROWS, 0))
+            send[p, ny + 8 :] = jnp.where(upper, pltpu.roll(above[p], ROWS, 0), below[p])
+
+
+def pack_x(temp, below, above):
     nx, ny, nz = temp.shape
-    ends = 2 * DEPTH
-    rows = 2 * DEPTH * ny + ny * LANES // nz
-    first = pl.BlockSpec((DEPTH, ny, nz), lambda i: (0, 0, 0))
-    final = pl.BlockSpec((DEPTH, ny, nz), lambda i: (nx // DEPTH - 1, 0, 0))
-    first_thin = pl.BlockSpec((ends, ny, LANES), lambda i: (0, 0, 0))
-    final_thin = pl.BlockSpec((ends, ny, LANES), lambda i: (nx // ends - 1, 0, 0))
-    whole = pl.BlockSpec((rows, nz), lambda i: (0, 0))
-    shape = jax.ShapeDtypeStruct((rows, nz), jnp.float32)
+
+    def ends(rows):
+        return (
+            pl.BlockSpec((HALO, rows, nz), lambda i: (0, 0, 0)),
+            pl.BlockSpec((HALO, rows, nz), lambda i: (nx // HALO - 1, 0, 0)),
+        )
+
+    first, final = ends(ny)
+    first_rows, final_rows = ends(8)
+    whole = pl.BlockSpec((HALO, ny + 16, nz), lambda i: (0, 0, 0))
+    shape = jax.ShapeDtypeStruct((HALO, ny + 16, nz), jnp.float32)
     return pl.pallas_call(
         pack_x_kernel,
         grid=(1,),
         out_shape=(shape, shape),
-        in_specs=[first, first, first_thin, final, final, final_thin],
+        in_specs=[first, final, first_rows, first_rows, final_rows, final_rows],
         out_specs=(whole, whole),
         compiler_params=params(64),
-        cost_estimate=cost(0, 4 * rows * nz * 4),
+        cost_estimate=cost(0, 4 * HALO * (ny + 16) * nz * 4),
         name="pack_x",
-    )(temp, cond, cond, temp, cond, cond)
-
-
-def pack_y_kernel(nx, ny, t0, k0, t7, k7, low_ref, high_ref, down_ref, up_ref):
-    upper = lax.broadcasted_iota(jnp.int32, down_ref.shape[1:], 0) < ROWS
-
-    def edge(x, t_first, k_first, t_final, k_final):
-        down_ref[x] = jnp.where(upper, t_first, pltpu.roll(k_first, ROWS, 0))
-        up_ref[x] = jnp.where(upper, pltpu.roll(t_final, ROWS, 0), k_final)
-
-    for side, base in ((low_ref, 0), (high_ref, DEPTH + nx)):
-        for p in range(DEPTH):
-            t_at, k_at = p * ny, (DEPTH + p) * ny
-            edge(
-                base + p,
-                side[t_at : t_at + 8, :],
-                side[k_at : k_at + 8, :],
-                side[t_at + ny - 8 : t_at + ny, :],
-                side[k_at + ny - 8 : k_at + ny, :],
-            )
-    for x in range(nx):
-        edge(DEPTH + x, t0[x], k0[x], t7[x], k7[x])
-
-
-def pack_y(temp, cond, low, high):
-    nx, ny, nz = temp.shape
-    first = pl.BlockSpec((nx, 8, nz), lambda i: (0, 0, 0))
-    final = pl.BlockSpec((nx, 8, nz), lambda i: (0, ny // 8 - 1, 0))
-    halo = pl.BlockSpec(low.shape, lambda i: (0, 0))
-    tall = nx + 2 * DEPTH
-    whole = pl.BlockSpec((tall, 8, nz), lambda i: (0, 0, 0))
-    shape = jax.ShapeDtypeStruct((tall, 8, nz), jnp.float32)
-    return pl.pallas_call(
-        functools.partial(pack_y_kernel, nx, ny),
-        grid=(1,),
-        out_shape=(shape, shape),
-        in_specs=[first, first, final, final, halo, halo],
-        out_specs=(whole, whole),
-        compiler_params=params(64),
-        cost_estimate=cost(0, 4 * tall * 8 * nz * 4),
-        name="pack_y",
-    )(temp, cond, temp, cond, low, high)
+    )(temp, temp, below, above, below, above)
 
 
 def coupling(a, b):
@@ -467,7 +446,7 @@
         stores.finish()
 
 
-def thin_planes(cond, ny, thin_ref, base_plane):
+def thin_planes(cond, ny, thin_ref):
     tall, _, wide, _ = cond.shape
     lane = lax.broadcasted_iota(jnp.int32, (wide, LANES), 1)
     y_lane = lax.broadcasted_iota(jnp.int32, (8, LANES), 1)
@@ -485,204 +464,139 @@
         for g in range(planes):
             rows = turned[8 * g : 8 * g + 8, :]
             moved = pltpu.roll(rows, LANES - wide, 1)
-            thin_ref[base_plane + base + g] = jnp.where(
+            thin_ref[base + g] = jnp.where(
                 y_lane < ny + ROWS, rows, jnp.where(y_lane >= LANES - ROWS, moved, 0.0)
             )
 
 
-def first_round_kernel(
-    t_ref, k_ref, low_ref, high_ref, below_ref, above_ref,
-    out_ref, low_out, high_out, cond_out, thin_ref,
-    loaded, field, between, gx, gy, gz, gb, carried, sems,
+def heat_kernel(
+    t_ref, k_ref, k_low, k_high, t_low, t_high, below_ref, above_ref, out_ref, thin_ref,
+    loaded, field, between, gx, gy, gz, gb, carried, placed, sems,
 ):
     nx, ny, nz = t_ref.shape
-    tall, wide = nx + 2 * DEPTH, ny + 2 * ROWS
+    tall, wide = nx + 2 * HALO, ny + 2 * ROWS
     tiles = wide // 8
     raw_t, raw_k = loaded.at[0], loaded.at[1]
     spans = lane_tiles(nz)
-    copies = [
-        pltpu.make_async_copy(
-            ref.at[:, :, pl.ds(z.start, LANES)],
-            loaded.at[which, pl.ds(DEPTH, nx), j, pl.ds(0, ny)],
-            sems.at[which, j],
-        )
-        for which, ref in ((1, k_ref), (0, t_ref))
-        for j, z in enumerate(spans)
-    ]
-    for copy in copies:
+    ends = (0, HALO + nx)
+
+    def fetch(which, k, ref, source_row, planes, at, row, rows):
+        return [
+            pltpu.make_async_copy(
+                ref.at[:, pl.ds(source_row, rows), pl.ds(z.start, LANES)],
+                loaded.at[which, pl.ds(at, planes), j, pl.ds(row, rows)],
+                sems.at[which, k, j],
+            )
+            for j, z in enumerate(spans)
+        ]
+
+    k_copies = fetch(1, 0, k_ref, 0, nx, HALO, 0, ny)
+    t_copies = fetch(0, 0, t_ref, 0, nx, HALO, 0, ny)
+    for k, (at, k_side, t_side) in enumerate(zip(ends, (k_low, k_high), (t_low, t_high))):
+        k_copies += fetch(1, 1 + k, k_side, 0, HALO, at, 0, ny)
+        k_copies += fetch(1, 3 + k, t_side, ny + 8, HALO, at, ny, 8)
+        t_copies += fetch(0, 1 + k, t_side, 0, HALO, at, 0, ny + 8)
+    for copy in k_copies + t_copies:
         copy.start()
     has_low, has_high, has_below, has_above = neighbours()
     upper = lax.broadcasted_iota(jnp.int32, (8, LANES), 0) < ROWS
-    for side, base in ((low_ref, 0), (high_ref, DEPTH + nx)):
-        for p in range(DEPTH):
-            for j, z in enumerate(spans):
-                raw_t[base + p, j, :ny] = side[p * ny : p * ny + ny, z]
-                raw_k[base + p, j, :ny] = side[(DEPTH + p) * ny : (DEPTH + p + 1) * ny, z]
-
-    @pl.loop(0, tall)
+
+    @pl.loop(0, nx)
     def _(x):
         for j, z in enumerate(spans):
             down, up = above_ref[x, :, z], below_ref[x, :, z]
-            raw_t[x, j, ny:] = jnp.where(upper, down, pltpu.roll(up, ROWS, 0))
-            raw_k[x, j, ny:] = jnp.where(upper, pltpu.roll(down, ROWS, 0), up)
-
-    for copy in copies:
+            raw_t[HALO + x, j, ny:] = jnp.where(upper, down, pltpu.roll(up, ROWS, 0))
+            raw_k[HALO + x, j, ny:] = jnp.where(upper, pltpu.roll(down, ROWS, 0), up)
+
+    for copy in k_copies:
         copy.wait()
 
-    piece = ny * LANES // nz
-    tail = 2 * DEPTH * ny
-    thin_planes(raw_k, ny, thin_ref, HALO - DEPTH)
-    for side, at in ((low_ref, HALO - DEPTH - 1), (high_ref, HALO + nx + DEPTH)):
-        edge = [side[tail:, z] for z in lane_tiles(nz)]
-        edge.append(jnp.zeros((LANES - ny, LANES), jnp.float32))
-        turned = jnp.concatenate(edge, axis=0).T
-        thin_ref[at] = turned[:8]
-    for at in [*range(HALO - DEPTH - 1), *range(HALO + nx + DEPTH + 1, nx + 2 * HALO)]:
-        thin_ref[at] = jnp.zeros((8, LANES), jnp.float32)
-
-    @pl.loop(0, tall)
-    def _(x):
+    thin_planes(raw_k, ny, thin_ref)
+
+    @pl.when(jnp.logical_not(has_above & has_below))
+    def _():
         missing = (upper & jnp.logical_not(has_above)) | (
             jnp.logical_not(upper) & jnp.logical_not(has_below)
         )
-        for j in range(len(spans)):
-            edge = raw_k[x, j, ny:]
-            last = jnp.broadcast_to(raw_k[x, j, ny - 1 : ny, :], edge.shape)
-            first = jnp.broadcast_to(raw_k[x, j, 0:1, :], edge.shape)
-            raw_k[x, j, ny:] = jnp.where(missing, jnp.where(upper, last, first), edge)
+
+        @pl.loop(0, tall)
+        def _(x):
+            for j in range(len(spans)):
+                edge = raw_k[x, j, ny:]
+                last = jnp.broadcast_to(raw_k[x, j, ny - 1 : ny, :], edge.shape)
+                first = jnp.broadcast_to(raw_k[x, j, 0:1, :], edge.shape)
+                raw_k[x, j, ny:] = jnp.where(missing, jnp.where(upper, last, first), edge)
 
     @pl.when(jnp.logical_not(has_low))
     def _():
-        for p in range(DEPTH):
-            raw_k[p] = raw_k[DEPTH]
+        raw_k[HALO - 1] = raw_k[HALO]
 
     @pl.when(jnp.logical_not(has_high))
     def _():
-        for p in range(DEPTH):
-            raw_k[DEPTH + nx + p] = raw_k[DEPTH + nx - 1]
-
-    @pl.loop(0, tall)
+        raw_k[HALO + nx] = raw_k[HALO + nx - 1]
+
+    def spread(which, target):
+        @pl.loop(0, tall)
+        def _(x):
+            for t in range(tiles):
+                rows = pl.ds(t, 8, stride=tiles)
+                for j, z in enumerate(spans):
+                    target[x, 8 * t : 8 * t + 8, z] = loaded[which, x, j, rows, :]
+
+    spread(1, between)
+    prepare(between, gx, gy, gz, gb)
+    for copy in t_copies:
+        copy.wait()
+    spread(0, field)
+
+    for x in (HALO - 1, HALO + nx):
+        between[x] = jnp.zeros((wide, nz), jnp.float32)
+
+    def inside(target):
+        return lambda x, t, z: (target, (x, slice(8 * t, 8 * t + 8), z))
+
+    def outside(x, t, z):
+        return placed, (x - HALO, z.start // LANES, pl.ds(t, 8, stride=tiles))
+
+    old, new = field, between
+    for step in range(1, STEPS):
+        begin = jnp.where(has_low, step, HALO)
+        end = jnp.where(has_high, tall - step, tall - HALO)
+        one_step(old, begin, end, inside(new), gx, gy, gz, gb, carried)
+        old, new = new, old
+    one_step(old, HALO, tall - HALO, outside, gx, gy, gz, gb, carried)
+
+    @pl.loop(0, nx)
     def _(x):
-        stores = Lagging(LAG)
-        for t in range(tiles):
-            rows = pl.ds(t, 8, stride=tiles)
-            for j, z in enumerate(spans):
-                stores.add(put(field, (x, slice(8 * t, 8 * t + 8), z), loaded[0, x, j, rows, :]))
-                stores.add(put(cond_out, (x, slice(8 * t, 8 * t + 8), z), loaded[1, x, j, rows, :]))
-        stores.finish()
-
-    prepare(cond_out, gx, gy, gz, gb)
-
-    def target(x, t, z):
-        return out_ref, (x - DEPTH, slice(8 * t, 8 * t + 8), z)
-
-    two_steps(field, between, gx, gy, gz, gb, carried, target)
-    low_out[...] = out_ref[:DEPTH]
-    high_out[...] = out_ref[nx - DEPTH :]
-
-
-def two_steps(field, between, gx, gy, gz, gb, carried, target):
-    tall = field.shape[0]
-    has_low, has_high, _, _ = neighbours()
-    for x in (1, tall - 2):
-        between[x] = jnp.zeros(field.shape[1:], jnp.float32)
-
-    def inner(x, t, z):
-        return between, (x, slice(8 * t, 8 * t + 8), z)
-
-    begin = jnp.where(has_low, 1, DEPTH)
-    end = jnp.where(has_high, tall - 1, tall - DEPTH)
-    one_step(field, begin, end, inner, gx, gy, gz, gb, carried)
-    one_step(between, DEPTH, tall - DEPTH, target, gx, gy, gz, gb, carried)
-
-
-def heat_scratch(tall, wide, nz):
-    big = pltpu.VMEM((tall, wide, nz), jnp.float32)
-    return [
-        big,
-        big,
-        big,
-        big,
-        big,
-        pltpu.VMEM((tall, wide, LANES), jnp.float32),
-        pltpu.VMEM((wide, nz), jnp.float32),
-    ]
-
-
-def first_round(temp, cond, low, high, below, above):
+        for j, z in enumerate(spans):
+            out_ref[x, :, z] = placed[x, j, :ny, :]
+
+
+def heat(temp, cond, k_low, k_high, t_low, t_high, below, above):
     nx, ny, nz = temp.shape
-    tall, wide = nx + 2 * DEPTH, ny + 2 * ROWS
+    tall, wide = nx + 2 * HALO, ny + 2 * ROWS
     hbm = pl.BlockSpec(memory_space=pl.ANY)
     vmem = pl.BlockSpec(memory_space=pltpu.VMEM)
-    plane = jax.ShapeDtypeStruct((DEPTH, wide, nz), jnp.float32)
+    big = pltpu.VMEM((tall, wide, nz), jnp.float32)
     return pl.pallas_call(
-        first_round_kernel,
+        heat_kernel,
         out_shape=(
-            jax.ShapeDtypeStruct((nx, wide, nz), jnp.float32),
-            plane,
-            plane,
-            jax.ShapeDtypeStruct((tall, wide, nz), jnp.float32),
-            jax.ShapeDtypeStruct((nx + 2 * HALO, 8, LANES), jnp.float32),
+            jax.ShapeDtypeStruct(temp.shape, jnp.float32),
+            jax.ShapeDtypeStruct((tall, 8, LANES), jnp.float32),
         ),
-        in_specs=[hbm, hbm] + [vmem] * 4,
+        in_specs=[hbm] * 6 + [vmem] * 2,
         scratch_shapes=[pltpu.VMEM((2, tall, nz // LANES, wide, LANES), jnp.float32)]
-        + heat_scratch(tall, wide, nz)
-        + [pltpu.SemaphoreType.DMA((2, nz // LANES))],
+        + [big] * 5
+        + [
+            pltpu.VMEM((tall, wide, LANES), jnp.float32),
+            pltpu.VMEM((wide, nz), jnp.float32),
+            pltpu.VMEM((nx, nz // LANES, wide, LANES), jnp.float32),
+            pltpu.SemaphoreType.DMA((2, 5, nz // LANES)),
+        ],
         compiler_params=params(64),
         cost_estimate=cost(tall * wide * nz * 100, 12 * nx * ny * nz * 4),
-        name="first_round",
-    )(temp, cond, low, high, below, above)
-
-
-def second_round_kernel(
-    t_ref, low_ref, high_ref, k_ref, out_ref,
-    cond, field, between, gx, gy, gz, gb, carried, placed, sems,
-):
-    nx, wide, nz = t_ref.shape
-    ny = out_ref.shape[1]
-    tiles = wide // 8
-    copies = [
-        pltpu.make_async_copy(k_ref, cond, sems.at[0]),
-        pltpu.make_async_copy(t_ref, field.at[pl.ds(DEPTH, nx)], sems.at[1]),
-        pltpu.make_async_copy(low_ref, field.at[pl.ds(0, DEPTH)], sems.at[2]),
-        pltpu.make_async_copy(high_ref, field.at[pl.ds(DEPTH + nx, DEPTH)], sems.at[3]),
-    ]
-    for copy in copies:
-        copy.start()
-    copies[0].wait()
-    prepare(cond, gx, gy, gz, gb)
-    for copy in copies[1:]:
-        copy.wait()
-
-    def target(x, t, z):
-        return placed, (x - DEPTH, z.start // LANES, pl.ds(t, 8, stride=tiles))
-
-    two_steps(field, between, gx, gy, gz, gb, carried, target)
-
-    @pl.loop(0, nx)
-    def _(x):
-        for j, z in enumerate(lane_tiles(out_ref.shape[2])):
-            out_ref[x, :, z] = placed[x, j, :ny, :]
-
-
-def second_round(temp, low, high, cond, shape):
-    nx, wide, nz = temp.shape
-    tall = cond.shape[0]
-    hbm = pl.BlockSpec(memory_space=pl.ANY)
-    return pl.pallas_call(
-        second_round_kernel,
-        out_shape=jax.ShapeDtypeStruct(shape, jnp.float32),
-        in_specs=[hbm] * 4,
-        scratch_shapes=[pltpu.VMEM((tall, wide, nz), jnp.float32)]
-        + heat_scratch(tall, wide, nz)
-        + [
-            pltpu.VMEM((nx, nz // LANES, wide, LANES), jnp.float32),
-            pltpu.SemaphoreType.DMA((4,)),
-        ],
-        compiler_params=params(64),
-        cost_estimate=cost(tall * wide * nz * 60, 8 * nx * wide * nz * 4),
-        name="second_round",
-    )(temp, low, high, cond)
+        name="heat",
+    )(temp, cond, k_low, k_high, t_low, t_high, below, above)
 
 
 def source_kernel(ny, all_ref, thin_ref, base_ref, out_ref):
@@ -829,25 +743,25 @@
         return term.reshape(count, blocks, BLK)
 
     whole = exchange(copies)
-    send_low, send_high = pack_x(temp, cond)
-    low, high = both_ways(send_low, send_high, "slab")
+    cond, copies = together(cond, copies)
+    send_low, send_high = cond[:HALO], cond[nx - HALO :]
+    k_low, k_high = both_ways(send_low, send_high, "slab")
+    whole = together(whole, send_low, send_high)[0]
+    temp, cond, term = together(temp, cond, sweep_terms(whole))
+    parts = exchange(term)
+    below, above = both_ways(*pack_y(temp, cond), "pair")
+    parts, below, above = together(parts, below, above)
+    copies, below, above = together(middle(parts, emitted, mirror_fraction), below, above)
+    whole = exchange(copies)
+    send_low, send_high = pack_x(temp, below, above)
+    t_low, t_high = both_ways(send_low, send_high, "slab")
     whole = together(whole, send_low, send_high)[0]
     parts = exchange(sweep_terms(whole))
-    copies, low, high = together(middle(parts, emitted, mirror_fraction), low, high)
-    whole = exchange(copies)
-    send_down, send_up = pack_y(temp, cond, low, high)
-    below, above = both_ways(send_down, send_up, "pair")
-    middle_temp, send_low, send_high, strided_cond, thin = first_round(
-        temp, cond, low, high, below, above
-    )
-    low, high = both_ways(send_low, send_high, "slab")
-    whole = together(whole, send_low, send_high)[0]
-    term, low, high = together(sweep_terms(whole), low, high)
-    parts = exchange(term)
-    base = second_round(middle_temp, low, high, strided_cond, temp.shape)
-    parts = together(parts, base)[0]
+    parts, t_low, t_high = together(parts, t_low, t_high)
     radiosity, source = last(parts, emitted, mirror_fraction, element_facing_site, nx * ny, count)
     everything = exchange(source)
+    below, source = together(below, source)
+    base, thin = heat(temp, cond, k_low, k_high, t_low, t_high, below, above)
 
     warmed_liner = add_source(everything, thin, base)
     return (radiosity, warmed_liner)

time: 133 us -> 143 us (1.075)
  blocking collectives: 33.5 us -> 0 us
  waiting for transfers between devices: 7.29 us -> 38.8 us
  starting transfers between devices: 35.6 us -> 49.8 us
  local copies, waits for them, and re-layouts: 4.16 us -> 2.24 us
    all_to_all x2 -> x0, blocking collectives: 33.5 us -> none  [exchange(): lax.all_to_all(rows, ('slab', 'pair'), split_axis=0, concat_axis=0, tiled...]
    ppermute x3, waiting for transfers between devices: 6.31 us -> 24.9 us  [both_ways(): from_low = lax.ppermute(high, axis, forward)]
    all_to_all x3 -> x5, starting transfers between devices: 18.5 us -> 33.3 us  [exchange(): lax.all_to_all(rows, ('slab', 'pair'), split_axis=0, concat_axis=0, tiled...]
    all_to_all x3 -> x5, waiting for transfers between devices: 0.97 us -> 11 us  [exchange(): lax.all_to_all(rows, ('slab', 'pair'), split_axis=0, concat_axis=0, tiled...]
    pallas_call x3 -> x2, Pallas kernels: 31.1 us -> 24.7 us  [the longest x1 22.6 us: heat(): pl.pallas_call(heat_kernel, out_shape=(jax.ShapeDtypeStruct(temp.shape, j...]
    unnamed x16 -> x0, local copies, waits for them, and re-layouts: 4.16 us -> none
    pallas_call x2, Pallas kernels: 9.31 us -> 13.3 us  [tile_terms(): pl.pallas_call(tiles_kernel, out_shape=jax.ShapeDtypeStruct(whole.shape,...]
    ppermute x3, waiting for transfers between devices: 0.01 us -> 2.92 us  [both_ways(): from_high = lax.ppermute(low, axis, backward)]
  transfers between devices with their start and end apart: 9 -> 11, of which waited for: 2 -> 7; matrix products, arithmetic and copies ran while one was open for 0% -> 2% of each run, Pallas kernels for 31% -> 25%
where the time goes in v8:
time: 143 us; the launch traced here: 141 us
  starting transfers between devices  49.8 us (35%)
  Pallas kernels  48.9 us (34%)
  waiting for transfers between devices  38.8 us (27%)
  local copies, waits for them, and re-layouts  2.24 us (2%)
    all_to_all x5, starting transfers between devices, exchange(): lax.all_to_all(rows, ('slab', 'pair'), split_axis=0, concat_axis=0, tiled...  33.3 us
    ppermute x3, waiting for transfers between devices, both_ways(): from_low = lax.ppermute(high, axis, forward)  24.9 us
    pallas_call x1, Pallas kernels, heat(): pl.pallas_call(heat_kernel, out_shape=(jax.ShapeDtypeStruct(temp.shape, j...  22.6 us
    pallas_call x2, Pallas kernels, tile_terms(): pl.pallas_call(tiles_kernel, out_shape=jax.ShapeDtypeStruct(whole.shape,...  13.3 us
    ppermute x3, starting transfers between devices, both_ways(): from_low = lax.ppermute(high, axis, forward)  12.6 us
    all_to_all x5, waiting for transfers between devices, exchange(): lax.all_to_all(rows, ('slab', 'pair'), split_axis=0, concat_axis=0, tiled...  11 us
    ppermute x3, starting transfers between devices, both_ways(): from_high = lax.ppermute(low, axis, backward)  3.84 us
    ppermute x3, waiting for transfers between devices, both_ways(): from_high = lax.ppermute(low, axis, backward)  2.92 us
  transfers between devices with their start and end apart: 11, of which 7 were waited for; matrix products, arithmetic and copies ran while one was open for 2% of the time, Pallas kernels for 25%

profile of v8, /device:TPU:0, one launch (start us, length us, event | category | flops | bytes accessed | tf_op | source)
XLA Modules:
  0.0 141.1 jit_solution(5915389797202587002)
XLA Ops:
  0.6 2.1 %emit.1 = (f32[16,128]{1,0:T(8,128)}, f32[32,16,128]{2,1,0:T(8,128)}) custom-call(f32[16,64,512]{2,1,0:T(8,128)} %t_ref, s32[16,128]{1,0:T(8,128)} %site_ref.3, f32[16,128]{1,0:T(8,128)} %mirror_ref.5), custom_call_target="tpu_custom_call" | custom-call | flops 10000 | bytes 900000 | tf_op jit(solution)/shard_map/emit/pallas_call | solution.py:96
  2.8 7.4 %all-to-all-start = ((f32[32,16,128]{2,1,0:T(8,128)}), f32[32,16,128]{2,1,0:T(8,128)}, u32[]{:S(2)}, u32[]{:S(2)}) async-start(f32[32,16,128]{2,1,0:T(8,128)} %get-tuple-element.32), calls=%async_computation | async-start | bytes 524288 | tf_op jit(solution)/shard_map/all_to_all | solution.py:705
  10.8 2.2 %fusion = (f32[4,64,512]{2,1,0:T(8,128)}, f32[4,64,512]{2,1,0:T(8,128)}) fusion(f32[16,64,512]{2,1,0:T(8,128)} %k_ref), kind=kLoop, calls=%fused_computation | loop fusion | bytes 2097152 | tf_op jit(solution)/shard_map/slice | solution.py:747
  13.1 7.7 %all-to-all-done = f32[32,16,128]{2,1,0:T(8,128)} async-done(((f32[32,16,128]{2,1,0:T(8,128)}), f32[32,16,128]{2,1,0:T(8,128)}, u32[]{:S(2)}, u32[]{:S(2)}) %all-to-all-start) | async-done | bytes 262176 | tf_op jit(solution)/shard_map/all_to_all | solution.py:705
  20.8 6.6 %tiles.2 = f32[512,128]{1,0:T(8,128)} custom-call(s32[1]{0:T(128)S(6)} %copy.11.live_ref, s32[2,256]{1,0:T(2,128)} %bitcast.7, s32[2,256]{1,0:T(2,128)} %bitcast.8, f32[512,128]{1,0:T(8,128)} %bitcast.1.whole_ref, f32[256,128,128]{2,1,0:T(8,128)} %tiles_ref.3), custom_call_target="tpu_custom_call" | custom-call | flops 134217728 | bytes 16777216 | tf_op jit(solution)/shard_map/tiles/pallas_call | solution.py:200
  27.4 6.2 %all-to-all-start.1 = ((f32[32,16,128]{2,1,0:T(8,128)}), f32[32,16,128]{2,1,0:T(8,128)}, u32[]{:S(2)}, u32[]{:S(2)}) async-start(f32[32,16,128]{2,1,0:T(8,128)} %bitcast.5), calls=%async_computation.1 | async-start | bytes 524288 | tf_op jit(solution)/shard_map/all_to_all | solution.py:705
  33.6 2.1 %pack_y.1 = (f32[16,8,512]{2,1,0:T(8,128)}, f32[16,8,512]{2,1,0:T(8,128)}) custom-call(f32[16,64,512]{2,1,0:T(8,128)} %t_ref, f32[16,64,512]{2,1,0:T(8,128)} %k_ref, f32[16,64,512]{2,1,0:T(8,128)} %t_ref, f32[16,64,512]{2,1,0:T(8,128)} %k_ref), custom_call_target="tpu_custom_call" | custom-call | bytes 1048576 | tf_op jit(solution)/shard_map/pack_y/pallas_call | solution.py:297
  35.7 2.8 %collective-permute-start = (f32[16,8,512]{2,1,0:T(8,128)}, f32[16,8,512]{2,1,0:T(8,128)}, u32[]{:S(2)}, u32[]{:S(2)}) collective-permute-start(f32[16,8,512]{2,1,0:T(8,128)} %get-tuple-element.38), channel_id=1, source_target_pairs={{0,1},{1,2},{2,3},{4,5},{5,6},{6,7},{8,9},{9,10},{10,11},{12,13},{... | collective-permute-start | bytes 786440 | tf_op jit(solution)/shard_map/ppermute | solution.py:716
  38.5 1.3 collective-permute-start.1
  39.8 0.0 collective-permute-done.below0.below1.below_ref
  39.8 2.9 %collective-permute-done.1.above0.above1.above_ref = f32[16,8,512]{2,1,0:T(8,128)} collective-permute-done((f32[16,8,512]{2,1,0:T(8,128)}, f32[16,8,512]{2,1,0:T(8,128)}, u32[]{:S(2)}, u32[]{:S(2)}) %collective-permute-start.1) | collective-permute-done | bytes 262176 | tf_op jit(solution)/shard_map/ppermute | solution.py:717
  42.7 1.5 %all-to-all-done.1.parts_ref = f32[32,16,128]{2,1,0:T(8,128)} async-done(((f32[32,16,128]{2,1,0:T(8,128)}), f32[32,16,128]{2,1,0:T(8,128)}, u32[]{:S(2)}, u32[]{:S(2)}) %all-to-all-start.1) | async-done | bytes 262176 | tf_op jit(solution)/shard_map/all_to_all | solution.py:705
  44.2 1.7 %middle.1 = f32[32,16,128]{2,1,0:T(8,128)} custom-call(f32[32,16,128]{2,1,0:T(8,128)} %all-to-all-done.1.parts_ref, f32[16,128]{1,0:T(8,128)} %get-tuple-element.41.emitted_ref, f32[16,128]{1,0:T(8,128)} %mirror_ref.5), custom_call_target="tpu_custom_call" | custom-call | flops 100000 | bytes 600000 | tf_op jit(solution)/shard_map/middle/pallas_call | solution.py:233
  45.9 7.6 %all-to-all-start.2 = ((f32[32,16,128]{2,1,0:T(8,128)}), f32[32,16,128]{2,1,0:T(8,128)}, u32[]{:S(2)}, u32[]{:S(2)}) async-start(f32[32,16,128]{2,1,0:T(8,128)} %middle.1), calls=%async_computation.2 | async-start | bytes 524288 | tf_op jit(solution)/shard_map/all_to_all | solution.py:705
  53.5 2.3 %pack_x.1 = (f32[4,80,512]{2,1,0:T(8,128)}, f32[4,80,512]{2,1,0:T(8,128)}) custom-call(f32[16,64,512]{2,1,0:T(8,128)} %t_ref, f32[16,64,512]{2,1,0:T(8,128)} %t_ref, f32[16,8,512]{2,1,0:T(8,128)} %collective-permute-done.below0.below1.below_ref, f32[16,8,512]{2,1,0:T(8,128)} %collective-permute-done.1.above0.above1.above_ref, ...), custom_call_target="tpu_custom_call" | custom-call | bytes 2621440 | tf_op jit(solution)/shard_map/pack_x/pallas_call | solution.py:335
  55.8 1.3 collective-permute-start.3
  57.1 5.4 %collective-permute-start.2 = (f32[4,80,512]{2,1,0:T(8,128)}, f32[4,80,512]{2,1,0:T(8,128)}, u32[]{:S(2)}, u32[]{:S(2)}) collective-permute-start(f32[4,80,512]{2,1,0:T(8,128)} %get-tuple-element.48), channel_id=1, source_target_pairs={{0,4},{4,8},{8,12},{12,16},{16,20},{20,24},{24,28},{1,5},{5,9},{9,... | collective-permute-start | bytes 1966088 | tf_op jit(solution)/shard_map/ppermute | solution.py:716
  62.6 1.5 %all-to-all-done.2 = f32[32,16,128]{2,1,0:T(8,128)} async-done(((f32[32,16,128]{2,1,0:T(8,128)}), f32[32,16,128]{2,1,0:T(8,128)}, u32[]{:S(2)}, u32[]{:S(2)}) %all-to-all-start.2) | async-done | bytes 262176 | tf_op jit(solution)/shard_map/all_to_all | solution.py:705
  64.1 6.6 %tiles.3 = f32[512,128]{1,0:T(8,128)} custom-call(s32[1]{0:T(128)S(6)} %copy.11.live_ref, s32[2,256]{1,0:T(2,128)} %bitcast.9, s32[2,256]{1,0:T(2,128)} %bitcast.10, f32[512,128]{1,0:T(8,128)} %bitcast.3.whole_ref, f32[256,128,128]{2,1,0:T(8,128)} %tiles_ref.3), custom_call_target="tpu_custom_call" | custom-call | flops 134217728 | bytes 16777216 | tf_op jit(solution)/shard_map/tiles/pallas_call | solution.py:200
  70.7 7.1 %all-to-all-start.3 = ((f32[32,16,128]{2,1,0:T(8,128)}), f32[32,16,128]{2,1,0:T(8,128)}, u32[]{:S(2)}, u32[]{:S(2)}) async-start(f32[32,16,128]{2,1,0:T(8,128)} %bitcast.6), calls=%async_computation.3 | async-start | bytes 524288 | tf_op jit(solution)/shard_map/all_to_all | solution.py:705
  77.9 4.4 %collective-permute-start.4 = (f32[4,64,512]{2,1,0:T(8,128)}, f32[4,64,512]{2,1,0:T(8,128)}, u32[]{:S(2)}, u32[]{:S(2)}) collective-permute-start(f32[4,64,512]{2,1,0:T(8,128)} %get-tuple-element.58), channel_id=1, source_target_pairs={{0,4},{4,8},{8,12},{12,16},{16,20},{20,24},{24,28},{1,5},{5,9},{9,... | collective-permute-start | bytes 1572872 | tf_op jit(solution)/shard_map/ppermute | solution.py:716
  82.3 1.3 collective-permute-start.5
  83.6 0.0 collective-permute-done.3.t_high
  83.6 19.9 %collective-permute-done.2.t_low = f32[4,80,512]{2,1,0:T(8,128)} collective-permute-done((f32[4,80,512]{2,1,0:T(8,128)}, f32[4,80,512]{2,1,0:T(8,128)}, u32[]{:S(2)}, u32[]{:S(2)}) %collective-permute-start.2) | collective-permute-done | bytes 655392 | tf_op jit(solution)/shard_map/ppermute | solution.py:716
  103.4 0.2 all-to-all-done.3.parts_ref
  103.7 2.2 %last.1 = (f32[16,128]{1,0:T(8,128)}, f32[32,8,128]{2,1,0:T(8,128)}) custom-call(f32[32,16,128]{2,1,0:T(8,128)} %all-to-all-done.3.parts_ref, f32[16,128]{1,0:T(8,128)} %get-tuple-element.41.emitted_ref, f32[16,128]{1,0:T(8,128)} %mirror_ref.5, s32[16,128]{1,0:T(8,128)} %site_ref.3), custom_call_target="tpu_custom_call" | custom-call | flops 10000000 | bytes 600000 | tf_op jit(solution)/shard_map/last/pallas_call | solution.py:273
  105.9 5.0 %all-to-all-start.4 = ((f32[32,8,128]{2,1,0:T(8,128)}), f32[32,8,128]{2,1,0:T(8,128)}, u32[]{:S(2)}, u32[]{:S(2)}) async-start(f32[32,8,128]{2,1,0:T(8,128)} %get-tuple-element.52), calls=%async_computation.4 | async-start | bytes 262144 | tf_op jit(solution)/shard_map/all_to_all | solution.py:705
  110.8 5.0 %collective-permute-done.4.k_low = f32[4,64,512]{2,1,0:T(8,128)} collective-permute-done((f32[4,64,512]{2,1,0:T(8,128)}, f32[4,64,512]{2,1,0:T(8,128)}, u32[]{:S(2)}, u32[]{:S(2)}) %collective-permute-start.4) | collective-permute-done | bytes 524320 | tf_op jit(solution)/shard_map/ppermute | solution.py:716
  115.9 0.0 collective-permute-done.5.k_high
  115.9 22.6 %heat.1 = (f32[16,64,512]{2,1,0:T(8,128)}, f32[24,8,128]{2,1,0:T(8,128)}) custom-call(f32[16,64,512]{2,1,0:T(8,128)} %t_ref, f32[16,64,512]{2,1,0:T(8,128)} %k_ref, f32[4,64,512]{2,1,0:T(8,128)} %collective-permute-done.4.k_low, f32[4,64,512]{2,1,0:T(8,128)} %collective-permute-done.5.k_high, f32[4,80,512]{2,1,0:T(8,128)} %collective-permute-done.2.t_low, ...), custom_call_target="tpu_custom_call" | custom-call | flops 88473600 | bytes 25165824 | tf_op jit(solution)/shard_map/heat/pallas_call | solution.py:581
  138.5 0.0 all-to-all-done.4.all_ref
  138.5 2.6 %add_source.1 = f32[16,64,512]{2,1,0:T(8,128)} custom-call(f32[32,8,128]{2,1,0:T(8,128)} %all-to-all-done.4.all_ref, f32[24,8,128]{2,1,0:T(8,128)} %get-tuple-element.56.thin_ref, f32[16,64,512]{2,1,0:T(8,128)} %get-tuple-element.57.base_ref), custom_call_target="tpu_custom_call", output_to_operand_aliasing={{}: (2, {})} | custom-call | flops 1000000 | bytes 1048576 | tf_op jit(solution)/shard_map/add_source/pallas_call | solution.py:687
Async XLA Ops:
  2.8 18.0 %all-to-all-start = ((f32[32,16,128]{2,1,0:T(8,128)}), f32[32,16,128]{2,1,0:T(8,128)}, u32[]{:S(2)}, u32[]{:S(2)}) async-start(f32[32,16,128]{2,1,0:T(8,128)} %get-tuple-element.32), calls=%async_computation | async-start | bytes 524288 | tf_op jit(solution)/shard_map/all_to_all | solution.py:705
  27.4 16.8 %all-to-all-start.1 = ((f32[32,16,128]{2,1,0:T(8,128)}), f32[32,16,128]{2,1,0:T(8,128)}, u32[]{:S(2)}, u32[]{:S(2)}) async-start(f32[32,16,128]{2,1,0:T(8,128)} %bitcast.5), calls=%async_computation.1 | async-start | bytes 524288 | tf_op jit(solution)/shard_map/all_to_all | solution.py:705
  35.7 4.1 %collective-permute-start = (f32[16,8,512]{2,1,0:T(8,128)}, f32[16,8,512]{2,1,0:T(8,128)}, u32[]{:S(2)}, u32[]{:S(2)}) collective-permute-start(f32[16,8,512]{2,1,0:T(8,128)} %get-tuple-element.38), channel_id=1, source_target_pairs={{0,1},{1,2},{2,3},{4,5},{5,6},{6,7},{8,9},{9,10},{10,11},{12,13},{... | collective-permute-start | bytes 786440 | tf_op jit(solution)/shard_map/ppermute | solution.py:716
  38.5 4.2 %collective-permute-start.1 = (f32[16,8,512]{2,1,0:T(8,128)}, f32[16,8,512]{2,1,0:T(8,128)}, u32[]{:S(2)}, u32[]{:S(2)}) collective-permute-start(f32[16,8,512]{2,1,0:T(8,128)} %get-tuple-element.39), channel_id=1, source_target_pairs={{1,0},{2,1},{3,2},{5,4},{6,5},{7,6},{9,8},{10,9},{11,10},{13,12},{... | collective-permute-start | bytes 786440 | tf_op jit(solution)/shard_map/ppermute | solution.py:717
  45.9 18.2 %all-to-all-start.2 = ((f32[32,16,128]{2,1,0:T(8,128)}), f32[32,16,128]{2,1,0:T(8,128)}, u32[]{:S(2)}, u32[]{:S(2)}) async-start(f32[32,16,128]{2,1,0:T(8,128)} %middle.1), calls=%async_computation.2 | async-start | bytes 524288 | tf_op jit(solution)/shard_map/all_to_all | solution.py:705
  55.8 27.7 %collective-permute-start.3 = (f32[4,80,512]{2,1,0:T(8,128)}, f32[4,80,512]{2,1,0:T(8,128)}, u32[]{:S(2)}, u32[]{:S(2)}) collective-permute-start(f32[4,80,512]{2,1,0:T(8,128)} %get-tuple-element.47), channel_id=1, source_target_pairs={{4,0},{8,4},{12,8},{16,12},{20,16},{24,20},{28,24},{5,1},{9,5},{13... | collective-permute-start | bytes 1966088 | tf_op jit(solution)/shard_map/ppermute | solution.py:717
  57.1 46.3 %collective-permute-start.2 = (f32[4,80,512]{2,1,0:T(8,128)}, f32[4,80,512]{2,1,0:T(8,128)}, u32[]{:S(2)}, u32[]{:S(2)}) collective-permute-start(f32[4,80,512]{2,1,0:T(8,128)} %get-tuple-element.48), channel_id=1, source_target_pairs={{0,4},{4,8},{8,12},{12,16},{16,20},{20,24},{24,28},{1,5},{5,9},{9,... | collective-permute-start | bytes 1966088 | tf_op jit(solution)/shard_map/ppermute | solution.py:716
  70.7 33.0 %all-to-all-start.3 = ((f32[32,16,128]{2,1,0:T(8,128)}), f32[32,16,128]{2,1,0:T(8,128)}, u32[]{:S(2)}, u32[]{:S(2)}) async-start(f32[32,16,128]{2,1,0:T(8,128)} %bitcast.6), calls=%async_computation.3 | async-start | bytes 524288 | tf_op jit(solution)/shard_map/all_to_all | solution.py:705
  77.9 38.0 %collective-permute-start.4 = (f32[4,64,512]{2,1,0:T(8,128)}, f32[4,64,512]{2,1,0:T(8,128)}, u32[]{:S(2)}, u32[]{:S(2)}) collective-permute-start(f32[4,64,512]{2,1,0:T(8,128)} %get-tuple-element.58), channel_id=1, source_target_pairs={{0,4},{4,8},{8,12},{12,16},{16,20},{20,24},{24,28},{1,5},{5,9},{9,... | collective-permute-start | bytes 1572872 | tf_op jit(solution)/shard_map/ppermute | solution.py:716
  82.3 33.6 %collective-permute-start.5 = (f32[4,64,512]{2,1,0:T(8,128)}, f32[4,64,512]{2,1,0:T(8,128)}, u32[]{:S(2)}, u32[]{:S(2)}) collective-permute-start(f32[4,64,512]{2,1,0:T(8,128)} %get-tuple-element.59), channel_id=1, source_target_pairs={{4,0},{8,4},{12,8},{16,12},{20,16},{24,20},{28,24},{5,1},{9,5},{13... | collective-permute-start | bytes 1572872 | tf_op jit(solution)/shard_map/ppermute | solution.py:717
  105.9 32.6 %all-to-all-start.4 = ((f32[32,8,128]{2,1,0:T(8,128)}), f32[32,8,128]{2,1,0:T(8,128)}, u32[]{:S(2)}, u32[]{:S(2)}) async-start(f32[32,8,128]{2,1,0:T(8,128)} %get-tuple-element.52), calls=%async_computation.4 | async-start | bytes 262144 | tf_op jit(solution)/shard_map/all_to_all | solution.py:705

commit v9 on v8

--- a/solution.py
+++ b/solution.py
@@ -750,7 +750,7 @@
     temp, cond, term = together(temp, cond, sweep_terms(whole))
     parts = exchange(term)
     below, above = both_ways(*pack_y(temp, cond), "pair")
-    parts, below, above = together(parts, below, above)
+    parts, below, above, k_low, k_high = together(parts, below, above, k_low, k_high)
     copies, below, above = together(middle(parts, emitted, mirror_fraction), below, above)
     whole = exchange(copies)
     send_low, send_high = pack_x(temp, below, above)

time: 143 us -> 127 us (0.89); the launches traced: 141 us -> 129 us
  waiting for transfers between devices: 38.8 us -> 21.6 us
  starting transfers between devices: 49.8 us -> 54.7 us
    ppermute x3, waiting for transfers between devices: 24.9 us -> 13.5 us  [both_ways(): from_low = lax.ppermute(high, axis, forward)]
    all_to_all x5, waiting for transfers between devices: 11 us -> 5.21 us  [exchange(): lax.all_to_all(rows, ('slab', 'pair'), split_axis=0, concat_axis=0, tiled...]
    all_to_all x5, starting transfers between devices: 33.3 us -> 38.3 us  [exchange(): lax.all_to_all(rows, ('slab', 'pair'), split_axis=0, concat_axis=0, tiled...]
  transfers between devices with their start and end apart: 11 -> 11, of which waited for: 7 -> 6; matrix products, arithmetic and copies ran while one was open for 2% -> 2% of each run, Pallas kernels for 25% -> 31%
where the time goes in v9:
time: 127 us; the launch traced here: 129 us
  starting transfers between devices  54.7 us (43%)
  Pallas kernels  48.8 us (38%)
  waiting for transfers between devices  21.6 us (17%)
  local copies, waits for them, and re-layouts  2.25 us (2%)
  between operations  1.41 us (1%)
    all_to_all x5, starting transfers between devices, exchange(): lax.all_to_all(rows, ('slab', 'pair'), split_axis=0, concat_axis=0, tiled...  38.3 us
    pallas_call x1, Pallas kernels, heat(): pl.pallas_call(heat_kernel, out_shape=(jax.ShapeDtypeStruct(temp.shape, j...  22.6 us
    ppermute x3, waiting for transfers between devices, both_ways(): from_low = lax.ppermute(high, axis, forward)  13.5 us
    pallas_call x2, Pallas kernels, tile_terms(): pl.pallas_call(tiles_kernel, out_shape=jax.ShapeDtypeStruct(whole.shape,...  13.2 us
    ppermute x3, starting transfers between devices, both_ways(): from_low = lax.ppermute(high, axis, forward)  12.6 us
    all_to_all x5, waiting for transfers between devices, exchange(): lax.all_to_all(rows, ('slab', 'pair'), split_axis=0, concat_axis=0, tiled...  5.21 us
    ppermute x3, starting transfers between devices, both_ways(): from_high = lax.ppermute(low, axis, backward)  3.84 us
    ppermute x3, waiting for transfers between devices, both_ways(): from_high = lax.ppermute(low, axis, backward)  2.89 us
  transfers between devices with their start and end apart: 11, of which 6 were waited for; matrix products, arithmetic and copies ran while one was open for 2% of the time, Pallas kernels for 31%

profile of v9, /device:TPU:0, one launch (start us, length us, event | category | flops | bytes accessed | tf_op | source)
XLA Modules:
  0.0 128.9 jit_solution(18433819317096738624)
XLA Ops:
  0.6 2.1 %emit.1 = (f32[16,128]{1,0:T(8,128)}, f32[32,16,128]{2,1,0:T(8,128)}) custom-call(f32[16,64,512]{2,1,0:T(8,128)} %t_ref, s32[16,128]{1,0:T(8,128)} %site_ref.3, f32[16,128]{1,0:T(8,128)} %mirror_ref.5), custom_call_target="tpu_custom_call" | custom-call | flops 10000 | bytes 900000 | tf_op jit(solution)/shard_map/emit/pallas_call | solution.py:96
  2.8 7.4 %all-to-all-start = ((f32[32,16,128]{2,1,0:T(8,128)}), f32[32,16,128]{2,1,0:T(8,128)}, u32[]{:S(2)}, u32[]{:S(2)}) async-start(f32[32,16,128]{2,1,0:T(8,128)} %get-tuple-element.34), calls=%async_computation | async-start | bytes 524288 | tf_op jit(solution)/shard_map/all_to_all | solution.py:705
  10.2 2.2 %fusion = (f32[4,64,512]{2,1,0:T(8,128)}, f32[4,64,512]{2,1,0:T(8,128)}) fusion(f32[16,64,512]{2,1,0:T(8,128)} %k_ref), kind=kLoop, calls=%fused_computation | loop fusion | bytes 2097152 | tf_op jit(solution)/shard_map/slice | solution.py:747
  12.4 4.4 %collective-permute-start.2 = (f32[4,64,512]{2,1,0:T(8,128)}, f32[4,64,512]{2,1,0:T(8,128)}, u32[]{:S(2)}, u32[]{:S(2)}) collective-permute-start(f32[4,64,512]{2,1,0:T(8,128)} %get-tuple-element.62), channel_id=1, source_target_pairs={{0,4},{4,8},{8,12},{12,16},{16,20},{20,24},{24,28},{1,5},{5,9},{9,... | collective-permute-start | bytes 1572872 | tf_op jit(solution)/shard_map/ppermute | solution.py:716
  16.8 1.3 collective-permute-start.3
  18.8 2.0 %all-to-all-done = f32[32,16,128]{2,1,0:T(8,128)} async-done(((f32[32,16,128]{2,1,0:T(8,128)}), f32[32,16,128]{2,1,0:T(8,128)}, u32[]{:S(2)}, u32[]{:S(2)}) %all-to-all-start) | async-done | bytes 262176 | tf_op jit(solution)/shard_map/all_to_all | solution.py:705
  20.8 6.6 %tiles.2 = f32[512,128]{1,0:T(8,128)} custom-call(s32[1]{0:T(128)S(6)} %copy.11.live_ref, s32[2,256]{1,0:T(2,128)} %bitcast.7, s32[2,256]{1,0:T(2,128)} %bitcast.8, f32[512,128]{1,0:T(8,128)} %bitcast.1.whole_ref, f32[256,128,128]{2,1,0:T(8,128)} %tiles_ref.3), custom_call_target="tpu_custom_call" | custom-call | flops 134217728 | bytes 16777216 | tf_op jit(solution)/shard_map/tiles/pallas_call | solution.py:200
  27.4 10.3 %all-to-all-start.1 = ((f32[32,16,128]{2,1,0:T(8,128)}), f32[32,16,128]{2,1,0:T(8,128)}, u32[]{:S(2)}, u32[]{:S(2)}) async-start(f32[32,16,128]{2,1,0:T(8,128)} %bitcast.5), calls=%async_computation.1 | async-start | bytes 524288 | tf_op jit(solution)/shard_map/all_to_all | solution.py:705
  37.7 2.1 %pack_y.1 = (f32[16,8,512]{2,1,0:T(8,128)}, f32[16,8,512]{2,1,0:T(8,128)}) custom-call(f32[16,64,512]{2,1,0:T(8,128)} %t_ref, f32[16,64,512]{2,1,0:T(8,128)} %k_ref, f32[16,64,512]{2,1,0:T(8,128)} %t_ref, f32[16,64,512]{2,1,0:T(8,128)} %k_ref), custom_call_target="tpu_custom_call" | custom-call | bytes 1048576 | tf_op jit(solution)/shard_map/pack_y/pallas_call | solution.py:297
  39.8 2.8 %collective-permute-start = (f32[16,8,512]{2,1,0:T(8,128)}, f32[16,8,512]{2,1,0:T(8,128)}, u32[]{:S(2)}, u32[]{:S(2)}) collective-permute-start(f32[16,8,512]{2,1,0:T(8,128)} %get-tuple-element.40), channel_id=1, source_target_pairs={{0,1},{1,2},{2,3},{4,5},{5,6},{6,7},{8,9},{9,10},{10,11},{12,13},{... | collective-permute-start | bytes 786440 | tf_op jit(solution)/shard_map/ppermute | solution.py:716
  42.5 1.3 collective-permute-start.1
  43.8 0.0 collective-permute-done.2.k_low
  43.8 0.0 collective-permute-done.3.k_high
  43.8 0.0 collective-permute-done.below0.below1.below_ref
  43.9 2.9 %collective-permute-done.1.above0.above1.above_ref = f32[16,8,512]{2,1,0:T(8,128)} collective-permute-done((f32[16,8,512]{2,1,0:T(8,128)}, f32[16,8,512]{2,1,0:T(8,128)}, u32[]{:S(2)}, u32[]{:S(2)}) %collective-permute-start.1) | collective-permute-done | bytes 262176 | tf_op jit(solution)/shard_map/ppermute | solution.py:717
  46.7 1.5 %all-to-all-done.1.parts_ref = f32[32,16,128]{2,1,0:T(8,128)} async-done(((f32[32,16,128]{2,1,0:T(8,128)}), f32[32,16,128]{2,1,0:T(8,128)}, u32[]{:S(2)}, u32[]{:S(2)}) %all-to-all-start.1) | async-done | bytes 262176 | tf_op jit(solution)/shard_map/all_to_all | solution.py:705
  48.3 1.7 %middle.1 = f32[32,16,128]{2,1,0:T(8,128)} custom-call(f32[32,16,128]{2,1,0:T(8,128)} %all-to-all-done.1.parts_ref, f32[16,128]{1,0:T(8,128)} %get-tuple-element.43.emitted_ref, f32[16,128]{1,0:T(8,128)} %mirror_ref.5), custom_call_target="tpu_custom_call" | custom-call | flops 100000 | bytes 600000 | tf_op jit(solution)/shard_map/middle/pallas_call | solution.py:233
  50.0 7.6 %all-to-all-start.2 = ((f32[32,16,128]{2,1,0:T(8,128)}), f32[32,16,128]{2,1,0:T(8,128)}, u32[]{:S(2)}, u32[]{:S(2)}) async-start(f32[32,16,128]{2,1,0:T(8,128)} %middle.1), calls=%async_computation.2 | async-start | bytes 524288 | tf_op jit(solution)/shard_map/all_to_all | solution.py:705
  57.6 2.3 %pack_x.1 = (f32[4,80,512]{2,1,0:T(8,128)}, f32[4,80,512]{2,1,0:T(8,128)}) custom-call(f32[16,64,512]{2,1,0:T(8,128)} %t_ref, f32[16,64,512]{2,1,0:T(8,128)} %t_ref, f32[16,8,512]{2,1,0:T(8,128)} %collective-permute-done.below0.below1.below_ref, f32[16,8,512]{2,1,0:T(8,128)} %collective-permute-done.1.above0.above1.above_ref, ...), custom_call_target="tpu_custom_call" | custom-call | bytes 2621440 | tf_op jit(solution)/shard_map/pack_x/pallas_call | solution.py:335
  59.9 1.3 collective-permute-start.5
  61.2 5.4 %collective-permute-start.4 = (f32[4,80,512]{2,1,0:T(8,128)}, f32[4,80,512]{2,1,0:T(8,128)}, u32[]{:S(2)}, u32[]{:S(2)}) collective-permute-start(f32[4,80,512]{2,1,0:T(8,128)} %get-tuple-element.50), channel_id=1, source_target_pairs={{0,4},{4,8},{8,12},{12,16},{16,20},{20,24},{24,28},{1,5},{5,9},{9,... | collective-permute-start | bytes 1966088 | tf_op jit(solution)/shard_map/ppermute | solution.py:716
  66.6 1.5 %all-to-all-done.2 = f32[32,16,128]{2,1,0:T(8,128)} async-done(((f32[32,16,128]{2,1,0:T(8,128)}), f32[32,16,128]{2,1,0:T(8,128)}, u32[]{:S(2)}, u32[]{:S(2)}) %all-to-all-start.2) | async-done | bytes 262176 | tf_op jit(solution)/shard_map/all_to_all | solution.py:705
  68.1 6.6 %tiles.3 = f32[512,128]{1,0:T(8,128)} custom-call(s32[1]{0:T(128)S(6)} %copy.11.live_ref, s32[2,256]{1,0:T(2,128)} %bitcast.9, s32[2,256]{1,0:T(2,128)} %bitcast.10, f32[512,128]{1,0:T(8,128)} %bitcast.3.whole_ref, f32[256,128,128]{2,1,0:T(8,128)} %tiles_ref.3), custom_call_target="tpu_custom_call" | custom-call | flops 134217728 | bytes 16777216 | tf_op jit(solution)/shard_map/tiles/pallas_call | solution.py:200
  74.7 8.0 %all-to-all-start.3 = ((f32[32,16,128]{2,1,0:T(8,128)}), f32[32,16,128]{2,1,0:T(8,128)}, u32[]{:S(2)}, u32[]{:S(2)}) async-start(f32[32,16,128]{2,1,0:T(8,128)} %bitcast.6), calls=%async_computation.3 | async-start | bytes 524288 | tf_op jit(solution)/shard_map/all_to_all | solution.py:705
  82.7 0.0 collective-permute-done.5.t_high
  82.7 13.5 %collective-permute-done.4.t_low = f32[4,80,512]{2,1,0:T(8,128)} collective-permute-done((f32[4,80,512]{2,1,0:T(8,128)}, f32[4,80,512]{2,1,0:T(8,128)}, u32[]{:S(2)}, u32[]{:S(2)}) %collective-permute-start.4) | collective-permute-done | bytes 655392 | tf_op jit(solution)/shard_map/ppermute | solution.py:716
  96.3 0.2 all-to-all-done.3.parts_ref
  96.4 2.2 %last.1 = (f32[16,128]{1,0:T(8,128)}, f32[32,8,128]{2,1,0:T(8,128)}) custom-call(f32[32,16,128]{2,1,0:T(8,128)} %all-to-all-done.3.parts_ref, f32[16,128]{1,0:T(8,128)} %get-tuple-element.43.emitted_ref, f32[16,128]{1,0:T(8,128)} %mirror_ref.5, s32[16,128]{1,0:T(8,128)} %site_ref.3), custom_call_target="tpu_custom_call" | custom-call | flops 10000000 | bytes 600000 | tf_op jit(solution)/shard_map/last/pallas_call | solution.py:273
  98.6 5.1 %all-to-all-start.4 = ((f32[32,8,128]{2,1,0:T(8,128)}), f32[32,8,128]{2,1,0:T(8,128)}, u32[]{:S(2)}, u32[]{:S(2)}) async-start(f32[32,8,128]{2,1,0:T(8,128)} %get-tuple-element.54), calls=%async_computation.4 | async-start | bytes 262144 | tf_op jit(solution)/shard_map/all_to_all | solution.py:705
  103.6 22.6 %heat.1 = (f32[16,64,512]{2,1,0:T(8,128)}, f32[24,8,128]{2,1,0:T(8,128)}) custom-call(f32[16,64,512]{2,1,0:T(8,128)} %t_ref, f32[16,64,512]{2,1,0:T(8,128)} %k_ref, f32[4,64,512]{2,1,0:T(8,128)} %collective-permute-done.2.k_low, f32[4,64,512]{2,1,0:T(8,128)} %collective-permute-done.3.k_high, f32[4,80,512]{2,1,0:T(8,128)} %collective-permute-done.4.t_low, ...), custom_call_target="tpu_custom_call" | custom-call | flops 88473600 | bytes 25165824 | tf_op jit(solution)/shard_map/heat/pallas_call | solution.py:581
  126.2 0.0 all-to-all-done.4.all_ref
  126.3 2.6 %add_source.1 = f32[16,64,512]{2,1,0:T(8,128)} custom-call(f32[32,8,128]{2,1,0:T(8,128)} %all-to-all-done.4.all_ref, f32[24,8,128]{2,1,0:T(8,128)} %get-tuple-element.60.thin_ref, f32[16,64,512]{2,1,0:T(8,128)} %get-tuple-element.61.base_ref), custom_call_target="tpu_custom_call", output_to_operand_aliasing={{}: (2, {})} | custom-call | flops 1000000 | bytes 1048576 | tf_op jit(solution)/shard_map/add_source/pallas_call | solution.py:687
Async XLA Ops:
  2.8 18.0 %all-to-all-start = ((f32[32,16,128]{2,1,0:T(8,128)}), f32[32,16,128]{2,1,0:T(8,128)}, u32[]{:S(2)}, u32[]{:S(2)}) async-start(f32[32,16,128]{2,1,0:T(8,128)} %get-tuple-element.34), calls=%async_computation | async-start | bytes 524288 | tf_op jit(solution)/shard_map/all_to_all | solution.py:705
  12.4 31.4 %collective-permute-start.2 = (f32[4,64,512]{2,1,0:T(8,128)}, f32[4,64,512]{2,1,0:T(8,128)}, u32[]{:S(2)}, u32[]{:S(2)}) collective-permute-start(f32[4,64,512]{2,1,0:T(8,128)} %get-tuple-element.62), channel_id=1, source_target_pairs={{0,4},{4,8},{8,12},{12,16},{16,20},{20,24},{24,28},{1,5},{5,9},{9,... | collective-permute-start | bytes 1572872 | tf_op jit(solution)/shard_map/ppermute | solution.py:716
  16.8 27.0 %collective-permute-start.3 = (f32[4,64,512]{2,1,0:T(8,128)}, f32[4,64,512]{2,1,0:T(8,128)}, u32[]{:S(2)}, u32[]{:S(2)}) collective-permute-start(f32[4,64,512]{2,1,0:T(8,128)} %get-tuple-element.63), channel_id=1, source_target_pairs={{4,0},{8,4},{12,8},{16,12},{20,16},{24,20},{28,24},{5,1},{9,5},{13... | collective-permute-start | bytes 1572872 | tf_op jit(solution)/shard_map/ppermute | solution.py:717
  27.4 20.9 %all-to-all-start.1 = ((f32[32,16,128]{2,1,0:T(8,128)}), f32[32,16,128]{2,1,0:T(8,128)}, u32[]{:S(2)}, u32[]{:S(2)}) async-start(f32[32,16,128]{2,1,0:T(8,128)} %bitcast.5), calls=%async_computation.1 | async-start | bytes 524288 | tf_op jit(solution)/shard_map/all_to_all | solution.py:705
  39.8 4.1 %collective-permute-start = (f32[16,8,512]{2,1,0:T(8,128)}, f32[16,8,512]{2,1,0:T(8,128)}, u32[]{:S(2)}, u32[]{:S(2)}) collective-permute-start(f32[16,8,512]{2,1,0:T(8,128)} %get-tuple-element.40), channel_id=1, source_target_pairs={{0,1},{1,2},{2,3},{4,5},{5,6},{6,7},{8,9},{9,10},{10,11},{12,13},{... | collective-permute-start | bytes 786440 | tf_op jit(solution)/shard_map/ppermute | solution.py:716
  42.5 4.2 %collective-permute-start.1 = (f32[16,8,512]{2,1,0:T(8,128)}, f32[16,8,512]{2,1,0:T(8,128)}, u32[]{:S(2)}, u32[]{:S(2)}) collective-permute-start(f32[16,8,512]{2,1,0:T(8,128)} %get-tuple-element.41), channel_id=1, source_target_pairs={{1,0},{2,1},{3,2},{5,4},{6,5},{7,6},{9,8},{10,9},{11,10},{13,12},{... | collective-permute-start | bytes 786440 | tf_op jit(solution)/shard_map/ppermute | solution.py:717
  50.0 18.2 %all-to-all-start.2 = ((f32[32,16,128]{2,1,0:T(8,128)}), f32[32,16,128]{2,1,0:T(8,128)}, u32[]{:S(2)}, u32[]{:S(2)}) async-start(f32[32,16,128]{2,1,0:T(8,128)} %middle.1), calls=%async_computation.2 | async-start | bytes 524288 | tf_op jit(solution)/shard_map/all_to_all | solution.py:705
  59.9 22.8 %collective-permute-start.5 = (f32[4,80,512]{2,1,0:T(8,128)}, f32[4,80,512]{2,1,0:T(8,128)}, u32[]{:S(2)}, u32[]{:S(2)}) collective-permute-start(f32[4,80,512]{2,1,0:T(8,128)} %get-tuple-element.49), channel_id=1, source_target_pairs={{4,0},{8,4},{12,8},{16,12},{20,16},{24,20},{28,24},{5,1},{9,5},{13... | collective-permute-start | bytes 1966088 | tf_op jit(solution)/shard_map/ppermute | solution.py:717
  61.2 35.1 %collective-permute-start.4 = (f32[4,80,512]{2,1,0:T(8,128)}, f32[4,80,512]{2,1,0:T(8,128)}, u32[]{:S(2)}, u32[]{:S(2)}) collective-permute-start(f32[4,80,512]{2,1,0:T(8,128)} %get-tuple-element.50), channel_id=1, source_target_pairs={{0,4},{4,8},{8,12},{12,16},{16,20},{20,24},{24,28},{1,5},{5,9},{9,... | collective-permute-start | bytes 1966088 | tf_op jit(solution)/shard_map/ppermute | solution.py:716
  74.7 21.7 %all-to-all-start.3 = ((f32[32,16,128]{2,1,0:T(8,128)}), f32[32,16,128]{2,1,0:T(8,128)}, u32[]{:S(2)}, u32[]{:S(2)}) async-start(f32[32,16,128]{2,1,0:T(8,128)} %bitcast.6), calls=%async_computation.3 | async-start | bytes 524288 | tf_op jit(solution)/shard_map/all_to_all | solution.py:705
  98.6 27.7 %all-to-all-start.4 = ((f32[32,8,128]{2,1,0:T(8,128)}), f32[32,8,128]{2,1,0:T(8,128)}, u32[]{:S(2)}, u32[]{:S(2)}) async-start(f32[32,8,128]{2,1,0:T(8,128)} %get-tuple-element.54), calls=%async_computation.4 | async-start | bytes 262144 | tf_op jit(solution)/shard_map/all_to_all | solution.py:705

commit v10 on v9

--- a/solution.py
+++ b/solution.py
@@ -14,7 +14,7 @@
 ROWS = STEPS
 LANES = 128
 CHUNK = 16
-LAG = 12
+LAG = 8
 
 step_size = 0.07
 
@@ -357,92 +357,94 @@
     return [slice(j * LANES, (j + 1) * LANES) for j in range(nz // LANES)]
 
 
-def prepare(cond, gx, gy, gz, gb):
-    tall, wide, nz = cond.shape
-    tiles = wide // 8
-    lane = lax.broadcasted_iota(jnp.int32, (8, LANES), 1)
-    half = 0.5 * step_size
-
-    @pl.loop(0, tall)
-    def _(x):
-        after = jnp.minimum(x + 1, tall - 1)
-        stores = Lagging(LAG)
-        for z in lane_tiles(nz):
-            last = z.stop == nz
-            for t in range(tiles):
-                rows = slice(8 * t, 8 * t + 8)
-                here = cond[x, rows, z]
-                stores.add(put(gx, (x, rows, z), half * (here + cond[after, rows, z])))
-                if t + 1 < tiles:
-                    beside = cond[x, 8 * t + 8 : 8 * t + 16, z]
-                else:
-                    beside = pltpu.roll(cond[x, :8, z], 7, 0)
-                stores.add(put(gy, (x, rows, z), half * (here + beside)))
-                turned = pltpu.roll(here, LANES - 1, 1)
-                if last:
-                    deeper = here
-                else:
-                    deeper = pltpu.roll(cond[x, rows, z.stop : z.stop + LANES], LANES - 1, 1)
-                deeper = jnp.where(lane < LANES - 1, turned, deeper)
-                stores.add(put(gz, (x, rows, z), half * (here + deeper)))
-                if z.start == 0:
-                    stores.add(put(gb, (x, rows), step_size * here))
-        stores.finish()
-
-
-def one_step(field, begin, end, target, gx, gy, gz, gb, carried):
+def one_step(field, cond, begin, end, target, carried):
     wide, nz = field.shape[1:]
     tiles = wide // 8
+    spans = lane_tiles(nz)
+    count = len(spans)
     lane = lax.broadcasted_iota(jnp.int32, (8, LANES), 1)
     sub = lax.broadcasted_iota(jnp.int32, (8, LANES), 0)
     _, _, has_below, has_above = neighbours()
     keep_above = (sub < 7) | has_above
     keep_below = (sub < 7) | has_below
 
-    carried[...] = gx[begin - 1] * (field[begin] - field[begin - 1])
-
-    @pl.loop(begin, end)
-    def _(x):
-        here, across_y = {}, {}
+    carried[...] = (cond[begin - 1] + cond[begin]) * (field[begin] - field[begin - 1])
+
+    def row_tile(ref, x, t):
+        return [ref[x, 8 * t : 8 * t + 8, z] for z in spans]
+
+    def first_rolled(ref, x):
+        return [pltpu.roll(v, 7, 0) for v in row_tile(ref, x, 0)]
+
+    def y_flux(t_now, k_now, t_next, k_next):
+        return [
+            (k_now[j] + k_next[j]) * (t_next[j] - t_now[j]) for j in range(count)
+        ]
+
+    def z_change(t_now, k_now):
+        t_turned = [pltpu.roll(v, LANES - 1, 1) for v in t_now]
+        k_turned = [pltpu.roll(v, LANES - 1, 1) for v in k_now]
+        flux = []
+        for j in range(count):
+            t_deep = t_turned[j + 1] if j + 1 < count else 0.0
+            k_deep = k_turned[j + 1] if j + 1 < count else k_now[j]
+            t_deep = jnp.where(lane < LANES - 1, t_turned[j], t_deep)
+            k_deep = jnp.where(lane < LANES - 1, k_turned[j], k_deep)
+            flux.append((k_now[j] + k_deep) * (t_deep - t_now[j]))
+        back = [pltpu.roll(f, 1, 1) for f in flux]
+        out = []
+        for j in range(count):
+            low = back[j - 1] if j else (k_now[0] + k_now[0]) * t_now[0]
+            out.append(flux[j] - jnp.where(lane > 0, back[j], low))
+        return out
+
+    @pl.loop(begin, end, step=2)
+    def _(base):
         stores = Lagging(LAG)
-        spans = lane_tiles(nz)
-        count = len(spans)
-
-        def tile(t, j):
-            if (t, j) not in here:
-                here[t, j] = field[x, 8 * t : 8 * t + 8, spans[j]]
-            return here[t, j]
-
-        def y_flux(t, j):
-            if (t, j) not in across_y:
-                if t + 1 < tiles:
-                    beside = tile(t + 1, j)
-                else:
-                    beside = pltpu.roll(tile(0, j), 7, 0)
-                across_y[t, j] = gy[x, 8 * t : 8 * t + 8, spans[j]] * (beside - tile(t, j))
-            return across_y[t, j]
-
+        planes = (base, base + 1)
+        low_y = []
+        for x in planes:
+            final = y_flux(
+                row_tile(field, x, tiles - 1),
+                row_tile(cond, x, tiles - 1),
+                first_rolled(field, x),
+                first_rolled(cond, x),
+            )
+            low_y.append([pltpu.roll(f, 1, 0) for f in final])
+        t_now = [row_tile(field, x, 0) for x in planes]
+        k_now = [row_tile(cond, x, 0) for x in planes]
         for t in range(tiles):
             rows = slice(8 * t, 8 * t + 8)
-            turned = [pltpu.roll(tile(t, j), LANES - 1, 1) for j in range(count)]
-            flux = []
-            for j in range(count):
-                deeper = turned[j + 1] if j + 1 < count else 0.0
-                deeper = jnp.where(lane < LANES - 1, turned[j], deeper)
-                flux.append(gz[x, rows, spans[j]] * (deeper - tile(t, j)))
-            back = [pltpu.roll(f, 1, 1) for f in flux]
-            for j in range(count):
-                now = tile(t, j)
-                low_z = back[j - 1] if j else gb[x, rows, :] * now
-                low_z = jnp.where(lane > 0, back[j], low_z)
-                x_flux = gx[x, rows, spans[j]] * (field[x + 1, rows, spans[j]] - now)
-                low_x = carried[rows, spans[j]]
-                stores.add(put(carried, (rows, spans[j]), x_flux))
-                low_y = y_flux(t - 1, j) if t else pltpu.roll(y_flux(tiles - 1, j), 1, 0)
-                new = now + (x_flux - low_x) + (y_flux(t, j) - low_y) + (flux[j] - low_z)
-                if t:
-                    new = jnp.where(keep_above if t <= ROWS else keep_below, new, 0.0)
-                stores.add(put(*target(x, t, spans[j]), new))
+            if t + 1 < tiles:
+                t_next = [row_tile(field, x, t + 1) for x in planes]
+                k_next = [row_tile(cond, x, t + 1) for x in planes]
+            else:
+                t_next = [first_rolled(field, x) for x in planes]
+                k_next = [first_rolled(cond, x) for x in planes]
+            total = []
+            for p in range(2):
+                high_y = y_flux(t_now[p], k_now[p], t_next[p], k_next[p])
+                change_z = z_change(t_now[p], k_now[p])
+                total.append(
+                    [
+                        t_now[p][j] + (high_y[j] - low_y[p][j]) + change_z[j]
+                        for j in range(count)
+                    ]
+                )
+                low_y[p] = high_y
+            for j, z in enumerate(spans):
+                low_x = carried[rows, z]
+                mid_x = (k_now[0][j] + k_now[1][j]) * (t_now[1][j] - t_now[0][j])
+                high_x = (k_now[1][j] + cond[base + 2, rows, z]) * (
+                    field[base + 2, rows, z] - t_now[1][j]
+                )
+                stores.add(put(carried, (rows, z), high_x))
+                for p, change_x in enumerate((mid_x - low_x, high_x - mid_x)):
+                    new = total[p][j] + change_x
+                    if t:
+                        new = jnp.where(keep_above if t <= ROWS else keep_below, new, 0.0)
+                    stores.add(put(*target(base + p, t, z), new))
+            t_now, k_now = t_next, k_next
         stores.finish()
 
 
@@ -471,7 +473,7 @@
 
 def heat_kernel(
     t_ref, k_ref, k_low, k_high, t_low, t_high, below_ref, above_ref, out_ref, thin_ref,
-    loaded, field, between, gx, gy, gz, gb, carried, placed, sems,
+    loaded, field, between, faces, carried, placed, sems,
 ):
     nx, ny, nz = t_ref.shape
     tall, wide = nx + 2 * HALO, ny + 2 * ROWS
@@ -535,22 +537,19 @@
     def _():
         raw_k[HALO + nx] = raw_k[HALO + nx - 1]
 
-    def spread(which, target):
+    def spread(which, target, scale):
         @pl.loop(0, tall)
         def _(x):
             for t in range(tiles):
                 rows = pl.ds(t, 8, stride=tiles)
                 for j, z in enumerate(spans):
-                    target[x, 8 * t : 8 * t + 8, z] = loaded[which, x, j, rows, :]
-
-    spread(1, between)
-    prepare(between, gx, gy, gz, gb)
+                    value = loaded[which, x, j, rows, :]
+                    target[x, 8 * t : 8 * t + 8, z] = value if scale is None else scale * value
+
+    spread(1, faces, 0.5 * step_size)
     for copy in t_copies:
         copy.wait()
-    spread(0, field)
-
-    for x in (HALO - 1, HALO + nx):
-        between[x] = jnp.zeros((wide, nz), jnp.float32)
+    spread(0, field, None)
 
     def inside(target):
         return lambda x, t, z: (target, (x, slice(8 * t, 8 * t + 8), z))
@@ -560,11 +559,15 @@
 
     old, new = field, between
     for step in range(1, STEPS):
-        begin = jnp.where(has_low, step, HALO)
-        end = jnp.where(has_high, tall - step, tall - HALO)
-        one_step(old, begin, end, inside(new), gx, gy, gz, gb, carried)
+        one_step(old, faces, step, tall - step, inside(new), carried)
+        for x, there in ((HALO - 1, has_low), (HALO + nx, has_high)):
+
+            @pl.when(jnp.logical_not(there))
+            def _():
+                new[x] = jnp.zeros((wide, nz), jnp.float32)
+
         old, new = new, old
-    one_step(old, HALO, tall - HALO, outside, gx, gy, gz, gb, carried)
+    one_step(old, faces, HALO, tall - HALO, outside, carried)
 
     @pl.loop(0, nx)
     def _(x):
@@ -586,9 +589,8 @@
         ),
         in_specs=[hbm] * 6 + [vmem] * 2,
         scratch_shapes=[pltpu.VMEM((2, tall, nz // LANES, wide, LANES), jnp.float32)]
-        + [big] * 5
+        + [big] * 3
         + [
-            pltpu.VMEM((tall, wide, LANES), jnp.float32),
             pltpu.VMEM((wide, nz), jnp.float32),
             pltpu.VMEM((nx, nz // LANES, wide, LANES), jnp.float32),
             pltpu.SemaphoreType.DMA((2, 5, nz // LANES)),

time: 127 us -> 142 us (1.12); the launches traced: 129 us -> 141 us
  Pallas kernels: 48.8 us -> 73.7 us
  starting transfers between devices: 54.7 us -> 43 us
    pallas_call x1, Pallas kernels: 22.6 us -> 36.6 us  [heat(): pl.pallas_call(heat_kernel, out_shape=(jax.ShapeDtypeStruct(temp.shape, j...]
    all_to_all x5, starting transfers between devices: 38.3 us -> 26.7 us  [exchange(): lax.all_to_all(rows, ('slab', 'pair'), split_axis=0, concat_axis=0, tiled...]
    pallas_call x2, Pallas kernels: 13.2 us -> 24.1 us  [tile_terms(): pl.pallas_call(tiles_kernel, out_shape=jax.ShapeDtypeStruct(whole.shape,...]
  transfers between devices with their start and end apart: 11 -> 11, of which waited for: 6 -> 6; matrix products, arithmetic and copies ran while one was open for 2% -> 2% of each run, Pallas kernels for 31% -> 46%
where the time goes in v10:
time: 142 us; the launch traced here: 141 us
  Pallas kernels  73.7 us (52%)
  starting transfers between devices  43 us (30%)
  waiting for transfers between devices  21 us (15%)
  local copies, waits for them, and re-layouts  2.25 us (2%)
    pallas_call x1, Pallas kernels, heat(): pl.pallas_call(heat_kernel, out_shape=(jax.ShapeDtypeStruct(temp.shape, j...  36.6 us
    all_to_all x5, starting transfers between devices, exchange(): lax.all_to_all(rows, ('slab', 'pair'), split_axis=0, concat_axis=0, tiled...  26.7 us
    pallas_call x2, Pallas kernels, tile_terms(): pl.pallas_call(tiles_kernel, out_shape=jax.ShapeDtypeStruct(whole.shape,...  24.1 us
    ppermute x3, waiting for transfers between devices, both_ways(): from_low = lax.ppermute(high, axis, forward)  12.8 us
    ppermute x3, starting transfers between devices, both_ways(): from_low = lax.ppermute(high, axis, forward)  12.5 us
    all_to_all x5, waiting for transfers between devices, exchange(): lax.all_to_all(rows, ('slab', 'pair'), split_axis=0, concat_axis=0, tiled...  5.34 us
    ppermute x3, starting transfers between devices, both_ways(): from_high = lax.ppermute(low, axis, backward)  3.84 us
    ppermute x3, waiting for transfers between devices, both_ways(): from_high = lax.ppermute(low, axis, backward)  2.9 us
  transfers between devices with their start and end apart: 11, of which 6 were waited for; matrix products, arithmetic and copies ran while one was open for 2% of the time, Pallas kernels for 46%

profile of v10, /device:TPU:0, one launch (start us, length us, event | category | flops | bytes accessed | tf_op | source)
XLA Modules:
  0.0 141.3 jit_solution(1116758915173512569)
XLA Ops:
  0.6 2.1 %emit.1 = (f32[16,128]{1,0:T(8,128)}, f32[32,16,128]{2,1,0:T(8,128)}) custom-call(f32[16,64,512]{2,1,0:T(8,128)} %t_ref, s32[16,128]{1,0:T(8,128)} %site_ref.3, f32[16,128]{1,0:T(8,128)} %mirror_ref.5), custom_call_target="tpu_custom_call" | custom-call | flops 10000 | bytes 900000 | tf_op jit(solution)/shard_map/emit/pallas_call | solution.py:96
  2.8 7.4 %all-to-all-start = ((f32[32,16,128]{2,1,0:T(8,128)}), f32[32,16,128]{2,1,0:T(8,128)}, u32[]{:S(2)}, u32[]{:S(2)}) async-start(f32[32,16,128]{2,1,0:T(8,128)} %get-tuple-element.34), calls=%async_computation | async-start | bytes 524288 | tf_op jit(solution)/shard_map/all_to_all | solution.py:707
  10.2 2.2 %fusion = (f32[4,64,512]{2,1,0:T(8,128)}, f32[4,64,512]{2,1,0:T(8,128)}) fusion(f32[16,64,512]{2,1,0:T(8,128)} %k_ref), kind=kLoop, calls=%fused_computation | loop fusion | bytes 2097152 | tf_op jit(solution)/shard_map/slice | solution.py:749
  12.4 4.4 %collective-permute-start.2 = (f32[4,64,512]{2,1,0:T(8,128)}, f32[4,64,512]{2,1,0:T(8,128)}, u32[]{:S(2)}, u32[]{:S(2)}) collective-permute-start(f32[4,64,512]{2,1,0:T(8,128)} %get-tuple-element.62), channel_id=1, source_target_pairs={{0,4},{4,8},{8,12},{12,16},{16,20},{20,24},{24,28},{1,5},{5,9},{9,... | collective-permute-start | bytes 1572872 | tf_op jit(solution)/shard_map/ppermute | solution.py:718
  16.8 1.3 collective-permute-start.3
  18.8 2.0 %all-to-all-done = f32[32,16,128]{2,1,0:T(8,128)} async-done(((f32[32,16,128]{2,1,0:T(8,128)}), f32[32,16,128]{2,1,0:T(8,128)}, u32[]{:S(2)}, u32[]{:S(2)}) %all-to-all-start) | async-done | bytes 262176 | tf_op jit(solution)/shard_map/all_to_all | solution.py:707
  20.8 12.0 %tiles.2 = f32[512,128]{1,0:T(8,128)} custom-call(s32[1]{0:T(128)S(6)} %copy.11.live_ref, s32[2,256]{1,0:T(2,128)} %bitcast.7, s32[2,256]{1,0:T(2,128)} %bitcast.8, f32[512,128]{1,0:T(8,128)} %bitcast.1.whole_ref, f32[256,128,128]{2,1,0:T(8,128)} %tiles_ref.3), custom_call_target="tpu_custom_call" | custom-call | flops 134217728 | bytes 16777216 | tf_op jit(solution)/shard_map/tiles/pallas_call | solution.py:200
  32.8 3.3 %all-to-all-start.1 = ((f32[32,16,128]{2,1,0:T(8,128)}), f32[32,16,128]{2,1,0:T(8,128)}, u32[]{:S(2)}, u32[]{:S(2)}) async-start(f32[32,16,128]{2,1,0:T(8,128)} %bitcast.5), calls=%async_computation.1 | async-start | bytes 524288 | tf_op jit(solution)/shard_map/all_to_all | solution.py:707
  36.1 2.1 %pack_y.1 = (f32[16,8,512]{2,1,0:T(8,128)}, f32[16,8,512]{2,1,0:T(8,128)}) custom-call(f32[16,64,512]{2,1,0:T(8,128)} %t_ref, f32[16,64,512]{2,1,0:T(8,128)} %k_ref, f32[16,64,512]{2,1,0:T(8,128)} %t_ref, f32[16,64,512]{2,1,0:T(8,128)} %k_ref), custom_call_target="tpu_custom_call" | custom-call | bytes 1048576 | tf_op jit(solution)/shard_map/pack_y/pallas_call | solution.py:297
  38.2 2.6 %collective-permute-start = (f32[16,8,512]{2,1,0:T(8,128)}, f32[16,8,512]{2,1,0:T(8,128)}, u32[]{:S(2)}, u32[]{:S(2)}) collective-permute-start(f32[16,8,512]{2,1,0:T(8,128)} %get-tuple-element.40), channel_id=1, source_target_pairs={{0,1},{1,2},{2,3},{4,5},{5,6},{6,7},{8,9},{9,10},{10,11},{12,13},{... | collective-permute-start | bytes 786440 | tf_op jit(solution)/shard_map/ppermute | solution.py:718
  40.8 1.3 collective-permute-start.1
  42.1 0.0 collective-permute-done.2.k_low
  42.1 0.0 collective-permute-done.3.k_high
  42.1 0.0 collective-permute-done.below0.below1.below_ref
  42.1 2.9 %collective-permute-done.1.above0.above1.above_ref = f32[16,8,512]{2,1,0:T(8,128)} collective-permute-done((f32[16,8,512]{2,1,0:T(8,128)}, f32[16,8,512]{2,1,0:T(8,128)}, u32[]{:S(2)}, u32[]{:S(2)}) %collective-permute-start.1) | collective-permute-done | bytes 262176 | tf_op jit(solution)/shard_map/ppermute | solution.py:719
  45.0 1.7 %all-to-all-done.1.parts_ref = f32[32,16,128]{2,1,0:T(8,128)} async-done(((f32[32,16,128]{2,1,0:T(8,128)}), f32[32,16,128]{2,1,0:T(8,128)}, u32[]{:S(2)}, u32[]{:S(2)}) %all-to-all-start.1) | async-done | bytes 262176 | tf_op jit(solution)/shard_map/all_to_all | solution.py:707
  46.7 1.7 %middle.1 = f32[32,16,128]{2,1,0:T(8,128)} custom-call(f32[32,16,128]{2,1,0:T(8,128)} %all-to-all-done.1.parts_ref, f32[16,128]{1,0:T(8,128)} %get-tuple-element.43.emitted_ref, f32[16,128]{1,0:T(8,128)} %mirror_ref.5), custom_call_target="tpu_custom_call" | custom-call | flops 100000 | bytes 600000 | tf_op jit(solution)/shard_map/middle/pallas_call | solution.py:233
  48.4 7.6 %all-to-all-start.2 = ((f32[32,16,128]{2,1,0:T(8,128)}), f32[32,16,128]{2,1,0:T(8,128)}, u32[]{:S(2)}, u32[]{:S(2)}) async-start(f32[32,16,128]{2,1,0:T(8,128)} %middle.1), calls=%async_computation.2 | async-start | bytes 524288 | tf_op jit(solution)/shard_map/all_to_all | solution.py:707
  56.0 2.3 %pack_x.1 = (f32[4,80,512]{2,1,0:T(8,128)}, f32[4,80,512]{2,1,0:T(8,128)}) custom-call(f32[16,64,512]{2,1,0:T(8,128)} %t_ref, f32[16,64,512]{2,1,0:T(8,128)} %t_ref, f32[16,8,512]{2,1,0:T(8,128)} %collective-permute-done.below0.below1.below_ref, f32[16,8,512]{2,1,0:T(8,128)} %collective-permute-done.1.above0.above1.above_ref, ...), custom_call_target="tpu_custom_call" | custom-call | bytes 2621440 | tf_op jit(solution)/shard_map/pack_x/pallas_call | solution.py:335
  58.3 1.3 collective-permute-start.5
  59.6 5.4 %collective-permute-start.4 = (f32[4,80,512]{2,1,0:T(8,128)}, f32[4,80,512]{2,1,0:T(8,128)}, u32[]{:S(2)}, u32[]{:S(2)}) collective-permute-start(f32[4,80,512]{2,1,0:T(8,128)} %get-tuple-element.50), channel_id=1, source_target_pairs={{0,4},{4,8},{8,12},{12,16},{16,20},{20,24},{24,28},{1,5},{5,9},{9,... | collective-permute-start | bytes 1966088 | tf_op jit(solution)/shard_map/ppermute | solution.py:718
  65.0 1.5 %all-to-all-done.2 = f32[32,16,128]{2,1,0:T(8,128)} async-done(((f32[32,16,128]{2,1,0:T(8,128)}), f32[32,16,128]{2,1,0:T(8,128)}, u32[]{:S(2)}, u32[]{:S(2)}) %all-to-all-start.2) | async-done | bytes 262176 | tf_op jit(solution)/shard_map/all_to_all | solution.py:707
  66.6 12.0 %tiles.3 = f32[512,128]{1,0:T(8,128)} custom-call(s32[1]{0:T(128)S(6)} %copy.11.live_ref, s32[2,256]{1,0:T(2,128)} %bitcast.9, s32[2,256]{1,0:T(2,128)} %bitcast.10, f32[512,128]{1,0:T(8,128)} %bitcast.3.whole_ref, f32[256,128,128]{2,1,0:T(8,128)} %tiles_ref.3), custom_call_target="tpu_custom_call" | custom-call | flops 134217728 | bytes 16777216 | tf_op jit(solution)/shard_map/tiles/pallas_call | solution.py:200
  78.6 3.3 %all-to-all-start.3 = ((f32[32,16,128]{2,1,0:T(8,128)}), f32[32,16,128]{2,1,0:T(8,128)}, u32[]{:S(2)}, u32[]{:S(2)}) async-start(f32[32,16,128]{2,1,0:T(8,128)} %bitcast.6), calls=%async_computation.3 | async-start | bytes 524288 | tf_op jit(solution)/shard_map/all_to_all | solution.py:707
  81.9 0.0 collective-permute-done.5.t_high
  81.9 12.7 %collective-permute-done.4.t_low = f32[4,80,512]{2,1,0:T(8,128)} collective-permute-done((f32[4,80,512]{2,1,0:T(8,128)}, f32[4,80,512]{2,1,0:T(8,128)}, u32[]{:S(2)}, u32[]{:S(2)}) %collective-permute-start.4) | collective-permute-done | bytes 655392 | tf_op jit(solution)/shard_map/ppermute | solution.py:718
  94.7 0.2 all-to-all-done.3.parts_ref
  94.8 2.2 %last.1 = (f32[16,128]{1,0:T(8,128)}, f32[32,8,128]{2,1,0:T(8,128)}) custom-call(f32[32,16,128]{2,1,0:T(8,128)} %all-to-all-done.3.parts_ref, f32[16,128]{1,0:T(8,128)} %get-tuple-element.43.emitted_ref, f32[16,128]{1,0:T(8,128)} %mirror_ref.5, s32[16,128]{1,0:T(8,128)} %site_ref.3), custom_call_target="tpu_custom_call" | custom-call | flops 10000000 | bytes 600000 | tf_op jit(solution)/shard_map/last/pallas_call | solution.py:273
  97.0 5.1 %all-to-all-start.4 = ((f32[32,8,128]{2,1,0:T(8,128)}), f32[32,8,128]{2,1,0:T(8,128)}, u32[]{:S(2)}, u32[]{:S(2)}) async-start(f32[32,8,128]{2,1,0:T(8,128)} %get-tuple-element.54), calls=%async_computation.4 | async-start | bytes 262144 | tf_op jit(solution)/shard_map/all_to_all | solution.py:707
  102.1 36.6 %heat.1 = (f32[16,64,512]{2,1,0:T(8,128)}, f32[24,8,128]{2,1,0:T(8,128)}) custom-call(f32[16,64,512]{2,1,0:T(8,128)} %t_ref, f32[16,64,512]{2,1,0:T(8,128)} %k_ref, f32[4,64,512]{2,1,0:T(8,128)} %collective-permute-done.2.k_low, f32[4,64,512]{2,1,0:T(8,128)} %collective-permute-done.3.k_high, f32[4,80,512]{2,1,0:T(8,128)} %collective-permute-done.4.t_low, ...), custom_call_target="tpu_custom_call" | custom-call | flops 88473600 | bytes 25165824 | tf_op jit(solution)/shard_map/heat/pallas_call | solution.py:584
  138.7 0.0 all-to-all-done.4.all_ref
  138.7 2.6 %add_source.1 = f32[16,64,512]{2,1,0:T(8,128)} custom-call(f32[32,8,128]{2,1,0:T(8,128)} %all-to-all-done.4.all_ref, f32[24,8,128]{2,1,0:T(8,128)} %get-tuple-element.60.thin_ref, f32[16,64,512]{2,1,0:T(8,128)} %get-tuple-element.61.base_ref), custom_call_target="tpu_custom_call", output_to_operand_aliasing={{}: (2, {})} | custom-call | flops 1000000 | bytes 1048576 | tf_op jit(solution)/shard_map/add_source/pallas_call | solution.py:689
Async XLA Ops:
  2.8 18.0 %all-to-all-start = ((f32[32,16,128]{2,1,0:T(8,128)}), f32[32,16,128]{2,1,0:T(8,128)}, u32[]{:S(2)}, u32[]{:S(2)}) async-start(f32[32,16,128]{2,1,0:T(8,128)} %get-tuple-element.34), calls=%async_computation | async-start | bytes 524288 | tf_op jit(solution)/shard_map/all_to_all | solution.py:707
  12.4 29.7 %collective-permute-start.2 = (f32[4,64,512]{2,1,0:T(8,128)}, f32[4,64,512]{2,1,0:T(8,128)}, u32[]{:S(2)}, u32[]{:S(2)}) collective-permute-start(f32[4,64,512]{2,1,0:T(8,128)} %get-tuple-element.62), channel_id=1, source_target_pairs={{0,4},{4,8},{8,12},{12,16},{16,20},{20,24},{24,28},{1,5},{5,9},{9,... | collective-permute-start | bytes 1572872 | tf_op jit(solution)/shard_map/ppermute | solution.py:718
  16.8 25.3 %collective-permute-start.3 = (f32[4,64,512]{2,1,0:T(8,128)}, f32[4,64,512]{2,1,0:T(8,128)}, u32[]{:S(2)}, u32[]{:S(2)}) collective-permute-start(f32[4,64,512]{2,1,0:T(8,128)} %get-tuple-element.63), channel_id=1, source_target_pairs={{4,0},{8,4},{12,8},{16,12},{20,16},{24,20},{28,24},{5,1},{9,5},{13... | collective-permute-start | bytes 1572872 | tf_op jit(solution)/shard_map/ppermute | solution.py:719
  32.8 13.9 %all-to-all-start.1 = ((f32[32,16,128]{2,1,0:T(8,128)}), f32[32,16,128]{2,1,0:T(8,128)}, u32[]{:S(2)}, u32[]{:S(2)}) async-start(f32[32,16,128]{2,1,0:T(8,128)} %bitcast.5), calls=%async_computation.1 | async-start | bytes 524288 | tf_op jit(solution)/shard_map/all_to_all | solution.py:707
  38.2 4.0 %collective-permute-start = (f32[16,8,512]{2,1,0:T(8,128)}, f32[16,8,512]{2,1,0:T(8,128)}, u32[]{:S(2)}, u32[]{:S(2)}) collective-permute-start(f32[16,8,512]{2,1,0:T(8,128)} %get-tuple-element.40), channel_id=1, source_target_pairs={{0,1},{1,2},{2,3},{4,5},{5,6},{6,7},{8,9},{9,10},{10,11},{12,13},{... | collective-permute-start | bytes 786440 | tf_op jit(solution)/shard_map/ppermute | solution.py:718
  40.8 4.2 %collective-permute-start.1 = (f32[16,8,512]{2,1,0:T(8,128)}, f32[16,8,512]{2,1,0:T(8,128)}, u32[]{:S(2)}, u32[]{:S(2)}) collective-permute-start(f32[16,8,512]{2,1,0:T(8,128)} %get-tuple-element.41), channel_id=1, source_target_pairs={{1,0},{2,1},{3,2},{5,4},{6,5},{7,6},{9,8},{10,9},{11,10},{13,12},{... | collective-permute-start | bytes 786440 | tf_op jit(solution)/shard_map/ppermute | solution.py:719
  48.4 18.2 %all-to-all-start.2 = ((f32[32,16,128]{2,1,0:T(8,128)}), f32[32,16,128]{2,1,0:T(8,128)}, u32[]{:S(2)}, u32[]{:S(2)}) async-start(f32[32,16,128]{2,1,0:T(8,128)} %middle.1), calls=%async_computation.2 | async-start | bytes 524288 | tf_op jit(solution)/shard_map/all_to_all | solution.py:707
  58.3 23.6 %collective-permute-start.5 = (f32[4,80,512]{2,1,0:T(8,128)}, f32[4,80,512]{2,1,0:T(8,128)}, u32[]{:S(2)}, u32[]{:S(2)}) collective-permute-start(f32[4,80,512]{2,1,0:T(8,128)} %get-tuple-element.49), channel_id=1, source_target_pairs={{4,0},{8,4},{12,8},{16,12},{20,16},{24,20},{28,24},{5,1},{9,5},{13... | collective-permute-start | bytes 1966088 | tf_op jit(solution)/shard_map/ppermute | solution.py:719
  59.6 35.1 %collective-permute-start.4 = (f32[4,80,512]{2,1,0:T(8,128)}, f32[4,80,512]{2,1,0:T(8,128)}, u32[]{:S(2)}, u32[]{:S(2)}) collective-permute-start(f32[4,80,512]{2,1,0:T(8,128)} %get-tuple-element.50), channel_id=1, source_target_pairs={{0,4},{4,8},{8,12},{12,16},{16,20},{20,24},{24,28},{1,5},{5,9},{9,... | collective-permute-start | bytes 1966088 | tf_op jit(solution)/shard_map/ppermute | solution.py:718
  78.6 16.2 %all-to-all-start.3 = ((f32[32,16,128]{2,1,0:T(8,128)}), f32[32,16,128]{2,1,0:T(8,128)}, u32[]{:S(2)}, u32[]{:S(2)}) async-start(f32[32,16,128]{2,1,0:T(8,128)} %bitcast.6), calls=%async_computation.3 | async-start | bytes 524288 | tf_op jit(solution)/shard_map/all_to_all | solution.py:707
  97.0 41.7 %all-to-all-start.4 = ((f32[32,8,128]{2,1,0:T(8,128)}), f32[32,8,128]{2,1,0:T(8,128)}, u32[]{:S(2)}, u32[]{:S(2)}) async-start(f32[32,8,128]{2,1,0:T(8,128)} %get-tuple-element.54), calls=%async_computation.4 | async-start | bytes 262144 | tf_op jit(solution)/shard_map/all_to_all | solution.py:707
